TPU v7x, 32 devices: a whole 2x2x4 slice. The times are simulated.
32 devices in a mesh: row: 2 (over core), col: 16 (over z, y, x).
Axes of the slice: x: 2, y: 2, z: 4, core: 2. Of those that a mesh axis runs over, the one named last changes fastest.
Arguments:
- image_tokens: bfloat16 [64, 512, 256], P('row', 'col'), may hold values from -6 to 6
- w_in: bfloat16 [256, 768], replicated, may hold values from -0.375 to 0.375
- conv_kernel: bfloat16 [3, 3, 768], replicated, may hold values from -2 to 2
- conv_bias: float32 [768], replicated, may hold values from -3 to 3
- long_filter: bfloat16 [64, 256], replicated, may hold values from -0.75 to 0.75
- skip_gain: float32 [256], replicated, may hold values from 0.5 to 1.5
- w_out: bfloat16 [256, 256], replicated, may hold values from -0.375 to 0.375
Outputs:
- layer_out: bfloat16 [64, 512, 256], P('row', 'col')
All inputs are finite; a program needn't handle non-finite values.
Results may differ from a plain program's by a relative error of at most 0.014.
Values may be sent and summed in bfloat16 or wider, within the bound.
No kernel may reach another device: no remote copies, remote signals or barrier semaphores. Data moves between devices by JAX's collectives and lax.ppermute only.
A program may use at most 64 MiB of HBM per device.

v0:
```python
import jax
import jax.numpy as jnp
from jax import lax
from jax.sharding import PartitionSpec as P


def extended(block, sides, width):
    for axis, dim in sides:
        count = lax.axis_size(axis)
        forward = [(i, i + 1) for i in range(count - 1)]
        backward = [(target, source) for source, target in forward]
        low = lax.ppermute(
            lax.slice_in_dim(block, block.shape[dim] - width, None, axis=dim), axis, forward
        )
        high = lax.ppermute(lax.slice_in_dim(block, 0, width, axis=dim), axis, backward)
        block = jnp.concatenate([low, block, high], axis=dim)
    return block


def depthwise(padded, kernel, bias, height, span):
    total = jnp.zeros((height, span, padded.shape[2]), jnp.float32) + bias
    for row_off in range(3):
        for col_off in range(3):
            window = padded[row_off : row_off + height, col_off : col_off + span, :].astype(
                jnp.float32
            )
            total = total + window * kernel[row_off, col_off].astype(jnp.float32)
    return total.astype(jnp.bfloat16)


def toeplitz(filt_rev, offset, out_count, src_count):
    margin = filt_rev.shape[0] // 3
    spare = margin // 2
    length = out_count + src_count - 1
    start = jnp.asarray(margin + margin - 1 - spare - (out_count - 1), jnp.int32) - jnp.asarray(
        offset, jnp.int32
    )
    window = lax.dynamic_slice_in_dim(filt_rev, start, length, 0)
    tiled = jnp.tile(window, (out_count + 1, 1))
    strided = tiled[out_count - 1 : out_count - 1 + out_count * (length - 1)]
    return strided.reshape(out_count, length - 1, filt_rev.shape[1])[:, :src_count]


def on_device(image_tokens, w_in, conv_kernel, conv_bias, long_filter, skip_gain, w_out):
    row_count, col_count, width = image_tokens.shape
    flat = image_tokens.reshape(row_count * col_count, width)
    projected = jnp.dot(flat, w_in, preferred_element_type=jnp.float32)
    projected = projected.astype(jnp.bfloat16).reshape(row_count, col_count, 3 * width)
    padded = extended(projected, (("row", 0), ("col", 1)), 1)
    mixed = depthwise(padded, conv_kernel, conv_bias, row_count, col_count)
    query = mixed[:, :, :width].astype(jnp.float32)
    key = mixed[:, :, width : 2 * width].astype(jnp.float32)
    value = mixed[:, :, 2 * width :].astype(jnp.float32)
    product = (key * value).astype(jnp.bfloat16)
    filt_pad = jnp.concatenate([jnp.zeros_like(long_filter), long_filter], axis=0)
    zero_band = jnp.zeros_like(filt_pad)
    filt_rev = jnp.concatenate([zero_band, jnp.flip(filt_pad, 0), zero_band], axis=0)
    my_start = lax.axis_index("row") * row_count
    empty_long = jnp.zeros((row_count, col_count, width), jnp.float32)
    total = empty_long
    piece = lax.all_gather(product, "row", axis=0, tiled=True)
    start = jnp.int32(0)
    piece_len = piece.shape[0]
    step_len = min(row_count, piece_len)
    for offset_row in range(0, piece_len, step_len):
        sub_piece = piece[offset_row : offset_row + step_len]
        sub_start = start + offset_row

        def work(running):
            toeplitz_block = toeplitz(filt_rev, my_start - sub_start, row_count, step_len)
            return running + jnp.einsum(
                "abc,bwc->awc", toeplitz_block, sub_piece, preferred_element_type=jnp.float32
            )

        def keep(running):
            return running

        total = lax.cond(sub_start < my_start + row_count, work, keep, total)
    gated = (query * (total + skip_gain * product.astype(jnp.float32))).astype(jnp.bfloat16)
    gated_flat = gated.reshape(row_count * col_count, width)
    final = jnp.dot(gated_flat, w_out, preferred_element_type=jnp.float32)
    return final.astype(jnp.bfloat16).reshape(row_count, col_count, width)


def solution(mesh):
    in_specs = (P("row", "col", None), P(), P(), P(), P(), P(), P())
    out_specs = P("row", "col", None)
    return jax.shard_map(
        on_device, mesh=mesh, in_specs=in_specs, out_specs=out_specs, check_vma=False
    )
```

profile of v0, /device:TPU:1, one launch (start us, length us, event | category | flops | bytes accessed | tf_op | source)
XLA Modules:
  0.0 104.8 jit_solution(5073421988976037191)
XLA Ops:
  6.5 0.0 copy-start
  6.5 0.0 all-gather.2.cloned.1.call-start
  6.5 1.0 copy-done
  7.6 1.6 %convolution_convert_fusion = bf16[1024,768]{1,0:T(8,128)(2,1)S(1)} fusion(bf16[1024,256]{1,0:T(8,128)(2,1)S(1)} %bitcast.18, bf16[256,768]{1,0:T(8,128)(2,1)} %param.12), kind=kOutput, calls=%fused_computation.9 | convolution fusion | flops 403439616 | bytes 2490368 | tf_op jit(solution)/shard_map/dot_general | solution.py:47
  9.2 1.3 %collective-permute-start = (bf16[1,32,768]{2,1,0:T(8,128)(2,1)S(1)}, bf16[1,32,768]{2,1,0:T(8,128)(2,1)S(1)}, u32[]{:S(2)}, u32[]{:S(2)}) collective-permute-start(bf16[1,32,768]{2,1,0:T(8,128)(2,1)S(1)} %get-tuple-element.63), channel_id=1, source_target_pairs={{0,16},{1,17},{2,18},{3,19},{4,20},{5,21},{6,22},{7,23},{8,24},{9,... | collective-permute-start | bytes 147464 | tf_op jit(solution)/shard_map/ppermute | solution.py:12
  10.5 3.0 %collective-permute-start.1 = (bf16[1,32,768]{2,1,0:T(8,128)(2,1)S(1)}, bf16[1,32,768]{2,1,0:T(8,128)(2,1)S(1)}, u32[]{:S(2)}, u32[]{:S(2)}) collective-permute-start(bf16[1,32,768]{2,1,0:T(8,128)(2,1)S(1)} %get-tuple-element.64), channel_id=1, source_target_pairs={{16,0},{17,1},{18,2},{19,3},{20,4},{21,5},{22,6},{23,7},{24,8},{25... | collective-permute-start | bytes 147464 | tf_op jit(solution)/shard_map/ppermute | solution.py:15
  13.5 0.0 collective-permute-done
  13.5 0.9 collective-permute-done.1
  14.4 0.2 pad_maximum_fusion.6
  14.5 0.0 copy-start.6
  14.5 4.0 %collective-permute-start.2 = (bf16[34,1,768]{2,1,0:T(2,128)(2,1)S(1)}, bf16[34,1,768]{2,1,0:T(2,128)(2,1)S(1)}, u32[]{:S(2)}, u32[]{:S(2)}) collective-permute-start(bf16[34,1,768]{2,1,0:T(2,128)(2,1)S(1)} %get-tuple-element.61), channel_id=1, source_target_pairs={{0,1},{1,2},{2,3},{3,4},{4,5},{5,6},{6,7},{7,8},{8,9},{9,10},{10,1... | collective-permute-start | bytes 156680 | tf_op jit(solution)/shard_map/ppermute | solution.py:12
  18.5 1.3 %collective-permute-start.3 = (bf16[34,1,768]{2,1,0:T(2,128)(2,1)S(1)}, bf16[34,1,768]{2,1,0:T(2,128)(2,1)S(1)}, u32[]{:S(2)}, u32[]{:S(2)}) collective-permute-start(bf16[34,1,768]{2,1,0:T(2,128)(2,1)S(1)} %get-tuple-element.62), channel_id=1, source_target_pairs={{1,0},{2,1},{3,2},{4,3},{5,4},{6,5},{7,6},{8,7},{9,8},{10,9},{11,1... | collective-permute-start | bytes 156680 | tf_op jit(solution)/shard_map/ppermute | solution.py:15
  19.8 0.0 copy-done.4
  19.8 0.1 convert_reduce_fusion.8
  19.9 0.5 collective-permute-done.2
  20.4 3.9 %collective-permute-done.3 = bf16[34,1,768]{2,1,0:T(2,128)(2,1)S(1)} collective-permute-done((bf16[34,1,768]{2,1,0:T(2,128)(2,1)S(1)}, bf16[34,1,768]{2,1,0:T(2,128)(2,1)S(1)}, u32[]{:S(2)}, u32[]{:S(2)}) %collective-permute-start.3) | collective-permute-done | bytes 52256 | tf_op jit(solution)/shard_map/ppermute | solution.py:15
  24.4 1.2 %maximum_maximum_fusion = (bf16[34,33,768]{2,1,0:T(8,128)(2,1)S(1)}, bf16[34,33,768]{2,1,0:T(8,128)(2,1)S(1)}) fusion(bf16[1,32,768]{2,1,0:T(8,128)(2,1)S(1)} %collective-permute-done.1, bf16[32,32,768]{2,1,0:T(8,128)(2,1)S(1)} %bitcast.20, bf16[1,32,768]{2,1,0:T(8,128)(2,1)S(1)} %collective-permute-done, bf16[34,1,768]{2,1,0:T(2,128)(2,1)S(1)} %collective-permute-done.2, ...), kind=kLoop, calls=%fused_computation.7 | loop fusion | flops 13787136 | bytes 5222400 | tf_op jit(solution)/shard_map/concatenate | solution.py:16
  25.6 0.0 copy-done.6
  25.6 0.0 copy-start.5
  25.6 4.1 %add_convert_fusion = bf16[32,32,768]{2,1,0:T(8,128)(2,1)S(1)} fusion(bf16[32,32,768]{2,1,0:T(8,128)(2,1)S(1)} %bitcast.21, bf16[34,33,768]{2,1,0:T(8,128)(2,1)S(1)} %get-tuple-element.60, bf16[1,32,768]{2,1,0:T(8,128)(2,1)S(1)} %collective-permute-done.1, bf16[34,33,768]{2,1,0:T(8,128)(2,1)S(1)} %get-tuple-element.59, ...), kind=kLoop, calls=%fused_computation.6 | loop fusion | flops 23592960 | bytes 12711936 | tf_op jit(solution)/shard_map/convert_element_type | solution.py:28
  29.7 0.9 multiply_convert_fusion.1
  30.7 0.0 all-gather.2.cloned.1.call-update
  30.7 0.0 copy-done.5
  30.7 0.1 rev.4
  30.9 12.1 %all-gather.2.cloned.1.call-done = bf16[64,32,256]{2,1,0:T(8,128)(2,1)} async-done(((bf16[32,32,256]{2,1,0:T(8,128)(2,1)}), bf16[64,32,256]{2,1,0:T(8,128)(2,1)}) %all-gather.2.cloned.1.call-update) | async-done | bytes 1048592 | tf_op jit(solution)/shard_map/all_gather | solution.py:61
  43.0 24.2 %conditional.2 = (f32[32,32,256]{1,0,2:T(8,128)}) conditional(s32[]{:T(128)} %convert_element_type.91, () %tuple.17, (s32[]{:T(128)}, bf16[384,256]{1,0:T(8,128)(2,1)S(1)}, bf16[64,32,256]{2,1,0:T(8,128)(2,1)}) %tuple.18), branch_computations={%region_0.1_spmd, %region_1.2_spmd} | conditional | flops 16777220 | bytes 20984918 | solution.py:78
  43.0 0.1 tile.4
  43.1 1.3 %tile.10 = bf16[2079,256]{1,0:T(8,128)(2,1)} reshape(bf16[33,63,256]{2,1,0:T(8,128)(2,1)S(1)} %tile.4) | data formatting | bytes 2128896 | tf_op jit(solution)/shard_map/cond/branch_1_fun/tile | solution.py:39
  44.4 2.5 %slice.133 = bf16[1984,256]{1,0:T(8,128)(2,1)} slice(bf16[2079,256]{1,0:T(8,128)(2,1)} %tile.10), slice={[31:2015], [0:256]} | slice | bytes 2031616 | tf_op jit(solution)/shard_map/cond/branch_1_fun/slice | solution.py:40
  46.9 2.3 %reshape.24 = bf16[32,62,256]{2,1,0:T(8,128)(2,1)} reshape(bf16[1984,256]{1,0:T(8,128)(2,1)} %slice.133) | data formatting | bytes 2031616 | tf_op jit(solution)/shard_map/cond/branch_1_fun/reshape | solution.py:41
  49.2 1.9 %slice.134 = bf16[32,32,256]{2,1,0:T(8,128)(2,1)} slice(bf16[32,62,256]{2,1,0:T(8,128)(2,1)} %reshape.24), slice={[0:32], [0:32], [0:256]} | slice | bytes 1048576 | tf_op jit(solution)/shard_map/cond/branch_1_fun/slice | solution.py:41
  51.1 4.6 %copy.29 = bf16[32,32,256]{1,0,2:T(8,128)(2,1)} copy(bf16[32,32,256]{2,1,0:T(8,128)(2,1)} %slice.134) | data formatting | bytes 1048576 | tf_op jit(solution)/shard_map/cond
  55.7 6.5 %copy.24 = bf16[64,32,256]{1,0,2:T(8,128)(2,1)} copy(bf16[64,32,256]{2,1,0:T(8,128)(2,1)S(1)} %copy-done.1) | data formatting | bytes 2097152 | tf_op jit(solution)/shard_map
  62.2 4.9 %convolution_bitcast_fusion = f32[32,32,256]{1,0,2:T(8,128)} fusion(bf16[32,32,256]{1,0,2:T(8,128)(2,1)} %copy.29, bf16[64,32,256]{1,0,2:T(8,128)(2,1)} %copy.24), kind=kOutput, calls=%fused_computation | convolution fusion | flops 16777216 | bytes 5242880 | tf_op jit(solution)/shard_map/cond/branch_1_fun/abc,bwc->awc/dot_general | solution.py:71
  67.1 28.8 %conditional.3 = (f32[32,32,256]{2,1,0:T(8,128)S(1)}) conditional(s32[]{:T(128)} %convert_element_type.90, f32[32,32,256]{1,0,2:T(8,128)} %get-tuple-element.67, (s32[]{:T(128)}, bf16[384,256]{1,0:T(8,128)(2,1)S(1)}, bf16[64,32,256]{2,1,0:T(8,128)(2,1)}, f32[32,32,256]{1,0,2:T(8,128)}) %tuple.19), branch_computations={%region_2.3_spmd, %region_3.4_spmd} | conditional | flops 17039364 | bytes 27276386 | solution.py:78
  67.2 0.1 tile.11
  67.3 1.3 %tile.12 = bf16[2079,256]{1,0:T(8,128)(2,1)} reshape(bf16[33,63,256]{2,1,0:T(8,128)(2,1)S(1)} %tile.11) | data formatting | bytes 2128896 | tf_op jit(solution)/shard_map/cond/branch_1_fun/tile | solution.py:39
  68.6 2.4 %slice.136 = bf16[1984,256]{1,0:T(8,128)(2,1)} slice(bf16[2079,256]{1,0:T(8,128)(2,1)} %tile.12), slice={[31:2015], [0:256]} | slice | bytes 2031616 | tf_op jit(solution)/shard_map/cond/branch_1_fun/slice | solution.py:40
  71.0 2.4 %reshape.25 = bf16[32,62,256]{2,1,0:T(8,128)(2,1)} reshape(bf16[1984,256]{1,0:T(8,128)(2,1)} %slice.136) | data formatting | bytes 2031616 | tf_op jit(solution)/shard_map/cond/branch_1_fun/reshape | solution.py:41
  73.4 1.9 %slice.137 = bf16[32,32,256]{2,1,0:T(8,128)(2,1)} slice(bf16[32,62,256]{2,1,0:T(8,128)(2,1)} %reshape.25), slice={[0:32], [0:32], [0:256]} | slice | bytes 1048576 | tf_op jit(solution)/shard_map/cond/branch_1_fun/slice | solution.py:41
  75.3 4.6 %copy.30 = bf16[32,32,256]{1,0,2:T(8,128)(2,1)} copy(bf16[32,32,256]{2,1,0:T(8,128)(2,1)} %slice.137) | data formatting | bytes 1048576 | tf_op jit(solution)/shard_map/cond
  79.8 6.5 %copy.25 = bf16[64,32,256]{1,0,2:T(8,128)(2,1)} copy(bf16[64,32,256]{2,1,0:T(8,128)(2,1)S(1)} %copy-done.2) | data formatting | bytes 2097152 | tf_op jit(solution)/shard_map
  86.3 6.1 %bitcast_add_fusion = f32[32,32,256]{1,0,2:T(8,128)} fusion(f32[32,32,256]{1,0,2:T(8,128)} %get-tuple-element.30, bf16[32,32,256]{1,0,2:T(8,128)(2,1)} %copy.30, bf16[64,32,256]{1,0,2:T(8,128)(2,1)} %copy.25), kind=kOutput, calls=%fused_computation.3 | convolution fusion | flops 17039360 | bytes 9437184 | tf_op jit(solution)/shard_map/cond/branch_1_fun/abc,bwc->awc/dot_general | solution.py:71
  92.5 3.5 %copy.28 = f32[32,32,256]{2,1,0:T(8,128)S(1)} copy(f32[32,32,256]{1,0,2:T(8,128)} %bitcast_add_fusion) | data formatting | bytes 2097152 | tf_op jit(solution)/shard_map/cond | solution.py:78
  96.0 0.0 copy-done.7
  96.0 0.3 multiply_convert_fusion
  96.3 0.6 copy-done.3
  96.9 1.1 %convolution_convert_fusion.1 = bf16[1024,256]{1,0:T(8,128)(2,1)} fusion(bf16[1024,256]{1,0:T(8,128)(2,1)S(1)} %bitcast.22, bf16[256,256]{1,0:T(8,128)(2,1)S(1)} %copy-done.3), kind=kOutput, calls=%fused_computation.12 | convolution fusion | flops 134479872 | bytes 1179648 | tf_op jit(solution)/shard_map/dot_general | solution.py:81
  (13 shorter events, 0.1 us)
Async XLA Ops:
  6.5 1.0 copy-start
  6.5 13.3 %copy-start.4 = (bf16[3,3,768]{2,1,0:T(4,128)(2,1)S(1)}, bf16[3,3,768]{2,1,0:T(4,128)(2,1)}, u32[]{:S(2)}) copy-start(bf16[3,3,768]{2,1,0:T(4,128)(2,1)} %param.13) | copy-start | bytes 41476
  6.5 36.4 %all-gather.2.cloned.1.call-start = ((), (), s32[]{:S(2)}) async-start(), calls=%async_computation | async-start | bytes 1572864 | tf_op jit(solution)/shard_map/all_gather | solution.py:61
  9.2 4.3 %collective-permute-start = (bf16[1,32,768]{2,1,0:T(8,128)(2,1)S(1)}, bf16[1,32,768]{2,1,0:T(8,128)(2,1)S(1)}, u32[]{:S(2)}, u32[]{:S(2)}) collective-permute-start(bf16[1,32,768]{2,1,0:T(8,128)(2,1)S(1)} %get-tuple-element.63), channel_id=1, source_target_pairs={{0,16},{1,17},{2,18},{3,19},{4,20},{5,21},{6,22},{7,23},{8,24},{9,... | collective-permute-start | bytes 147464 | tf_op jit(solution)/shard_map/ppermute | solution.py:12
  10.5 3.9 %collective-permute-start.1 = (bf16[1,32,768]{2,1,0:T(8,128)(2,1)S(1)}, bf16[1,32,768]{2,1,0:T(8,128)(2,1)S(1)}, u32[]{:S(2)}, u32[]{:S(2)}) collective-permute-start(bf16[1,32,768]{2,1,0:T(8,128)(2,1)S(1)} %get-tuple-element.64), channel_id=1, source_target_pairs={{16,0},{17,1},{18,2},{19,3},{20,4},{21,5},{22,6},{23,7},{24,8},{25... | collective-permute-start | bytes 147464 | tf_op jit(solution)/shard_map/ppermute | solution.py:15
  14.5 11.1 %copy-start.6 = (f32[768]{0:T(1024)S(1)}, f32[768]{0:T(1024)}, u32[]{:S(2)}) copy-start(f32[768]{0:T(1024)} %param.14) | copy-start | bytes 9220
  14.5 5.9 %collective-permute-start.2 = (bf16[34,1,768]{2,1,0:T(2,128)(2,1)S(1)}, bf16[34,1,768]{2,1,0:T(2,128)(2,1)S(1)}, u32[]{:S(2)}, u32[]{:S(2)}) collective-permute-start(bf16[34,1,768]{2,1,0:T(2,128)(2,1)S(1)} %get-tuple-element.61), channel_id=1, source_target_pairs={{0,1},{1,2},{2,3},{3,4},{4,5},{5,6},{6,7},{7,8},{8,9},{9,10},{10,1... | collective-permute-start | bytes 156680 | tf_op jit(solution)/shard_map/ppermute | solution.py:12
  18.5 5.9 %collective-permute-start.3 = (bf16[34,1,768]{2,1,0:T(2,128)(2,1)S(1)}, bf16[34,1,768]{2,1,0:T(2,128)(2,1)S(1)}, u32[]{:S(2)}, u32[]{:S(2)}) collective-permute-start(bf16[34,1,768]{2,1,0:T(2,128)(2,1)S(1)} %get-tuple-element.62), channel_id=1, source_target_pairs={{1,0},{2,1},{3,2},{4,3},{5,4},{6,5},{7,6},{8,7},{9,8},{10,9},{11,1... | collective-permute-start | bytes 156680 | tf_op jit(solution)/shard_map/ppermute | solution.py:15
  25.6 5.1 %copy-start.5 = (bf16[64,256]{1,0:T(8,128)(2,1)S(1)}, bf16[64,256]{1,0:T(8,128)(2,1)}, u32[]{:S(2)}) copy-start(bf16[64,256]{1,0:T(8,128)(2,1)} %param.15) | copy-start | bytes 98308
  46.9 8.8 %copy-start.1 = (bf16[64,32,256]{2,1,0:T(8,128)(2,1)S(1)}, bf16[64,32,256]{2,1,0:T(8,128)(2,1)}, u32[]{:S(2)}) copy-start(bf16[64,32,256]{2,1,0:T(8,128)(2,1)} %get-tuple-element.44) | copy-start | bytes 3145732 | tf_op jit(solution)/shard_map/cond
  67.1 28.8 %copy-start.7 = (f32[256]{0:T(256)S(1)}, f32[256]{0:T(256)}, u32[]{:S(2)}) copy-start(f32[256]{0:T(256)} %param.16) | copy-start | bytes 3076
  71.0 8.8 %copy-start.2 = (bf16[64,32,256]{2,1,0:T(8,128)(2,1)S(1)}, bf16[64,32,256]{2,1,0:T(8,128)(2,1)}, u32[]{:S(2)}) copy-start(bf16[64,32,256]{2,1,0:T(8,128)(2,1)} %get-tuple-element.47) | copy-start | bytes 3145732 | tf_op jit(solution)/shard_map/cond
  96.0 0.9 copy-start.3
Sparse Core Ops, SparseCore 0:
  30.8 12.1 all-gather.1
where the time goes:
time: 105 us
  local copies, waits for them, and re-layouts  43.7 us (42%)
  waiting for transfers between devices  17.4 us (17%)
  matrix products  13.7 us (13%)
  between operations  13.6 us (13%)
  starting transfers between devices  9.57 us (9%)
  other arithmetic  6.79 us (6%)
    another operation x2, local copies, waits for them, and re-layouts  13 us
    all_gather x1, waiting for transfers between devices, on_device(): piece = lax.all_gather(product, 'row', axis=0, tiled=True)  12.1 us
    dot_general x2, matrix products, work(): jnp.einsum('abc,bwc->awc', toeplitz_block, sub_piece, preferred_element_t...  11.1 us
    cond x6, local copies, waits for them, and re-layouts  9.15 us
    ppermute x2, starting transfers between devices, extended(): lax.ppermute(lax.slice_in_dim(block, block.shape[dim] - width, None, axis...  5.24 us
    slice x2, local copies, waits for them, and re-layouts, toeplitz(): strided = tiled[out_count - 1:out_count - 1 + out_count * (length - 1)]  4.91 us
    ppermute x2, waiting for transfers between devices, extended(): lax.ppermute(lax.slice_in_dim(block, 0, width, axis=dim), axis, backward)  4.78 us
    reshape x2, local copies, waits for them, and re-layouts, toeplitz(): strided.reshape(out_count, length - 1, filt_rev.shape[1])[:, :src_count]  4.73 us
  transfers between devices with their start and end apart: 5, of which 4 were waited for; matrix products, arithmetic and copies ran while one was open for 0% of the time, Pallas kernels for 0%

commit v1 on v0

v1 whole, which is shorter than its diff:
```python
import jax
import jax.numpy as jnp
import numpy as np
from jax import lax
from jax.experimental import pallas as pl
from jax.experimental.pallas import tpu as pltpu
from jax.sharding import PartitionSpec as P

F32 = jnp.float32
BF16 = jnp.bfloat16


def transforms(half, group):
    size = 2 * half
    slot = np.arange(half)[:, None]
    pos = np.arange(half)[None, :]
    angle = 2 * np.pi * slot * pos / size
    real, imag = np.cos(angle), -np.sin(angle)
    imag[0] = (-1.0) ** np.arange(half)
    forward = np.concatenate([real, imag], 0)
    back_real = 2 * np.cos(angle.T) / size
    back_real[:, 0] = 1 / size
    back_imag = -2 * np.sin(angle.T) / size
    back_imag[:, 0] = (-1.0) ** np.arange(half) / size
    backward = np.concatenate([back_real, back_imag], 1)
    lag = np.arange(size)[None, :]
    angle = 2 * np.pi * slot * lag / size
    real, imag = np.cos(angle), -np.sin(angle)
    imag[0] = 0
    real2 = real.copy()
    real2[0] = (-1.0) ** np.arange(size)
    near = (lag < half).astype(np.float64)
    sign = (-1.0) ** slot
    sign2 = sign.copy()
    sign2[0] = 1
    spectra = np.concatenate(
        [real * near, imag * near, real2 * near, real * sign, imag * sign, real2 * sign2], 0
    )
    eye = np.eye(group)
    return np.kron(forward, eye), np.kron(backward, eye), spectra


def pick_column(block, column):
    rows, cols, width = block.shape
    at = lax.broadcasted_iota(jnp.int32, (rows, rows * cols), 1)
    want = lax.broadcasted_iota(jnp.int32, (rows, rows * cols), 0) * cols + column
    chosen = jnp.where(at == want, 1.0, 0.0).astype(BF16)
    return jnp.dot(
        chosen, block.reshape(rows * cols, width), preferred_element_type=F32
    ).astype(BF16)


def strip_kernel(own_ref, other_ref, strip_ref):
    core = lax.axis_index("row")
    rows, cols, _ = own_ref.shape
    part = cols // 2
    start = pl.multiple_of(core * part, part)
    column = core * (part - 1)
    mine = pick_column(own_ref[:, pl.ds(start, part), :], column)
    theirs = pick_column(other_ref[:, pl.ds(start, part), :], column)
    strip_ref[pl.ds(pl.multiple_of(core * rows, rows), rows), :] = mine
    strip_ref[pl.ds(pl.multiple_of((1 - core) * rows, rows), rows), :] = theirs


def main_kernel(
    own_ref, other_ref, halo_ref, w_in_ref, taps_ref, filt_ref, gain_ref, w_out_ref,
    fwd_ref, bwd_ref, spec_ref,
    mine_ref, send_ref,
    x_ref, p_ref, edge_ref, u_ref, q_ref, prod_ref, h_ref, z_ref, out_ref,
):
    core = lax.axis_index("row")
    rows, cols, width = own_ref.shape
    part = cols // 2
    height = 2 * rows
    start = pl.multiple_of(core * part, part)
    far = pl.multiple_of((1 - core) * part, part)
    inner = core * (part - 1)
    own_at = core * rows
    other_at = (1 - core) * rows

    x_ref[pl.ds(own_at, rows)] = own_ref[:, pl.ds(start, part), :]
    x_ref[pl.ds(other_at, rows)] = other_ref[:, pl.ds(start, part), :]

    p_ref[0] = jnp.zeros(p_ref.shape[1:], F32)
    p_ref[height + 1] = jnp.zeros(p_ref.shape[1:], F32)
    for row in range(0, height, rows):
        got = jnp.dot(
            x_ref[row : row + rows].reshape(rows * part, width),
            w_in_ref[...],
            preferred_element_type=F32,
        )
        p_ref[row + 1 : row + rows + 1] = got.reshape(rows, part, 3 * width)

    own_in = pick_column(own_ref[:, pl.ds(far, part), :], inner)
    other_in = pick_column(other_ref[:, pl.ds(far, part), :], inner)
    first = jnp.where(core == 0, own_in, other_in)
    second = jnp.where(core == 0, other_in, own_in)
    within = jnp.concatenate([first, second], 0)
    outside = halo_ref[...]
    for side, tokens in (
        (0, jnp.where(core == 0, outside, within)),
        (1, jnp.where(core == 0, within, outside)),
    ):
        edge_ref[...] = jnp.zeros(edge_ref.shape, F32)
        edge_ref[8 : 8 + height, :] = jnp.dot(tokens, w_in_ref[...], preferred_element_type=F32)
        total = jnp.zeros((height, 3 * width), F32)
        for a in range(3):
            tap = 3 * a + 2 * side
            total = total + edge_ref[7 + a : 7 + a + height, :] * taps_ref[tap : tap + 1, :]
        u_ref[side] = total.reshape(height // 8, 8, 3 * width)

    lanes = 128
    group = 8
    chunk = 8
    n_group = part // group
    sub = lax.broadcasted_iota(jnp.int32, (group, lanes), 0)
    is_first = sub == 0
    is_last = sub == group - 1

    def mix(base, i):
        row0 = i * chunk
        at = slice(base, base + lanes)
        tap = [
            [jnp.broadcast_to(taps_ref[3 * a + b : 3 * a + b + 1, at], (group, lanes)) for b in range(3)]
            for a in range(3)
        ]
        bias = jnp.broadcast_to(taps_ref[9:10, at], (group, lanes))
        loaded = [
            [p_ref[row0 + r, g * group : (g + 1) * group, at] for g in range(n_group)]
            for r in range(chunk + 2)
        ]
        out = []
        for r in range(chunk):
            u = [
                [
                    loaded[r][g] * tap[0][b] + loaded[r + 1][g] * tap[1][b] + loaded[r + 2][g] * tap[2][b]
                    for b in range(3)
                ]
                for g in range(n_group)
            ]
            right_turn = [pltpu.roll(u[g][0], 1, 0) for g in range(n_group)]
            left_turn = [pltpu.roll(u[g][2], group - 1, 0) for g in range(n_group)]
            west = jnp.broadcast_to(u_ref[0, i, r : r + 1, at], (group, lanes))
            east = jnp.broadcast_to(u_ref[1, i, r : r + 1, at], (group, lanes))
            line = []
            for g in range(n_group):
                before = west if g == 0 else right_turn[g - 1]
                after = east if g == n_group - 1 else left_turn[g + 1]
                value = u[g][1] + bias
                value = value + jnp.where(is_first, before, right_turn[g])
                value = value + jnp.where(is_last, after, left_turn[g])
                line.append(value)
            out.append(line)
        return out

    def stage(i, carry):
        row0 = i * chunk
        for base in range(0, width, lanes):
            at = slice(base, base + lanes)
            query = mix(base, i)
            for g in range(n_group):
                for r in range(chunk):
                    q_ref[g, row0 + r, :, at] = query[r][g]
            key = mix(width + base, i)
            value = mix(2 * width + base, i)
            for g in range(n_group):
                for r in range(0, chunk, 2):
                    two = jnp.concatenate(
                        [key[r][g] * value[r][g], key[r + 1][g] * value[r + 1][g]], 0
                    )
                    prod_ref[g, pl.ds(pl.multiple_of((row0 + r) * group, 2 * group), 2 * group), at] = (
                        two.astype(BF16)
                    )
        return carry

    lax.fori_loop(0, height // chunk, stage, 0)

    filt = filt_ref[...]
    h_ref[...] = jnp.dot(spec_ref[0], filt, preferred_element_type=F32) + jnp.dot(
        spec_ref[1], filt, preferred_element_type=F32
    )
    gain = gain_ref[...]
    h_ref[0:rows, :] = h_ref[0:rows, :] + gain
    h_ref[2 * rows : 3 * rows, :] = h_ref[2 * rows : 3 * rows, :] + gain

    block = rows * group
    for g in range(n_group):
        low = jnp.dot(fwd_ref[...], prod_ref[g, :block], preferred_element_type=F32)
        high = jnp.dot(fwd_ref[...], prod_ref[g, block:], preferred_element_type=F32)
        for k in range(0, rows, 2):
            parts = [[], [], [], []]
            for s in (k, k + 1):
                near_r, near_i, near_2, all_r, all_i, all_2 = (
                    jnp.broadcast_to(h_ref[j * rows + s : j * rows + s + 1, :], (group, width))
                    for j in range(6)
                )
                re, im = slice(s * group, (s + 1) * group), slice(block + s * group, block + (s + 1) * group)
                lr, li, hr, hi = low[re], low[im], high[re], high[im]
                parts[0].append(lr * near_r - li * near_i)
                parts[1].append(lr * near_i + li * near_2)
                parts[2].append(lr * all_r - li * all_i + hr * near_r - hi * near_i)
                parts[3].append(lr * all_i + li * all_2 + hr * near_i + hi * near_2)
            for j in range(4):
                at = (j % 2) * block + k * group
                z_ref[j // 2, at : at + 2 * group, :] = jnp.concatenate(parts[j], 0).astype(BF16)
        for h in range(2):
            conv = jnp.dot(bwd_ref[...], z_ref[h], preferred_element_type=F32)
            gated = q_ref[g, h * rows : (h + 1) * rows].reshape(block, width) * conv
            final = jnp.dot(gated.astype(BF16), w_out_ref[...], preferred_element_type=F32)
            out_ref[h * rows : (h + 1) * rows, g * group : (g + 1) * group, :] = final.reshape(
                rows, group, width
            )
    mine_ref[...] = out_ref[pl.ds(own_at, rows)].astype(BF16)
    send_ref[...] = out_ref[pl.ds(other_at, rows)].astype(BF16)


def on_device(image_tokens, w_in, conv_kernel, conv_bias, long_filter, skip_gain, w_out):
    rows, cols, width = image_tokens.shape
    part, group = cols // 2, 8
    height = 2 * rows
    n_col = lax.axis_size("col")
    core = lax.axis_index("row")
    fwd, bwd, spectra = transforms(rows, group)
    spec_hi = spectra.astype(BF16)
    spec_lo = (spectra - spec_hi.astype(np.float64)).astype(BF16)
    spec = np.stack([spec_hi, spec_lo])
    taps = jnp.concatenate(
        [conv_kernel.reshape(9, 3 * width).astype(F32), conv_bias[None], jnp.zeros((6, 3 * width), F32)], 0
    )

    swap = [(0, 1), (1, 0)]
    other = lax.ppermute(image_tokens, "row", swap)
    vmem = pl.BlockSpec(memory_space=pltpu.VMEM)
    strip = pl.pallas_call(
        strip_kernel,
        out_shape=jax.ShapeDtypeStruct((height, width), BF16),
        in_specs=[vmem, vmem],
        out_specs=vmem,
    )(image_tokens, other)
    pairs = []
    for j in range(n_col - 1):
        pairs += [(n_col + j, j + 1), (j + 1, n_col + j)]
    halo = lax.ppermute(strip, ("row", "col"), pairs)
    half_shape = jax.ShapeDtypeStruct((rows, part, width), BF16)
    mine, send = pl.pallas_call(
        main_kernel,
        out_shape=(half_shape, half_shape),
        in_specs=[vmem] * 11,
        out_specs=(vmem, vmem),
        scratch_shapes=[
            pltpu.VMEM((height, part, width), BF16),
            pltpu.VMEM((height + 2, part, 3 * width), F32),
            pltpu.VMEM((height + 16, 3 * width), F32),
            pltpu.VMEM((2, height // 8, 8, 3 * width), F32),
            pltpu.VMEM((part // group, height, group, width), F32),
            pltpu.VMEM((part // group, height * group, width), BF16),
            pltpu.VMEM((6 * rows, width), F32),
            pltpu.VMEM((2, 2 * rows * group, width), BF16),
            pltpu.VMEM((height, part, width), F32),
        ],
        compiler_params=pltpu.CompilerParams(vmem_limit_bytes=32 * 1024 * 1024),
    )(
        image_tokens, other, halo, w_in, taps, long_filter, skip_gain[None], w_out,
        fwd.astype(BF16), bwd.astype(BF16), spec,
    )
    theirs = lax.ppermute(send, "row", swap)
    return jnp.where(
        core == 0,
        jnp.concatenate([mine, theirs], 1),
        jnp.concatenate([theirs, mine], 1),
    )


def solution(mesh):
    in_specs = (P("row", "col", None), P(), P(), P(), P(), P(), P())
    out_specs = P("row", "col", None)
    return jax.shard_map(
        on_device, mesh=mesh, in_specs=in_specs, out_specs=out_specs, check_vma=False
    )
```

time: 105 us -> 24.7 us (0.24)
  the two profiles are of different devices: /device:TPU:1 before, /device:TPU:7 now
where the time goes in v1:
time: 24.7 us; the launch traced here: 24.3 us
  Pallas kernels  7.38 us (30%)
  waiting for transfers between devices  6.18 us (25%)
  local copies, waits for them, and re-layouts  5.42 us (22%)
  starting transfers between devices  4.11 us (17%)
  other arithmetic  1.12 us (5%)
    pallas_call x1, Pallas kernels, on_device(): pl.pallas_call(main_kernel, out_shape=(half_shape, half_shape), in_specs=...  5.32 us
    unnamed x22, local copies, waits for them, and re-layouts  4.6 us
    ppermute x1, waiting for transfers between devices, on_device(): halo = lax.ppermute(strip, ('row', 'col'), pairs)  3.78 us
    ppermute x1, starting transfers between devices, on_device(): halo = lax.ppermute(strip, ('row', 'col'), pairs)  3.37 us
    pallas_call x1, Pallas kernels, on_device(): pl.pallas_call(strip_kernel, out_shape=jax.ShapeDtypeStruct((height, widt...  2.06 us
    ppermute x1, waiting for transfers between devices, on_device(): theirs = lax.ppermute(send, 'row', swap)  1.52 us
    select_n x1, other arithmetic, on_device(): jnp.where(core == 0, jnp.concatenate([mine, theirs], 1), jnp.concatenate(...  1.04 us
    ppermute x1, waiting for transfers between devices, on_device(): other = lax.ppermute(image_tokens, 'row', swap)  0.89 us
  transfers between devices with their start and end apart: 3, of which 3 were waited for; matrix products, arithmetic and copies ran while one was open for 4% of the time, Pallas kernels for 0%

profile of v1, /device:TPU:7, one launch (start us, length us, event | category | flops | bytes accessed | tf_op | source)
XLA Modules:
  0.0 24.3 jit_solution(9205305681797329902)
XLA Ops:
  0.0 0.0 copy-start.10
  0.0 0.7 %collective-permute-start = (bf16[32,32,256]{2,1,0:T(8,128)(2,1)}, bf16[32,32,256]{2,1,0:T(8,128)(2,1)S(1)}, u32[]{:S(2)}, u32[]{:S(2)}) collective-permute-start(bf16[32,32,256]{2,1,0:T(8,128)(2,1)} %own_ref.3), channel_id=1, source_target_pairs={{0,16},{16,0},{1,17},{17,1},{2,18},{18,2},{3,19},{19,3},{4,20},{20... | collective-permute-start | bytes 1572872 | tf_op jit(solution)/shard_map/ppermute | solution.py:232
  0.7 0.0 copy-start.8
  0.7 0.7 %reshape.3 = f32[9,768]{1,0:T(8,128)S(1)} reshape(bf16[3,3,768]{2,1,0:T(4,128)(2,1)} %param.12) | data formatting | bytes 41472 | tf_op jit(solution)/shard_map/convert_element_type | solution.py:228
  1.4 0.0 copy-done.10
  1.5 0.1 pad.6.clone
  1.5 0.0 copy-start
  1.5 0.0 copy-start.3
  1.5 0.9 %collective-permute-done.other_ref = bf16[32,32,256]{2,1,0:T(8,128)(2,1)S(1)} collective-permute-done((bf16[32,32,256]{2,1,0:T(8,128)(2,1)}, bf16[32,32,256]{2,1,0:T(8,128)(2,1)S(1)}, u32[]{:S(2)}, u32[]{:S(2)}) %collective-permute-start) | collective-permute-done | bytes 524320 | tf_op jit(solution)/shard_map/ppermute | solution.py:232
  2.4 0.0 copy-start.1
  2.4 0.8 %copy-done.1 = bf16[32,32,256]{2,1,0:T(8,128)(2,1)} copy-done((bf16[32,32,256]{2,1,0:T(8,128)(2,1)}, bf16[32,32,256]{2,1,0:T(8,128)(2,1)S(1)}, u32[]{:S(2)}) %copy-start.1) | copy-done | bytes 524312
  3.2 0.0 copy-start.4
  3.2 2.1 %shard_map.100 = bf16[64,256]{1,0:T(8,128)(2,1)} custom-call(bf16[32,32,256]{2,1,0:T(8,128)(2,1)} %own_ref.3, bf16[32,32,256]{2,1,0:T(8,128)(2,1)} %copy-done.1), custom_call_target="tpu_custom_call" | custom-call | tf_op jit(solution)/shard_map/pallas_call | solution.py:234
  5.3 3.4 %collective-permute-start.1 = (bf16[64,256]{1,0:T(8,128)(2,1)}, bf16[64,256]{1,0:T(8,128)(2,1)S(1)}, u32[]{:S(2)}, u32[]{:S(2)}) collective-permute-start(bf16[64,256]{1,0:T(8,128)(2,1)} %shard_map.100), channel_id=1, source_target_pairs={{16,1},{1,16},{17,2},{2,17},{18,3},{3,18},{19,4},{4,19},{20,5},{5,... | collective-permute-start | bytes 98312 | tf_op jit(solution)/shard_map/ppermute | solution.py:243
  8.7 0.1 maximum_maximum_fusion.taps_ref
  8.7 0.0 copy-start.9
  8.7 3.8 %collective-permute-done.1.halo_ref = bf16[64,256]{1,0:T(8,128)(2,1)S(1)} collective-permute-done((bf16[64,256]{1,0:T(8,128)(2,1)}, bf16[64,256]{1,0:T(8,128)(2,1)S(1)}, u32[]{:S(2)}, u32[]{:S(2)}) %collective-permute-start.1) | collective-permute-done | bytes 32800 | tf_op jit(solution)/shard_map/ppermute | solution.py:243
  12.5 0.0 copy-done.8
  12.5 0.0 copy-done
  12.5 0.0 copy-done.3
  12.5 0.0 copy-done.4
  12.5 0.0 copy-done.9
  12.5 0.0 copy-start.2
  12.6 1.0 %copy-done.2 = bf16[32,32,256]{2,1,0:T(8,128)(2,1)S(1)} copy-done((bf16[32,32,256]{2,1,0:T(8,128)(2,1)S(1)}, bf16[32,32,256]{2,1,0:T(8,128)(2,1)}, u32[]{:S(2)}) %copy-start.2) | copy-done | bytes 524312
  13.6 0.0 copy-start.5
  13.6 0.9 %copy-done.5 = bf16[256,512]{1,0:T(8,128)(2,1)S(1)} copy-done((bf16[256,512]{1,0:T(8,128)(2,1)S(1)}, bf16[256,512]{1,0:T(8,128)(2,1)}, u32[]{:S(2)}) %copy-start.5) | copy-done | bytes 262168
  14.5 0.0 copy-start.6
  14.5 0.9 %copy-done.6 = bf16[256,256]{1,0:T(8,128)(2,1)S(1)} copy-done((bf16[256,256]{1,0:T(8,128)(2,1)S(1)}, bf16[256,256]{1,0:T(8,128)(2,1)}, u32[]{:S(2)}) %copy-start.6) | copy-done | bytes 131096
  15.4 0.0 copy-start.7
  15.4 0.9 %copy-done.7 = bf16[2,192,64]{2,1,0:T(8,128)(2,1)S(1)} copy-done((bf16[2,192,64]{2,1,0:T(8,128)(2,1)S(1)}, bf16[2,192,64]{2,1,0:T(8,128)(2,1)}, u32[]{:S(2)}) %copy-start.7) | copy-done | bytes 49176
  16.3 5.3 %shard_map.101 = (bf16[32,16,256]{2,1,0:T(8,128)(2,1)S(1)}, bf16[32,16,256]{2,1,0:T(8,128)(2,1)S(1)}) custom-call(bf16[32,32,256]{2,1,0:T(8,128)(2,1)S(1)} %copy-done, bf16[32,32,256]{2,1,0:T(8,128)(2,1)S(1)} %copy-done.2, bf16[64,256]{1,0:T(8,128)(2,1)S(1)} %collective-permute-done.1.halo_ref, bf16[256,768]{1,0:T(8,128)(2,1)S(1)} %copy-done.3, ...), custom_call_target="tpu_custom_call" | custom-call | tf_op jit(solution)/shard_map/pallas_call | solution.py:245
  21.7 0.1 collective-permute-start.2
  21.7 1.5 %collective-permute-done.2 = bf16[32,16,256]{2,1,0:T(8,128)(2,1)S(1)} collective-permute-done((bf16[32,16,256]{2,1,0:T(8,128)(2,1)S(1)}, bf16[32,16,256]{2,1,0:T(8,128)(2,1)S(1)}, u32[]{:S(2)}, u32[]{:S(2)}) %collective-permute-start.2) | collective-permute-done | bytes 262176 | tf_op jit(solution)/shard_map/ppermute | solution.py:266
  23.3 1.0 %maximum_select_fusion = bf16[32,32,256]{2,1,0:T(8,128)(2,1)} fusion(bf16[32,16,256]{2,1,0:T(8,128)(2,1)S(1)} %collective-permute-done.2, bf16[32,16,256]{2,1,0:T(8,128)(2,1)S(1)} %get-tuple-element.7, pred[]{:T(512)S(6)} %eq.3), kind=kLoop, calls=%fused_computation | loop fusion | flops 2359296 | bytes 1048577 | tf_op jit(solution)/shard_map/jit(_where)/select_n | solution.py:267
  (2 shorter events, 0.0 us)
Async XLA Ops:
  0.0 1.4 %copy-start.10 = (f32[768]{0:T(1024)S(1)}, f32[768]{0:T(1024)}, u32[]{:S(2)}) copy-start(f32[768]{0:T(1024)} %param.13) | copy-start | bytes 9220
  0.0 2.4 %collective-permute-start = (bf16[32,32,256]{2,1,0:T(8,128)(2,1)}, bf16[32,32,256]{2,1,0:T(8,128)(2,1)S(1)}, u32[]{:S(2)}, u32[]{:S(2)}) collective-permute-start(bf16[32,32,256]{2,1,0:T(8,128)(2,1)} %own_ref.3), channel_id=1, source_target_pairs={{0,16},{16,0},{1,17},{17,1},{2,18},{18,2},{3,19},{19,3},{4,20},{20... | collective-permute-start | bytes 1572872 | tf_op jit(solution)/shard_map/ppermute | solution.py:232
  0.7 11.8 %copy-start.8 = (bf16[64,256]{1,0:T(8,128)(2,1)S(1)}, bf16[64,256]{1,0:T(8,128)(2,1)}, u32[]{:S(2)}) copy-start(bf16[64,256]{1,0:T(8,128)(2,1)} %filt_ref.1) | copy-start | bytes 98308
  1.5 11.0 %copy-start = (bf16[32,32,256]{2,1,0:T(8,128)(2,1)S(1)}, bf16[32,32,256]{2,1,0:T(8,128)(2,1)}, u32[]{:S(2)}) copy-start(bf16[32,32,256]{2,1,0:T(8,128)(2,1)} %own_ref.3) | copy-start | bytes 1572868
  1.5 11.0 %copy-start.3 = (bf16[256,768]{1,0:T(8,128)(2,1)S(1)}, bf16[256,768]{1,0:T(8,128)(2,1)}, u32[]{:S(2)}) copy-start(bf16[256,768]{1,0:T(8,128)(2,1)} %w_in_ref.1) | copy-start | bytes 1179652
  2.4 0.8 %copy-start.1 = (bf16[32,32,256]{2,1,0:T(8,128)(2,1)}, bf16[32,32,256]{2,1,0:T(8,128)(2,1)S(1)}, u32[]{:S(2)}) copy-start(bf16[32,32,256]{2,1,0:T(8,128)(2,1)S(1)} %collective-permute-done.other_ref) | copy-start | bytes 1572868
  3.2 9.3 %copy-start.4 = (bf16[512,256]{1,0:T(8,128)(2,1)S(1)}, bf16[512,256]{1,0:T(8,128)(2,1)}, u32[]{:S(2)}) copy-start(bf16[512,256]{1,0:T(8,128)(2,1)} %constant.16.clone.fwd_ref) | copy-start | bytes 786436
  5.3 7.2 %collective-permute-start.1 = (bf16[64,256]{1,0:T(8,128)(2,1)}, bf16[64,256]{1,0:T(8,128)(2,1)S(1)}, u32[]{:S(2)}, u32[]{:S(2)}) collective-permute-start(bf16[64,256]{1,0:T(8,128)(2,1)} %shard_map.100), channel_id=1, source_target_pairs={{16,1},{1,16},{17,2},{2,17},{18,3},{3,18},{19,4},{4,19},{20,5},{5,... | collective-permute-start | bytes 98312 | tf_op jit(solution)/shard_map/ppermute | solution.py:243
  8.7 3.8 %copy-start.9 = (f32[256]{0:T(256)S(1)}, f32[256]{0:T(256)}, u32[]{:S(2)}) copy-start(f32[256]{0:T(256)} %param.15) | copy-start | bytes 3076
  12.5 1.0 %copy-start.2 = (bf16[32,32,256]{2,1,0:T(8,128)(2,1)S(1)}, bf16[32,32,256]{2,1,0:T(8,128)(2,1)}, u32[]{:S(2)}) copy-start(bf16[32,32,256]{2,1,0:T(8,128)(2,1)} %copy-done.1) | copy-start | bytes 1572868
  13.6 0.9 %copy-start.5 = (bf16[256,512]{1,0:T(8,128)(2,1)S(1)}, bf16[256,512]{1,0:T(8,128)(2,1)}, u32[]{:S(2)}) copy-start(bf16[256,512]{1,0:T(8,128)(2,1)} %constant.17.clone.bwd_ref) | copy-start | bytes 786436
  14.5 0.9 %copy-start.6 = (bf16[256,256]{1,0:T(8,128)(2,1)S(1)}, bf16[256,256]{1,0:T(8,128)(2,1)}, u32[]{:S(2)}) copy-start(bf16[256,256]{1,0:T(8,128)(2,1)} %w_out_ref.1) | copy-start | bytes 393220
  15.4 0.9 %copy-start.7 = (bf16[2,192,64]{2,1,0:T(8,128)(2,1)S(1)}, bf16[2,192,64]{2,1,0:T(8,128)(2,1)}, u32[]{:S(2)}) copy-start(bf16[2,192,64]{2,1,0:T(8,128)(2,1)} %constant.18.clone.spec_ref) | copy-start | bytes 147460
  21.7 1.6 %collective-permute-start.2 = (bf16[32,16,256]{2,1,0:T(8,128)(2,1)S(1)}, bf16[32,16,256]{2,1,0:T(8,128)(2,1)S(1)}, u32[]{:S(2)}, u32[]{:S(2)}) collective-permute-start(bf16[32,16,256]{2,1,0:T(8,128)(2,1)S(1)} %get-tuple-element.8), channel_id=1, source_target_pairs={{0,16},{16,0},{1,17},{17,1},{2,18},{18,2},{3,19},{19,3},{4,20},{20... | collective-permute-start | bytes 786440 | tf_op jit(solution)/shard_map/ppermute | solution.py:266

commit v2 on v0

v2 whole, which is shorter than its diff:
```python
import jax
import jax.numpy as jnp
import numpy as np
from jax import lax
from jax.experimental import pallas as pl
from jax.experimental.layout import Layout, with_layout_constraint
from jax.experimental.pallas import tpu as pltpu
from jax.sharding import PartitionSpec as P

F32 = jnp.float32
BF16 = jnp.bfloat16


def transforms(half, group):
    size = 2 * half
    slot = np.arange(half)[:, None]
    pos = np.arange(half)[None, :]
    angle = 2 * np.pi * slot * pos / size
    real, imag = np.cos(angle), -np.sin(angle)
    imag[0] = (-1.0) ** np.arange(half)
    forward = np.concatenate([real, imag], 0)
    back_real = 2 * np.cos(angle.T) / size
    back_real[:, 0] = 1 / size
    back_imag = -2 * np.sin(angle.T) / size
    back_imag[:, 0] = (-1.0) ** np.arange(half) / size
    backward = np.concatenate([back_real, back_imag], 1)
    lag = np.arange(size)[None, :]
    angle = 2 * np.pi * slot * lag / size
    real, imag = np.cos(angle), -np.sin(angle)
    imag[0] = 0
    real2 = real.copy()
    real2[0] = (-1.0) ** np.arange(size)
    near = (lag < half).astype(np.float64)
    sign = (-1.0) ** slot
    sign2 = sign.copy()
    sign2[0] = 1
    spectra = np.concatenate(
        [real * near, imag * near, real2 * near, real * sign, imag * sign, real2 * sign2], 0
    )
    eye = np.eye(group)
    return np.kron(forward, eye), np.kron(backward, eye), spectra


LANES = 128
GROUP = 8
CHUNK = 8


def prep_kernel(
    own_hbm, w_in_hbm, w_out_hbm, fwd_hbm, bwd_hbm, spec_hbm, filt_hbm, gain_hbm, kernel_hbm, bias_hbm,
    own_ref, w_in_ref, w_out_ref, fwd_ref, bwd_ref, taps_ref, h_ref,
    spec_ref, filt_ref, gain_ref, kernel_ref, bias_ref, sems,
):
    rows, part, _ = own_ref.shape
    start = pl.multiple_of(lax.axis_index("row") * part, part)
    moves = [
        (own_hbm.at[:, pl.ds(start, part), :], own_ref),
        (w_in_hbm, w_in_ref),
        (spec_hbm, spec_ref),
        (filt_hbm, filt_ref),
        (gain_hbm, gain_ref),
        (kernel_hbm, kernel_ref),
        (bias_hbm, bias_ref),
        (fwd_hbm, fwd_ref),
        (bwd_hbm, bwd_ref),
        (w_out_hbm, w_out_ref),
    ]
    copies = [pltpu.make_async_copy(src, dst, sems.at[i]) for i, (src, dst) in enumerate(moves)]
    for copy in copies:
        copy.start()
    for copy in copies:
        copy.wait()
    for a in range(3):
        taps_ref[3 * a : 3 * a + 3, :] = kernel_ref[a].astype(F32)
    taps_ref[9:10, :] = bias_ref[...]
    filt = filt_ref[...]
    h_ref[...] = jnp.dot(spec_ref[0], filt, preferred_element_type=F32) + jnp.dot(
        spec_ref[1], filt, preferred_element_type=F32
    )
    gain = gain_ref[...]
    h_ref[0:rows, :] = h_ref[0:rows, :] + gain
    h_ref[2 * rows : 3 * rows, :] = h_ref[2 * rows : 3 * rows, :] + gain


def edge_terms(tokens, taps, w_in_ref, edge_ref):
    height = tokens.shape[0]
    edge_ref[0:8, :] = jnp.zeros((8, edge_ref.shape[1]), F32)
    edge_ref[8 + height : 16 + height, :] = jnp.zeros((8, edge_ref.shape[1]), F32)
    edge_ref[8 : 8 + height, :] = jnp.dot(tokens, w_in_ref[...], preferred_element_type=F32)
    total = edge_ref[7 : 7 + height, :] * taps[0]
    for a in (1, 2):
        total = total + edge_ref[7 + a : 7 + a + height, :] * taps[a]
    return total


def column_group(mixed, fwd_ref, bwd_ref, w_out_ref, h_ref, prod_ref, z_ref, put):
    height_group, width = prod_ref.shape
    height = height_group // GROUP
    rows = height // 2
    block = rows * GROUP
    for row in range(0, height, 2):
        for base in range(0, width, LANES):
            two = [mixed(r, width + base) * mixed(r, 2 * width + base) for r in (row, row + 1)]
            prod_ref[row * GROUP : (row + 2) * GROUP, base : base + LANES] = jnp.concatenate(
                two, 0
            ).astype(BF16)
    low = jnp.dot(fwd_ref[...], prod_ref[:block], preferred_element_type=F32)
    high = jnp.dot(fwd_ref[...], prod_ref[block:], preferred_element_type=F32)
    for k in range(0, rows, 2):
        parts = [[], [], [], []]
        for s in (k, k + 1):
            near_r, near_i, near_2, all_r, all_i, all_2 = (
                jnp.broadcast_to(h_ref[j * rows + s : j * rows + s + 1, :], (GROUP, width))
                for j in range(6)
            )
            re, im = slice(s * GROUP, (s + 1) * GROUP), slice(block + s * GROUP, block + (s + 1) * GROUP)
            lr, li, hr, hi = low[re], low[im], high[re], high[im]
            parts[0].append(lr * near_r - li * near_i)
            parts[1].append(lr * near_i + li * near_2)
            parts[2].append(lr * all_r - li * all_i + hr * near_r - hi * near_i)
            parts[3].append(lr * all_i + li * all_2 + hr * near_i + hi * near_2)
        for j in range(4):
            at = (j % 2) * block + k * GROUP
            z_ref[j // 2, at : at + 2 * GROUP, :] = jnp.concatenate(parts[j], 0).astype(BF16)
    for h in range(2):
        conv = jnp.dot(bwd_ref[...], z_ref[h], preferred_element_type=F32)
        gated = []
        for r in range(rows):
            line = [
                mixed(h * rows + r, base) * conv[r * GROUP : (r + 1) * GROUP, base : base + LANES]
                for base in range(0, width, LANES)
            ]
            gated.append(jnp.concatenate(line, 1))
        final = jnp.dot(
            jnp.concatenate(gated, 0).astype(BF16), w_out_ref[...], preferred_element_type=F32
        )
        put(h, final.reshape(rows, GROUP, width))


def inner_kernel(
    own_ref, other_ref, within_ref, w_in_ref, taps_ref, fwd_ref, bwd_ref, w_out_ref, h_ref,
    mixed_ref, inner_ref,
    p_ref, edge_ref, u_ref, prod_ref, z_ref,
):
    core = lax.axis_index("row")
    rows, part, width = own_ref.shape
    height = 2 * rows
    start = pl.multiple_of(core * part, part)
    n_group = part // GROUP

    p_ref[0] = jnp.zeros(p_ref.shape[1:], F32)
    p_ref[height + 1] = jnp.zeros(p_ref.shape[1:], F32)
    for at, tokens in (
        (core * rows, own_ref[...]),
        ((1 - core) * rows, other_ref[:, pl.ds(start, part), :]),
    ):
        got = jnp.dot(
            tokens.reshape(rows * part, width), w_in_ref[...], preferred_element_type=F32
        )
        p_ref[pl.ds(at + 1, rows)] = got.reshape(rows, part, 3 * width)

    taps = [
        jnp.where(core == 0, taps_ref[3 * a + 2 : 3 * a + 3, :], taps_ref[3 * a : 3 * a + 1, :])
        for a in range(3)
    ]
    total = edge_terms(within_ref[...], taps, w_in_ref, edge_ref)
    u_ref[1 - core] = total.reshape(height // 8, 8, 3 * width)
    u_ref[core] = jnp.zeros(u_ref.shape[1:], F32)

    sub = lax.broadcasted_iota(jnp.int32, (GROUP, LANES), 0)
    is_first = sub == 0
    is_last = sub == GROUP - 1

    def stage(i, carry):
        row0 = i * CHUNK
        for base in range(0, 3 * width, LANES):
            at = slice(base, base + LANES)
            tap = [
                [
                    jnp.broadcast_to(taps_ref[3 * a + b : 3 * a + b + 1, at], (GROUP, LANES))
                    for b in range(3)
                ]
                for a in range(3)
            ]
            bias = jnp.broadcast_to(taps_ref[9:10, at], (GROUP, LANES))
            loaded = [
                [p_ref[row0 + r, g * GROUP : (g + 1) * GROUP, at] for g in range(n_group)]
                for r in range(CHUNK + 2)
            ]
            for r in range(CHUNK):
                u = [
                    [
                        loaded[r][g] * tap[0][b]
                        + loaded[r + 1][g] * tap[1][b]
                        + loaded[r + 2][g] * tap[2][b]
                        for b in range(3)
                    ]
                    for g in range(n_group)
                ]
                right_turn = [pltpu.roll(u[g][0], 1, 0) for g in range(n_group)]
                left_turn = [pltpu.roll(u[g][2], GROUP - 1, 0) for g in range(n_group)]
                west = jnp.broadcast_to(u_ref[0, i, r : r + 1, at], (GROUP, LANES))
                east = jnp.broadcast_to(u_ref[1, i, r : r + 1, at], (GROUP, LANES))
                for g in range(n_group):
                    before = west if g == 0 else right_turn[g - 1]
                    after = east if g == n_group - 1 else left_turn[g + 1]
                    value = u[g][1] + bias
                    value = value + jnp.where(is_first, before, right_turn[g])
                    value = value + jnp.where(is_last, after, left_turn[g])
                    slot = core if g == 0 else 1 - core
                    mixed_ref[slot, row0 + r, :, at] = value
        return carry

    lax.fori_loop(0, height // CHUNK, stage, 0)

    def put(h, final):
        inner_ref[h * rows : (h + 1) * rows] = final

    column_group(
        lambda r, base: mixed_ref[1, r, :, base : base + LANES],
        fwd_ref, bwd_ref, w_out_ref, h_ref, prod_ref, z_ref, put,
    )


def edge_kernel(
    halo_ref, mixed_ref, inner_ref, w_in_ref, taps_ref, fwd_ref, bwd_ref, w_out_ref, h_ref,
    mine_ref, send_ref,
    edge_ref, u_ref, fix_ref, prod_ref, z_ref, out_ref,
):
    core = lax.axis_index("row")
    rows, part, width = mine_ref.shape
    height = 2 * rows
    taps = [
        jnp.where(core == 0, taps_ref[3 * a : 3 * a + 1, :], taps_ref[3 * a + 2 : 3 * a + 3, :])
        for a in range(3)
    ]
    total = edge_terms(halo_ref[...], taps, w_in_ref, edge_ref)
    u_ref[...] = total.reshape(height // 8, 8, 3 * width)
    sub = lax.broadcasted_iota(jnp.int32, (GROUP, LANES), 0)
    at_edge = sub == core * (GROUP - 1)
    for base in range(0, 3 * width, LANES):
        at = slice(base, base + LANES)
        for r in range(height):
            add = jnp.broadcast_to(u_ref[r // 8, r % 8 : r % 8 + 1, at], (GROUP, LANES))
            fix_ref[r, :, at] = mixed_ref[0, r, :, at] + jnp.where(at_edge, add, 0.0)

    def put(h, final):
        out_ref[core, h * rows : (h + 1) * rows] = final

    column_group(
        lambda r, base: fix_ref[r, :, base : base + LANES],
        fwd_ref, bwd_ref, w_out_ref, h_ref, prod_ref, z_ref, put,
    )
    out_ref[1 - core] = inner_ref[...]
    for ref, at in ((mine_ref, core * rows), (send_ref, (1 - core) * rows)):
        ref[...] = jnp.concatenate(
            [out_ref[g, pl.ds(at, rows)] for g in range(part // GROUP)], 1
        ).astype(BF16)


def store_kernel(mine_ref, full_hbm, sem):
    _, part, _ = mine_ref.shape
    start = pl.multiple_of(lax.axis_index("row") * part, part)
    copy = pltpu.make_async_copy(mine_ref, full_hbm.at[:, pl.ds(start, part), :], sem)
    copy.start()
    copy.wait()


def fill_kernel(full_in, theirs_ref, full_hbm, sem):
    _, part, _ = theirs_ref.shape
    start = pl.multiple_of((1 - lax.axis_index("row")) * part, part)
    copy = pltpu.make_async_copy(theirs_ref, full_hbm.at[:, pl.ds(start, part), :], sem)
    copy.start()
    copy.wait()


def on_device(image_tokens, w_in, conv_kernel, conv_bias, long_filter, skip_gain, w_out):
    rows, cols, width = image_tokens.shape
    part = cols // 2
    height = 2 * rows
    n_col = lax.axis_size("col")
    core = lax.axis_index("row")
    fwd, bwd, spectra = transforms(rows, GROUP)
    spec_hi = spectra.astype(BF16)
    spec_lo = (spectra - spec_hi.astype(np.float64)).astype(BF16)
    spec = np.stack([spec_hi, spec_lo])
    vmem = pl.BlockSpec(memory_space=pltpu.VMEM)
    hbm = pl.BlockSpec(memory_space=pltpu.HBM)
    shape = jax.ShapeDtypeStruct
    limit = pltpu.CompilerParams(vmem_limit_bytes=24 * 1024 * 1024)

    swap = [(0, 1), (1, 0)]
    rowmajor = Layout((0, 1, 2))
    image_tokens = with_layout_constraint(image_tokens, rowmajor)
    other = with_layout_constraint(lax.ppermute(image_tokens, "row", swap), rowmajor)

    def keep(array):
        return pltpu.with_memory_space_constraint(array, pltpu.HBM)

    own, w_in_v, w_out_v, fwd_v, bwd_v, taps, spectrum = pl.pallas_call(
        prep_kernel,
        out_shape=(
            shape((rows, part, width), BF16),
            shape(w_in.shape, BF16),
            shape(w_out.shape, BF16),
            shape(fwd.shape, BF16),
            shape(bwd.shape, BF16),
            shape((16, 3 * width), F32),
            shape((6 * rows, width), F32),
        ),
        in_specs=[hbm] * 10,
        out_specs=(vmem,) * 7,
        scratch_shapes=[
            pltpu.VMEM(spec.shape, BF16),
            pltpu.VMEM(long_filter.shape, BF16),
            pltpu.VMEM((1, width), F32),
            pltpu.VMEM(conv_kernel.shape, BF16),
            pltpu.VMEM((1, 3 * width), F32),
            pltpu.SemaphoreType.DMA((10,)),
        ],
        compiler_params=limit,
        cost_estimate=pl.CostEstimate(flops=0, bytes_accessed=3 * 1024 * 1024, transcendentals=0),
    )(
        keep(image_tokens), keep(w_in), keep(w_out), keep(fwd.astype(BF16)), keep(bwd.astype(BF16)),
        keep(spec), keep(long_filter), keep(skip_gain[None]), keep(conv_kernel), keep(conv_bias[None]),
    )

    def by_core(low, high):
        return jnp.where(core == 0, low, high)

    def column(low, high):
        mine = by_core(image_tokens[:, low], image_tokens[:, high])
        theirs = by_core(other[:, low], other[:, high])
        return jnp.concatenate([by_core(mine, theirs), by_core(theirs, mine)], 0)

    pairs = []
    for j in range(n_col - 1):
        pairs += [(n_col + j, j + 1), (j + 1, n_col + j)]
    halo = lax.ppermute(column(0, cols - 1), ("row", "col"), pairs)
    within = column(part, part - 1)
    mixed, inner = pl.pallas_call(
        inner_kernel,
        out_shape=(
            shape((2, height, GROUP, 3 * width), F32),
            shape((height, GROUP, width), F32),
        ),
        in_specs=[vmem] * 9,
        out_specs=(vmem,) * 2,
        scratch_shapes=[
            pltpu.VMEM((height + 2, part, 3 * width), F32),
            pltpu.VMEM((height + 16, 3 * width), F32),
            pltpu.VMEM((2, height // 8, 8, 3 * width), F32),
            pltpu.VMEM((height * GROUP, width), BF16),
            pltpu.VMEM((2, 2 * rows * GROUP, width), BF16),
        ],
        compiler_params=limit,
        cost_estimate=pl.CostEstimate(flops=10**9, bytes_accessed=12 * 1024 * 1024, transcendentals=0),
    )(own, other, within, w_in_v, taps, fwd_v, bwd_v, w_out_v, spectrum)
    half_shape = shape((rows, part, width), BF16)
    mine, send = pl.pallas_call(
        edge_kernel,
        out_shape=(half_shape, half_shape),
        in_specs=[vmem] * 9,
        out_specs=(vmem, vmem),
        scratch_shapes=[
            pltpu.VMEM((height + 16, 3 * width), F32),
            pltpu.VMEM((height // 8, 8, 3 * width), F32),
            pltpu.VMEM((height, GROUP, 3 * width), F32),
            pltpu.VMEM((height * GROUP, width), BF16),
            pltpu.VMEM((2, 2 * rows * GROUP, width), BF16),
            pltpu.VMEM((2, height, GROUP, width), F32),
        ],
        compiler_params=limit,
        cost_estimate=pl.CostEstimate(flops=3 * 10**8, bytes_accessed=4 * 1024 * 1024, transcendentals=0),
    )(halo, mixed, inner, w_in_v, taps, fwd_v, bwd_v, w_out_v, spectrum)
    theirs = lax.ppermute(send, "row", swap)
    full_shape = shape((rows, cols, width), BF16)
    full = pl.pallas_call(
        store_kernel,
        out_shape=full_shape,
        in_specs=[vmem],
        out_specs=hbm,
        scratch_shapes=[pltpu.SemaphoreType.DMA],
        cost_estimate=pl.CostEstimate(flops=0, bytes_accessed=512 * 1024, transcendentals=0),
    )(mine)
    return pl.pallas_call(
        fill_kernel,
        out_shape=full_shape,
        in_specs=[hbm, vmem],
        out_specs=hbm,
        scratch_shapes=[pltpu.SemaphoreType.DMA],
        input_output_aliases={0: 0},
        cost_estimate=pl.CostEstimate(flops=0, bytes_accessed=512 * 1024, transcendentals=0),
    )(full, theirs)


def solution(mesh):
    in_specs = (P("row", "col", None), P(), P(), P(), P(), P(), P())
    out_specs = P("row", "col", None)
    return jax.shard_map(
        on_device, mesh=mesh, in_specs=in_specs, out_specs=out_specs, check_vma=False
    )
```

time: 105 us -> 20 us (0.19)
  the two profiles are of different devices: /device:TPU:1 before, /device:TPU:0 now
where the time goes in v2:
time: 20 us; the launch traced here: 19.7 us
  Pallas kernels  10.5 us (52%)
  starting transfers between devices  4.97 us (25%)
  local copies, waits for them, and re-layouts  3.98 us (20%)
    pallas_call x1, Pallas kernels, on_device(): pl.pallas_call(inner_kernel, out_shape=(shape((2, height, GROUP, 3 * widt...  4.06 us
    ppermute x1, starting transfers between devices, on_device(): theirs = lax.ppermute(send, 'row', swap)  3.85 us
    pallas_call x1, Pallas kernels, on_device(): pl.pallas_call(fill_kernel, out_shape=full_shape, in_specs=[hbm, vmem], o...  1.66 us
    pallas_call x1, Pallas kernels, on_device(): pl.pallas_call(store_kernel, out_shape=full_shape, in_specs=[vmem], out_s...  1.66 us
    pallas_call x1, Pallas kernels, on_device(): pl.pallas_call(prep_kernel, out_shape=(shape((rows, part, width), BF16),...  1.63 us
    pallas_call x1, Pallas kernels, on_device(): pl.pallas_call(edge_kernel, out_shape=(half_shape, half_shape), in_specs=...  1.52 us
    unnamed x4, local copies, waits for them, and re-layouts  1.4 us
    broadcast_in_dim x1, local copies, waits for them, and re-layouts, on_device(): conv_bias[None]  1.27 us
  transfers between devices with their start and end apart: 3, of which 0 were waited for; matrix products, arithmetic and copies ran while one was open for 13% of the time, Pallas kernels for 37%

profile of v2, /device:TPU:0, one launch (start us, length us, event | category | flops | bytes accessed | tf_op | source)
XLA Modules:
  0.0 19.7 jit_solution(2158315001003901890)
XLA Ops:
  0.0 0.5 %collective-permute-start = (bf16[32,32,256]{2,1,0:T(8,128)(2,1)}, bf16[32,32,256]{2,1,0:T(8,128)(2,1)S(1)}, u32[]{:S(2)}, u32[]{:S(2)}) collective-permute-start(bf16[32,32,256]{2,1,0:T(8,128)(2,1)} %own_hbm), channel_id=1, source_target_pairs={{0,16},{16,0},{1,17},{17,1},{2,18},{18,2},{3,19},{19,3},{4,20},{20... | collective-permute-start | bytes 1572872 | tf_op jit(solution)/shard_map/ppermute | solution.py:295
  0.5 1.3 %broadcast_in_dim.7.bias_hbm = f32[1,768]{1,0:T(1,128)} reshape(f32[768]{0:T(1024)} %param.13) | data formatting | bytes 6144 | tf_op jit(solution)/shard_map/broadcast_in_dim | solution.py:325
  1.7 1.6 %shard_map.100 = (bf16[32,16,256]{2,1,0:T(8,128)(2,1)S(1)}, bf16[256,768]{1,0:T(8,128)(2,1)S(1)}, bf16[256,256]{1,0:T(8,128)(2,1)S(1)}, bf16[512,256]{1,0:T(8,12...) custom-call(bf16[32,32,256]{2,1,0:T(8,128)(2,1)} %own_hbm, ...), custom_call_target="tpu_custom_call" | custom-call | bytes 3145728 | tf_op jit(solution)/shard_map/pallas_call | solution.py:300
  3.4 1.2 %fusion.1 = (bf16[32,1,256]{2,1,0:T(2,128)(2,1)S(1)}, bf16[32,1,256]{2,1,0:T(2,128)(2,1)S(1)}, bf16[32,1,256]{2,1,0:T(2,128)(2,1)S(1)}, bf16[32,1,256]{2,1,0:T(2,128)(2,1)S(1)}) fusion(bf16[32,32,256]{2,1,0:T(8,128)(2,1)} %own_hbm), kind=kLoop, calls=%fused_computation.11 | loop fusion | bytes 131072 | tf_op jit(solution)/shard_map/slice | solution.py:332
  4.6 0.0 collective-permute-done.other_ref
  4.6 0.1 fusion
  4.7 0.7 %collective-permute-start.1 = (bf16[64,256]{1,0:T(8,128)(2,1)S(1)}, bf16[64,256]{1,0:T(8,128)(2,1)S(1)}, u32[]{:S(2)}, u32[]{:S(2)}) collective-permute-start(bf16[64,256]{1,0:T(8,128)(2,1)S(1)} %pad_maximum_fusion), channel_id=1, source_target_pairs={{16,1},{1,16},{17,2},{2,17},{18,3},{3,18},{19,4},{4,19},{20,5},{5,... | collective-permute-start | bytes 98312 | tf_op jit(solution)/shard_map/ppermute | solution.py:339
  5.5 4.1 %shard_map.101 = (f32[2,64,8,768]{3,2,1,0:T(8,128)S(1)}, f32[64,8,256]{2,1,0:T(8,128)S(1)}) custom-call(bf16[32,16,256]{2,1,0:T(8,128)(2,1)S(1)} %get-tuple-element.16.own_ref, bf16[32,32,256]{2,1,0:T(8,128)(2,1)S(1)} %collective-permute-done.other_ref, bf16[64,256]{1,0:T(8,128)(2,1)S(1)} %pad_maximum_fusion.1.within_ref, ...), custom_call_target="tpu_custom_call" | custom-call | flops 1000000000 | bytes 12582912 | tf_op jit(solution)/shard_map/pallas_call | solution.py:341
  9.5 0.0 collective-permute-done.1.halo_ref
  9.5 1.5 %shard_map.102 = (bf16[32,16,256]{2,1,0:T(8,128)(2,1)S(1)}, bf16[32,16,256]{2,1,0:T(8,128)(2,1)S(1)}) custom-call(bf16[64,256]{1,0:T(8,128)(2,1)S(1)} %collective-permute-done.1.halo_ref, f32[2,64,8,768]{3,2,1,0:T(8,128)S(1)} %get-tuple-element.23.mixed_ref, f32[64,8,256]{2,1,0:T(8,128)S(1)} %get-tuple-element.24.inner_ref, ...), custom_call_target="tpu_custom_call" | custom-call | flops 300000000 | bytes 4194304 | tf_op jit(solution)/shard_map/pallas_call | solution.py:360
  11.1 0.0 copy-start
  11.1 0.7 %copy-done = bf16[32,16,256]{2,1,0:T(8,128)(2,1)} copy-done((bf16[32,16,256]{2,1,0:T(8,128)(2,1)}, bf16[32,16,256]{2,1,0:T(8,128)(2,1)S(1)}, u32[]{:S(2)}) %copy-start) | copy-done | bytes 262168
  11.8 3.9 %collective-permute-start.2 = (bf16[32,16,256]{2,1,0:T(8,128)(2,1)S(1)}, bf16[32,16,256]{2,1,0:T(8,128)(2,1)S(1)}, u32[]{:S(2)}, u32[]{:S(2)}) collective-permute-start(bf16[32,16,256]{2,1,0:T(8,128)(2,1)S(1)} %get-tuple-element.26), channel_id=1, source_target_pairs={{0,16},{16,0},{1,17},{17,1},{2,18},{18,2},{3,19},{19,3},{4,20},{20... | collective-permute-start | bytes 786440 | tf_op jit(solution)/shard_map/ppermute | solution.py:376
  15.6 1.7 %shard_map.103.full_in = bf16[32,32,256]{2,1,0:T(8,128)(2,1)} custom-call(bf16[32,16,256]{2,1,0:T(8,128)(2,1)} %copy-done), custom_call_target="tpu_custom_call" | custom-call | bytes 524288 | tf_op jit(solution)/shard_map/pallas_call | solution.py:378
  17.3 0.0 collective-permute-done.2.theirs_ref
  17.3 0.0 copy-start.1
  17.3 0.7 %copy-done.1 = bf16[32,16,256]{2,1,0:T(8,128)(2,1)} copy-done((bf16[32,16,256]{2,1,0:T(8,128)(2,1)}, bf16[32,16,256]{2,1,0:T(8,128)(2,1)S(1)}, u32[]{:S(2)}) %copy-start.1) | copy-done | bytes 262168
  18.0 1.7 %shard_map.104 = bf16[32,32,256]{2,1,0:T(8,128)(2,1)} custom-call(bf16[32,32,256]{2,1,0:T(8,128)(2,1)} %shard_map.103.full_in, bf16[32,16,256]{2,1,0:T(8,128)(2,1)} %copy-done.1), custom_call_target="tpu_custom_call", output_to_operand_aliasing={{}: (0, {})} | custom-call | bytes 524288 | tf_op jit(solution)/shard_map/pallas_call | solution.py:386
  (6 shorter events, 0.1 us)
Async XLA Ops:
  0.0 4.6 %collective-permute-start = (bf16[32,32,256]{2,1,0:T(8,128)(2,1)}, bf16[32,32,256]{2,1,0:T(8,128)(2,1)S(1)}, u32[]{:S(2)}, u32[]{:S(2)}) collective-permute-start(bf16[32,32,256]{2,1,0:T(8,128)(2,1)} %own_hbm), channel_id=1, source_target_pairs={{0,16},{16,0},{1,17},{17,1},{2,18},{18,2},{3,19},{19,3},{4,20},{20... | collective-permute-start | bytes 1572872 | tf_op jit(solution)/shard_map/ppermute | solution.py:295
  4.7 4.8 %collective-permute-start.1 = (bf16[64,256]{1,0:T(8,128)(2,1)S(1)}, bf16[64,256]{1,0:T(8,128)(2,1)S(1)}, u32[]{:S(2)}, u32[]{:S(2)}) collective-permute-start(bf16[64,256]{1,0:T(8,128)(2,1)S(1)} %pad_maximum_fusion), channel_id=1, source_target_pairs={{16,1},{1,16},{17,2},{2,17},{18,3},{3,18},{19,4},{4,19},{20,5},{5,... | collective-permute-start | bytes 98312 | tf_op jit(solution)/shard_map/ppermute | solution.py:339
  11.1 0.7 %copy-start = (bf16[32,16,256]{2,1,0:T(8,128)(2,1)}, bf16[32,16,256]{2,1,0:T(8,128)(2,1)S(1)}, u32[]{:S(2)}) copy-start(bf16[32,16,256]{2,1,0:T(8,128)(2,1)S(1)} %get-tuple-element.25.mine_ref) | copy-start | bytes 786436
  11.8 5.5 %collective-permute-start.2 = (bf16[32,16,256]{2,1,0:T(8,128)(2,1)S(1)}, bf16[32,16,256]{2,1,0:T(8,128)(2,1)S(1)}, u32[]{:S(2)}, u32[]{:S(2)}) collective-permute-start(bf16[32,16,256]{2,1,0:T(8,128)(2,1)S(1)} %get-tuple-element.26), channel_id=1, source_target_pairs={{0,16},{16,0},{1,17},{17,1},{2,18},{18,2},{3,19},{19,3},{4,20},{20... | collective-permute-start | bytes 786440 | tf_op jit(solution)/shard_map/ppermute | solution.py:376
  17.3 0.7 %copy-start.1 = (bf16[32,16,256]{2,1,0:T(8,128)(2,1)}, bf16[32,16,256]{2,1,0:T(8,128)(2,1)S(1)}, u32[]{:S(2)}) copy-start(bf16[32,16,256]{2,1,0:T(8,128)(2,1)S(1)} %collective-permute-done.2.theirs_ref) | copy-start | bytes 786436

commit v3 on v2

--- a/solution.py
+++ b/solution.py
@@ -51,10 +51,9 @@
     own_ref, w_in_ref, w_out_ref, fwd_ref, bwd_ref, taps_ref, h_ref,
     spec_ref, filt_ref, gain_ref, kernel_ref, bias_ref, sems,
 ):
-    rows, part, _ = own_ref.shape
-    start = pl.multiple_of(lax.axis_index("row") * part, part)
+    rows = own_ref.shape[0]
     moves = [
-        (own_hbm.at[:, pl.ds(start, part), :], own_ref),
+        (own_hbm, own_ref),
         (w_in_hbm, w_in_ref),
         (spec_hbm, spec_ref),
         (filt_hbm, filt_ref),
@@ -72,7 +71,7 @@
         copy.wait()
     for a in range(3):
         taps_ref[3 * a : 3 * a + 3, :] = kernel_ref[a].astype(F32)
-    taps_ref[9:10, :] = bias_ref[...]
+    taps_ref[9, :] = bias_ref[...]
     filt = filt_ref[...]
     h_ref[...] = jnp.dot(spec_ref[0], filt, preferred_element_type=F32) + jnp.dot(
         spec_ref[1], filt, preferred_element_type=F32
@@ -143,7 +142,8 @@
     p_ref, edge_ref, u_ref, prod_ref, z_ref,
 ):
     core = lax.axis_index("row")
-    rows, part, width = own_ref.shape
+    rows, cols, width = own_ref.shape
+    part = cols // 2
     height = 2 * rows
     start = pl.multiple_of(core * part, part)
     n_group = part // GROUP
@@ -151,7 +151,7 @@
     p_ref[0] = jnp.zeros(p_ref.shape[1:], F32)
     p_ref[height + 1] = jnp.zeros(p_ref.shape[1:], F32)
     for at, tokens in (
-        (core * rows, own_ref[...]),
+        (core * rows, own_ref[:, pl.ds(start, part), :]),
         ((1 - core) * rows, other_ref[:, pl.ds(start, part), :]),
     ):
         got = jnp.dot(
@@ -258,22 +258,6 @@
         ).astype(BF16)
 
 
-def store_kernel(mine_ref, full_hbm, sem):
-    _, part, _ = mine_ref.shape
-    start = pl.multiple_of(lax.axis_index("row") * part, part)
-    copy = pltpu.make_async_copy(mine_ref, full_hbm.at[:, pl.ds(start, part), :], sem)
-    copy.start()
-    copy.wait()
-
-
-def fill_kernel(full_in, theirs_ref, full_hbm, sem):
-    _, part, _ = theirs_ref.shape
-    start = pl.multiple_of((1 - lax.axis_index("row")) * part, part)
-    copy = pltpu.make_async_copy(theirs_ref, full_hbm.at[:, pl.ds(start, part), :], sem)
-    copy.start()
-    copy.wait()
-
-
 def on_device(image_tokens, w_in, conv_kernel, conv_bias, long_filter, skip_gain, w_out):
     rows, cols, width = image_tokens.shape
     part = cols // 2
@@ -297,10 +281,10 @@
     def keep(array):
         return pltpu.with_memory_space_constraint(array, pltpu.HBM)
 
-    own, w_in_v, w_out_v, fwd_v, bwd_v, taps, spectrum = pl.pallas_call(
+    block, w_in_v, w_out_v, fwd_v, bwd_v, taps, spectrum = pl.pallas_call(
         prep_kernel,
         out_shape=(
-            shape((rows, part, width), BF16),
+            shape(image_tokens.shape, BF16),
             shape(w_in.shape, BF16),
             shape(w_out.shape, BF16),
             shape(fwd.shape, BF16),
@@ -315,21 +299,23 @@
             pltpu.VMEM(long_filter.shape, BF16),
             pltpu.VMEM((1, width), F32),
             pltpu.VMEM(conv_kernel.shape, BF16),
-            pltpu.VMEM((1, 3 * width), F32),
+            pltpu.VMEM(conv_bias.shape, F32),
             pltpu.SemaphoreType.DMA((10,)),
         ],
         compiler_params=limit,
         cost_estimate=pl.CostEstimate(flops=0, bytes_accessed=3 * 1024 * 1024, transcendentals=0),
     )(
         keep(image_tokens), keep(w_in), keep(w_out), keep(fwd.astype(BF16)), keep(bwd.astype(BF16)),
-        keep(spec), keep(long_filter), keep(skip_gain[None]), keep(conv_kernel), keep(conv_bias[None]),
-    )
+        keep(spec), keep(long_filter), keep(skip_gain[None]), keep(conv_kernel), keep(conv_bias),
+    )
+
+    own = with_layout_constraint(block, rowmajor)
 
     def by_core(low, high):
         return jnp.where(core == 0, low, high)
 
     def column(low, high):
-        mine = by_core(image_tokens[:, low], image_tokens[:, high])
+        mine = by_core(own[:, low], own[:, high])
         theirs = by_core(other[:, low], other[:, high])
         return jnp.concatenate([by_core(mine, theirs), by_core(theirs, mine)], 0)
 
@@ -374,24 +360,7 @@
         cost_estimate=pl.CostEstimate(flops=3 * 10**8, bytes_accessed=4 * 1024 * 1024, transcendentals=0),
     )(halo, mixed, inner, w_in_v, taps, fwd_v, bwd_v, w_out_v, spectrum)
     theirs = lax.ppermute(send, "row", swap)
-    full_shape = shape((rows, cols, width), BF16)
-    full = pl.pallas_call(
-        store_kernel,
-        out_shape=full_shape,
-        in_specs=[vmem],
-        out_specs=hbm,
-        scratch_shapes=[pltpu.SemaphoreType.DMA],
-        cost_estimate=pl.CostEstimate(flops=0, bytes_accessed=512 * 1024, transcendentals=0),
-    )(mine)
-    return pl.pallas_call(
-        fill_kernel,
-        out_shape=full_shape,
-        in_specs=[hbm, vmem],
-        out_specs=hbm,
-        scratch_shapes=[pltpu.SemaphoreType.DMA],
-        input_output_aliases={0: 0},
-        cost_estimate=pl.CostEstimate(flops=0, bytes_accessed=512 * 1024, transcendentals=0),
-    )(full, theirs)
+    return by_core(jnp.concatenate([mine, theirs], 1), jnp.concatenate([theirs, mine], 1))
 
 
 def solution(mesh):

time: 20 us -> 15.3 us (0.77)
  local copies, waits for them, and re-layouts: 3.98 us -> 0.4 us
  Pallas kernels: 10.5 us -> 7.28 us
  waiting for transfers between devices: 0.01 us -> 1.17 us
  other arithmetic: 0.05 us -> 1.08 us
    pallas_call x3 -> x1, Pallas kernels: 4.95 us -> 1.71 us  [on_device(): pl.pallas_call(prep_kernel, out_shape=(shape(image_tokens.shape, BF16), s...]
    unnamed x4 -> x0, local copies, waits for them, and re-layouts: 1.4 us -> none
    broadcast_in_dim x1 -> x0, local copies, waits for them, and re-layouts: 1.27 us -> none  [on_device(): conv_bias[None]]
    slice x1 -> x0, local copies, waits for them, and re-layouts: 1.21 us -> none  [column(): mine = by_core(image_tokens[:, low], image_tokens[:, high])]
    ppermute x1, waiting for transfers between devices: 0.01 us -> 1.16 us  [on_device(): theirs = lax.ppermute(send, 'row', swap)]
    select_n x4 -> x3, other arithmetic: 0.05 us -> 1.07 us  [by_core(): return jnp.where(core == 0, low, high)]
    another operation x0 -> x1, local copies, waits for them, and re-layouts: none -> 0.29 us  [on_device(): own = with_layout_constraint(block, rowmajor)]
  transfers between devices with their start and end apart: 3 -> 3, of which waited for: 0 -> 1; matrix products, arithmetic and copies ran while one was open for 13% -> 2% of each run, Pallas kernels for 37% -> 38%
where the time goes in v3:
time: 15.3 us; the launch traced here: 15.1 us
  Pallas kernels  7.28 us (48%)
  starting transfers between devices  5.11 us (33%)
  waiting for transfers between devices  1.17 us (8%)
  other arithmetic  1.08 us (7%)
  local copies, waits for them, and re-layouts  0.4 us (3%)
    pallas_call x1, Pallas kernels, on_device(): pl.pallas_call(inner_kernel, out_shape=(shape((2, height, GROUP, 3 * widt...  4.06 us
    ppermute x1, starting transfers between devices, on_device(): theirs = lax.ppermute(send, 'row', swap)  3.99 us
    pallas_call x1, Pallas kernels, on_device(): pl.pallas_call(prep_kernel, out_shape=(shape(image_tokens.shape, BF16), s...  1.71 us
    pallas_call x1, Pallas kernels, on_device(): pl.pallas_call(edge_kernel, out_shape=(half_shape, half_shape), in_specs=...  1.52 us
    ppermute x1, waiting for transfers between devices, on_device(): theirs = lax.ppermute(send, 'row', swap)  1.16 us
    select_n x3, other arithmetic, by_core(): return jnp.where(core == 0, low, high)  1.07 us
    ppermute x1, starting transfers between devices, on_device(): halo = lax.ppermute(column(0, cols - 1), ('row', 'col'), pairs)  0.66 us
    ppermute x1, starting transfers between devices, on_device(): lax.ppermute(image_tokens, 'row', swap)  0.45 us
  transfers between devices with their start and end apart: 3, of which 1 were waited for; matrix products, arithmetic and copies ran while one was open for 2% of the time, Pallas kernels for 38%

profile of v3, /device:TPU:0, one launch (start us, length us, event | category | flops | bytes accessed | tf_op | source)
XLA Modules:
  0.0 15.1 jit_solution(17226932469826259290)
XLA Ops:
  0.0 0.5 %collective-permute-start = (bf16[32,32,256]{2,1,0:T(8,128)(2,1)}, bf16[32,32,256]{2,1,0:T(8,128)(2,1)S(1)}, u32[]{:S(2)}, u32[]{:S(2)}) collective-permute-start(bf16[32,32,256]{2,1,0:T(8,128)(2,1)} %own_hbm), channel_id=1, source_target_pairs={{0,16},{16,0},{1,17},{17,1},{2,18},{18,2},{3,19},{19,3},{4,20},{20... | collective-permute-start | bytes 1572872 | tf_op jit(solution)/shard_map/ppermute | solution.py:279
  0.5 1.7 %shard_map.100 = (bf16[32,32,256]{2,1,0:T(8,128)(2,1)S(1)}, bf16[256,768]{1,0:T(8,128)(2,1)S(1)}, bf16[256,256]{1,0:T(8,128)(2,1)S(1)}, bf16[512,256]{1,0:T(8,12...) custom-call(bf16[32,32,256]{2,1,0:T(8,128)(2,1)} %own_hbm, ...), custom_call_target="tpu_custom_call" | custom-call | bytes 3145728 | tf_op jit(solution)/shard_map/pallas_call | solution.py:284
  2.2 0.3 %copy.11 = bf16[32,32,256]{2,0,1:T(8,128)(2,1)S(1)} copy(bf16[32,32,256]{2,1,0:T(8,128)(2,1)S(1)} %get-tuple-element.16.own_ref) | data formatting | bytes 1048576 | tf_op jit(solution)/shard_map/layout_constraint | solution.py:312
  2.5 0.0 collective-permute-done.other_ref
  2.5 0.1 fusion
  2.7 0.7 %collective-permute-start.1 = (bf16[64,256]{1,0:T(8,128)(2,1)S(1)}, bf16[64,256]{1,0:T(8,128)(2,1)S(1)}, u32[]{:S(2)}, u32[]{:S(2)}) collective-permute-start(bf16[64,256]{1,0:T(8,128)(2,1)S(1)} %pad_maximum_fusion), channel_id=1, source_target_pairs={{16,1},{1,16},{17,2},{2,17},{18,3},{3,18},{19,4},{4,19},{20,5},{5,... | collective-permute-start | bytes 98312 | tf_op jit(solution)/shard_map/ppermute | solution.py:325
  3.3 4.1 %shard_map.101 = (f32[2,64,8,768]{3,2,1,0:T(8,128)S(1)}, f32[64,8,256]{2,1,0:T(8,128)S(1)}) custom-call(bf16[32,32,256]{2,1,0:T(8,128)(2,1)S(1)} %get-tuple-element.16.own_ref, bf16[32,32,256]{2,1,0:T(8,128)(2,1)S(1)} %collective-permute-done.other_ref, bf16[64,256]{1,0:T(8,128)(2,1)S(1)} %pad_maximum_fusion.1.within_ref, ...), custom_call_target="tpu_custom_call" | custom-call | flops 1000000000 | bytes 12582912 | tf_op jit(solution)/shard_map/pallas_call | solution.py:327
  7.4 0.0 collective-permute-done.1.halo_ref
  7.4 1.5 %shard_map.102 = (bf16[32,16,256]{2,1,0:T(8,128)(2,1)S(1)}, bf16[32,16,256]{2,1,0:T(8,128)(2,1)S(1)}) custom-call(bf16[64,256]{1,0:T(8,128)(2,1)S(1)} %collective-permute-done.1.halo_ref, f32[2,64,8,768]{3,2,1,0:T(8,128)S(1)} %get-tuple-element.23.mixed_ref, f32[64,8,256]{2,1,0:T(8,128)S(1)} %get-tuple-element.24.inner_ref, ...), custom_call_target="tpu_custom_call" | custom-call | flops 300000000 | bytes 4194304 | tf_op jit(solution)/shard_map/pallas_call | solution.py:346
  8.9 4.0 %collective-permute-start.2 = (bf16[32,16,256]{2,1,0:T(8,128)(2,1)S(1)}, bf16[32,16,256]{2,1,0:T(8,128)(2,1)S(1)}, u32[]{:S(2)}, u32[]{:S(2)}) collective-permute-start(bf16[32,16,256]{2,1,0:T(8,128)(2,1)S(1)} %get-tuple-element.26), channel_id=1, source_target_pairs={{0,16},{16,0},{1,17},{17,1},{2,18},{18,2},{3,19},{19,3},{4,20},{20... | collective-permute-start | bytes 786440 | tf_op jit(solution)/shard_map/ppermute | solution.py:362
  12.9 1.2 %collective-permute-done.2 = bf16[32,16,256]{2,1,0:T(8,128)(2,1)S(1)} collective-permute-done((bf16[32,16,256]{2,1,0:T(8,128)(2,1)S(1)}, bf16[32,16,256]{2,1,0:T(8,128)(2,1)S(1)}, u32[]{:S(2)}, u32[]{:S(2)}) %collective-permute-start.2) | collective-permute-done | bytes 262176 | tf_op jit(solution)/shard_map/ppermute | solution.py:362
  14.1 1.0 %maximum_select_fusion = bf16[32,32,256]{2,1,0:T(8,128)(2,1)} fusion(bf16[32,16,256]{2,1,0:T(8,128)(2,1)S(1)} %collective-permute-done.2, bf16[32,16,256]{2,1,0:T(8,128)(2,1)S(1)} %get-tuple-element.25, pred[]{:T(512)S(6)} %eq.2), kind=kLoop, calls=%fused_computation | loop fusion | flops 2359296 | bytes 1048577 | tf_op jit(solution)/shard_map/jit(_where)/select_n | solution.py:315
  (4 shorter events, 0.0 us)
Async XLA Ops:
  0.0 2.5 %collective-permute-start = (bf16[32,32,256]{2,1,0:T(8,128)(2,1)}, bf16[32,32,256]{2,1,0:T(8,128)(2,1)S(1)}, u32[]{:S(2)}, u32[]{:S(2)}) collective-permute-start(bf16[32,32,256]{2,1,0:T(8,128)(2,1)} %own_hbm), channel_id=1, source_target_pairs={{0,16},{16,0},{1,17},{17,1},{2,18},{18,2},{3,19},{19,3},{4,20},{20... | collective-permute-start | bytes 1572872 | tf_op jit(solution)/shard_map/ppermute | solution.py:279
  2.7 4.7 %collective-permute-start.1 = (bf16[64,256]{1,0:T(8,128)(2,1)S(1)}, bf16[64,256]{1,0:T(8,128)(2,1)S(1)}, u32[]{:S(2)}, u32[]{:S(2)}) collective-permute-start(bf16[64,256]{1,0:T(8,128)(2,1)S(1)} %pad_maximum_fusion), channel_id=1, source_target_pairs={{16,1},{1,16},{17,2},{2,17},{18,3},{3,18},{19,4},{4,19},{20,5},{5,... | collective-permute-start | bytes 98312 | tf_op jit(solution)/shard_map/ppermute | solution.py:325
  8.9 5.2 %collective-permute-start.2 = (bf16[32,16,256]{2,1,0:T(8,128)(2,1)S(1)}, bf16[32,16,256]{2,1,0:T(8,128)(2,1)S(1)}, u32[]{:S(2)}, u32[]{:S(2)}) collective-permute-start(bf16[32,16,256]{2,1,0:T(8,128)(2,1)S(1)} %get-tuple-element.26), channel_id=1, source_target_pairs={{0,16},{16,0},{1,17},{17,1},{2,18},{18,2},{3,19},{19,3},{4,20},{20... | collective-permute-start | bytes 786440 | tf_op jit(solution)/shard_map/ppermute | solution.py:362

commit v4 on v3

v4 whole, which is shorter than its diff:
```python
import jax
import jax.numpy as jnp
import numpy as np
from jax import lax
from jax.experimental import pallas as pl
from jax.experimental.layout import Layout, with_layout_constraint
from jax.experimental.pallas import tpu as pltpu
from jax.sharding import PartitionSpec as P

F32 = jnp.float32
BF16 = jnp.bfloat16


def transforms(half, group):
    size = 2 * half
    slot = np.arange(half)[:, None]
    pos = np.arange(half)[None, :]
    angle = 2 * np.pi * slot * pos / size
    real, imag = np.cos(angle), -np.sin(angle)
    imag[0] = (-1.0) ** np.arange(half)
    forward = np.concatenate([real, imag], 0)
    back_real = 2 * np.cos(angle.T) / size
    back_real[:, 0] = 1 / size
    back_imag = -2 * np.sin(angle.T) / size
    back_imag[:, 0] = (-1.0) ** np.arange(half) / size
    backward = np.concatenate([back_real, back_imag], 1)
    lag = np.arange(size)[None, :]
    angle = 2 * np.pi * slot * lag / size
    real, imag = np.cos(angle), -np.sin(angle)
    imag[0] = 0
    real2 = real.copy()
    real2[0] = (-1.0) ** np.arange(size)
    near = (lag < half).astype(np.float64)
    sign = (-1.0) ** slot
    sign2 = sign.copy()
    sign2[0] = 1
    spectra = np.concatenate(
        [real * near, imag * near, real2 * near, real * sign, imag * sign, real2 * sign2], 0
    )
    eye = np.eye(group)
    return np.kron(forward, eye), np.kron(backward, eye), spectra


LANES = 128
GROUP = 8
CHUNK = 8


def prep_kernel(
    own_hbm, w_in_hbm, w_out_hbm, fwd_hbm, bwd_hbm, spec_hbm, filt_hbm, gain_hbm, kernel_hbm, bias_hbm,
    own_ref, w_in_ref, w_out_ref, fwd_ref, bwd_ref, taps_ref, h_ref,
    spec_ref, filt_ref, gain_ref, kernel_ref, bias_ref, sems,
):
    rows = own_ref.shape[0]
    moves = [
        (own_hbm, own_ref),
        (w_in_hbm, w_in_ref),
        (spec_hbm, spec_ref),
        (filt_hbm, filt_ref),
        (gain_hbm, gain_ref),
        (kernel_hbm, kernel_ref),
        (bias_hbm, bias_ref),
        (fwd_hbm, fwd_ref),
        (bwd_hbm, bwd_ref),
        (w_out_hbm, w_out_ref),
    ]
    copies = [pltpu.make_async_copy(src, dst, sems.at[i]) for i, (src, dst) in enumerate(moves)]
    for copy in copies:
        copy.start()
    for copy in copies:
        copy.wait()
    for a in range(3):
        taps_ref[3 * a : 3 * a + 3, :] = kernel_ref[a].astype(F32)
    taps_ref[9, :] = bias_ref[...]
    filt = filt_ref[...]
    h_ref[...] = jnp.dot(spec_ref[0], filt, preferred_element_type=F32) + jnp.dot(
        spec_ref[1], filt, preferred_element_type=F32
    )
    gain = gain_ref[...]
    h_ref[0:rows, :] = h_ref[0:rows, :] + gain
    h_ref[2 * rows : 3 * rows, :] = h_ref[2 * rows : 3 * rows, :] + gain


def edge_terms(tokens, taps, w_in_ref, edge_ref):
    height = tokens.shape[0]
    edge_ref[0:8, :] = jnp.zeros((8, edge_ref.shape[1]), F32)
    edge_ref[8 + height : 16 + height, :] = jnp.zeros((8, edge_ref.shape[1]), F32)
    edge_ref[8 : 8 + height, :] = jnp.dot(tokens, w_in_ref[...], preferred_element_type=F32)
    total = edge_ref[7 : 7 + height, :] * taps[0]
    for a in (1, 2):
        total = total + edge_ref[7 + a : 7 + a + height, :] * taps[a]
    return total.reshape(height // 8, 8, edge_ref.shape[1])


def column_taps(taps_ref, core, on_core0):
    first, second = on_core0, 2 - on_core0
    return [
        jnp.where(
            core == 0,
            taps_ref[3 * a + first : 3 * a + first + 1, :],
            taps_ref[3 * a + second : 3 * a + second + 1, :],
        )
        for a in range(3)
    ]


def depthwise_steps(load, side_ref, taps_ref, chunk, store, bases):
    sub = lax.broadcasted_iota(jnp.int32, (GROUP, LANES), 0)
    is_first = sub == 0
    is_last = sub == GROUP - 1
    for base in bases:
        at = slice(base, base + LANES)
        tap = [
            [
                jnp.broadcast_to(taps_ref[3 * a + b : 3 * a + b + 1, at], (GROUP, LANES))
                for b in range(3)
            ]
            for a in range(3)
        ]
        bias = jnp.broadcast_to(taps_ref[9:10, at], (GROUP, LANES))
        loaded = [load(chunk * CHUNK + r, at) for r in range(CHUNK + 2)]
        for r in range(CHUNK):
            u = [
                loaded[r] * tap[0][b] + loaded[r + 1] * tap[1][b] + loaded[r + 2] * tap[2][b]
                for b in range(3)
            ]
            west = jnp.broadcast_to(side_ref[0, chunk, r : r + 1, at], (GROUP, LANES))
            east = jnp.broadcast_to(side_ref[1, chunk, r : r + 1, at], (GROUP, LANES))
            value = u[1] + bias
            value = value + jnp.where(is_first, west, pltpu.roll(u[0], 1, 0))
            value = value + jnp.where(is_last, east, pltpu.roll(u[2], GROUP - 1, 0))
            store(chunk * CHUNK + r, at, value)
        yield


def conv_steps(mixed, fwd_ref, bwd_ref, w_out_ref, h_ref, prod_ref, z_ref, put):
    height_group, width = prod_ref.shape
    height = height_group // GROUP
    rows = height // 2
    block = rows * GROUP
    spectra = []
    for h in range(2):
        for row in range(h * rows, (h + 1) * rows, 2):
            for base in range(0, width, LANES):
                two = [mixed(r, width + base) * mixed(r, 2 * width + base) for r in (row, row + 1)]
                prod_ref[row * GROUP : (row + 2) * GROUP, base : base + LANES] = jnp.concatenate(
                    two, 0
                ).astype(BF16)
            if row % 8 == 6:
                yield
        spectra.append(
            jnp.dot(
                fwd_ref[...], prod_ref[h * block : (h + 1) * block], preferred_element_type=F32
            )
        )
        yield
    low, high = spectra
    for k in range(0, rows, 2):
        parts = [[], [], [], []]
        for s in (k, k + 1):
            near_r, near_i, near_2, all_r, all_i, all_2 = (
                jnp.broadcast_to(h_ref[j * rows + s : j * rows + s + 1, :], (GROUP, width))
                for j in range(6)
            )
            re, im = slice(s * GROUP, (s + 1) * GROUP), slice(block + s * GROUP, block + (s + 1) * GROUP)
            lr, li, hr, hi = low[re], low[im], high[re], high[im]
            parts[0].append(lr * near_r - li * near_i)
            parts[1].append(lr * near_i + li * near_2)
            parts[2].append(lr * all_r - li * all_i + hr * near_r - hi * near_i)
            parts[3].append(lr * all_i + li * all_2 + hr * near_i + hi * near_2)
        for j in range(4):
            at = (j % 2) * block + k * GROUP
            z_ref[j // 2, at : at + 2 * GROUP, :] = jnp.concatenate(parts[j], 0).astype(BF16)
        if k % 4 == 2:
            yield
    convs = []
    for h in range(2):
        convs.append(jnp.dot(bwd_ref[...], z_ref[h], preferred_element_type=F32))
        yield
    for h in range(2):
        gated = []
        for r in range(rows):
            line = [
                mixed(h * rows + r, base) * convs[h][r * GROUP : (r + 1) * GROUP, base : base + LANES]
                for base in range(0, width, LANES)
            ]
            gated.append(jnp.concatenate(line, 1))
        final = jnp.dot(
            jnp.concatenate(gated, 0).astype(BF16), w_out_ref[...], preferred_element_type=F32
        )
        put(h, final.reshape(rows, GROUP, width))
        yield


def split_halves(out_ref, core, mine_ref, send_ref):
    mine_ref[...] = out_ref[core].astype(BF16)
    send_ref[...] = out_ref[1 - core].astype(BF16)


def inner_kernel(
    own_ref, other_ref, near_ref, far_ref, edge_near_ref,
    w_in_ref, taps_ref, fwd_ref, bwd_ref, w_out_ref, h_ref,
    edge_mixed_ref, mine_ref, send_ref,
    p_ref, strip_ref, side_ref, edge_side_ref, mixed_ref, prod_ref, z_ref, out_ref,
):
    core = lax.axis_index("row")
    rows, cols, width = own_ref.shape
    part = cols // 2
    height = 2 * rows
    start = pl.multiple_of(core * part, part)

    for slot in range(2):
        p_ref[slot, 0] = jnp.zeros((GROUP, 3 * width), F32)
        p_ref[slot, height + 1] = jnp.zeros((GROUP, 3 * width), F32)
    for row, ref in ((core * rows, own_ref), ((1 - core) * rows, other_ref)):
        tokens = ref[:, pl.ds(start, part), :].reshape(rows * part, width)
        got = jnp.dot(tokens, w_in_ref[...], preferred_element_type=F32)
        got = got.reshape(rows, part, 3 * width)
        p_ref[core, pl.ds(row + 1, rows)] = got[:, :GROUP]
        p_ref[1 - core, pl.ds(row + 1, rows)] = got[:, GROUP:]

    side_ref[core] = edge_terms(
        near_ref[...], column_taps(taps_ref, core, 0), w_in_ref, strip_ref.at[0]
    )
    side_ref[1 - core] = edge_terms(
        far_ref[...], column_taps(taps_ref, core, 2), w_in_ref, strip_ref.at[1]
    )
    edge_side_ref[1 - core] = edge_terms(
        edge_near_ref[...], column_taps(taps_ref, core, 2), w_in_ref, strip_ref.at[2]
    )
    edge_side_ref[core] = jnp.zeros(edge_side_ref.shape[1:], F32)

    def store_inner(row, at, value):
        mixed_ref[row, :, at] = value

    def inner_chunk(i, carry):
        steps = depthwise_steps(
            lambda row, at: p_ref[1, row, :, at], side_ref, taps_ref, i, store_inner,
            range(0, 3 * width, LANES),
        )
        for _ in steps:
            pass
        return carry

    lax.fori_loop(0, height // CHUNK, inner_chunk, 0)

    def store_edge(row, at, value):
        edge_mixed_ref[row, :, at] = value

    def put(h, final):
        out_ref[h] = final

    edge = [
        depthwise_steps(
            lambda row, at: p_ref[0, row, :, at], edge_side_ref, taps_ref, i, store_edge, [base]
        )
        for i in range(height // CHUNK)
        for base in range(0, 3 * width, LANES)
    ]
    conv = conv_steps(
        lambda r, base: mixed_ref[r, :, base : base + LANES],
        fwd_ref, bwd_ref, w_out_ref, h_ref, prod_ref, z_ref, put,
    )
    done = 0
    for _ in conv:
        for step in edge[done : done + 2]:
            for _ in step:
                pass
        done += 2
    for step in edge[done:]:
        for _ in step:
            pass
    split_halves(out_ref, core, mine_ref, send_ref)


def edge_kernel(
    halo_ref, mixed_ref, w_in_ref, taps_ref, fwd_ref, bwd_ref, w_out_ref, h_ref,
    mine_ref, send_ref,
    strip_ref, side_ref, prod_ref, z_ref, out_ref,
):
    core = lax.axis_index("row")
    side_ref[...] = edge_terms(
        halo_ref[...], column_taps(taps_ref, core, 0), w_in_ref, strip_ref
    )
    sub = lax.broadcasted_iota(jnp.int32, (GROUP, LANES), 0)
    at_edge = sub == core * (GROUP - 1)

    def mixed(r, base):
        at = slice(base, base + LANES)
        add = jnp.broadcast_to(side_ref[r // 8, r % 8 : r % 8 + 1, at], (GROUP, LANES))
        return mixed_ref[r, :, at] + jnp.where(at_edge, add, 0.0)

    def put(h, final):
        out_ref[h] = final

    for _ in conv_steps(
        mixed, fwd_ref, bwd_ref, w_out_ref, h_ref, prod_ref, z_ref, put
    ):
        pass
    split_halves(out_ref, core, mine_ref, send_ref)


def on_device(image_tokens, w_in, conv_kernel, conv_bias, long_filter, skip_gain, w_out):
    rows, cols, width = image_tokens.shape
    part = cols // 2
    height = 2 * rows
    n_col = lax.axis_size("col")
    core = lax.axis_index("row")
    fwd, bwd, spectra = transforms(rows, GROUP)
    spec_hi = spectra.astype(BF16)
    spec_lo = (spectra - spec_hi.astype(np.float64)).astype(BF16)
    spec = np.stack([spec_hi, spec_lo])
    vmem = pl.BlockSpec(memory_space=pltpu.VMEM)
    hbm = pl.BlockSpec(memory_space=pltpu.HBM)
    shape = jax.ShapeDtypeStruct
    limit = pltpu.CompilerParams(vmem_limit_bytes=24 * 1024 * 1024)

    swap = [(0, 1), (1, 0)]
    rowmajor = Layout((0, 1, 2))
    image_tokens = with_layout_constraint(image_tokens, rowmajor)
    other = with_layout_constraint(lax.ppermute(image_tokens, "row", swap), rowmajor)

    def keep(array):
        return pltpu.with_memory_space_constraint(array, pltpu.HBM)

    block, w_in_v, w_out_v, fwd_v, bwd_v, taps, spectrum = pl.pallas_call(
        prep_kernel,
        out_shape=(
            shape(image_tokens.shape, BF16),
            shape(w_in.shape, BF16),
            shape(w_out.shape, BF16),
            shape(fwd.shape, BF16),
            shape(bwd.shape, BF16),
            shape((16, 3 * width), F32),
            shape((6 * rows, width), F32),
        ),
        in_specs=[hbm] * 10,
        out_specs=(vmem,) * 7,
        scratch_shapes=[
            pltpu.VMEM(spec.shape, BF16),
            pltpu.VMEM(long_filter.shape, BF16),
            pltpu.VMEM((1, width), F32),
            pltpu.VMEM(conv_kernel.shape, BF16),
            pltpu.VMEM(conv_bias.shape, F32),
            pltpu.SemaphoreType.DMA((10,)),
        ],
        compiler_params=limit,
        cost_estimate=pl.CostEstimate(flops=0, bytes_accessed=3 * 1024 * 1024, transcendentals=0),
    )(
        keep(image_tokens), keep(w_in), keep(w_out), keep(fwd.astype(BF16)), keep(bwd.astype(BF16)),
        keep(spec), keep(long_filter), keep(skip_gain[None]), keep(conv_kernel), keep(conv_bias),
    )

    own = block

    def by_core(low, high):
        return jnp.where(core == 0, low, high)

    def column(low, high):
        mine = by_core(own[:, low], own[:, high])
        theirs = by_core(other[:, low], other[:, high])
        return jnp.concatenate([by_core(mine, theirs), by_core(theirs, mine)], 0)

    pairs = []
    for j in range(n_col - 1):
        pairs += [(n_col + j, j + 1), (j + 1, n_col + j)]
    halo = lax.ppermute(column(0, cols - 1), ("row", "col"), pairs)
    half_shape = shape((rows, GROUP, width), BF16)
    edge_mixed, mine_in, send_in = pl.pallas_call(
        inner_kernel,
        out_shape=(shape((height, GROUP, 3 * width), F32), half_shape, half_shape),
        in_specs=[vmem] * 11,
        out_specs=(vmem,) * 3,
        scratch_shapes=[
            pltpu.VMEM((2, height + 2, GROUP, 3 * width), F32),
            pltpu.VMEM((3, height + 16, 3 * width), F32),
            pltpu.VMEM((2, height // 8, 8, 3 * width), F32),
            pltpu.VMEM((2, height // 8, 8, 3 * width), F32),
            pltpu.VMEM((height, GROUP, 3 * width), F32),
            pltpu.VMEM((height * GROUP, width), BF16),
            pltpu.VMEM((2, 2 * rows * GROUP, width), BF16),
            pltpu.VMEM((2, rows, GROUP, width), F32),
        ],
        compiler_params=limit,
        cost_estimate=pl.CostEstimate(flops=10**9, bytes_accessed=12 * 1024 * 1024, transcendentals=0),
    )(
        block, other, column(GROUP - 1, cols - GROUP), column(part, part - 1),
        column(GROUP, cols - 1 - GROUP), w_in_v, taps, fwd_v, bwd_v, w_out_v, spectrum,
    )
    theirs_in = lax.ppermute(send_in, "row", swap)
    mine_edge, send_edge = pl.pallas_call(
        edge_kernel,
        out_shape=(half_shape, half_shape),
        in_specs=[vmem] * 8,
        out_specs=(vmem, vmem),
        scratch_shapes=[
            pltpu.VMEM((height + 16, 3 * width), F32),
            pltpu.VMEM((height // 8, 8, 3 * width), F32),
            pltpu.VMEM((height * GROUP, width), BF16),
            pltpu.VMEM((2, 2 * rows * GROUP, width), BF16),
            pltpu.VMEM((2, rows, GROUP, width), F32),
        ],
        compiler_params=limit,
        cost_estimate=pl.CostEstimate(flops=3 * 10**8, bytes_accessed=4 * 1024 * 1024, transcendentals=0),
    )(halo, edge_mixed, w_in_v, taps, fwd_v, bwd_v, w_out_v, spectrum)
    theirs_edge = lax.ppermute(send_edge, "row", swap)
    return by_core(
        jnp.concatenate([mine_edge, mine_in, theirs_in, theirs_edge], 1),
        jnp.concatenate([theirs_edge, theirs_in, mine_in, mine_edge], 1),
    )


def solution(mesh):
    in_specs = (P("row", "col", None), P(), P(), P(), P(), P(), P())
    out_specs = P("row", "col", None)
    return jax.shard_map(
        on_device, mesh=mesh, in_specs=in_specs, out_specs=out_specs, check_vma=False
    )
```

time: 15.3 us -> 15.4 us (level)
  Pallas kernels: 7.28 us -> 7.04 us
    another operation x1 -> x0, local copies, waits for them, and re-layouts: 0.29 us -> none  [on_device(): own = with_layout_constraint(block, rowmajor)]
    pallas_call x0 -> x1, local copies, waits for them, and re-layouts: none -> 0.29 us  [on_device(): pl.pallas_call(prep_kernel, out_shape=(shape(image_tokens.shape, BF16), s...]
    pallas_call x1, Pallas kernels: 1.52 us -> 1.23 us  [on_device(): pl.pallas_call(edge_kernel, out_shape=(half_shape, half_shape), in_specs=...]
    ppermute x1 -> x2, waiting for transfers between devices: 1.16 us -> 1.31 us  [the longest x1 1.31 us: on_device(): theirs_edge = lax.ppermute(send_edge, 'row', swap)]
    ppermute x1 -> x2, starting transfers between devices: 3.99 us -> 4.09 us  [the longest x1 4 us: on_device(): theirs_in = lax.ppermute(send_in, 'row', swap)]
    select_n x3 -> x4, other arithmetic: 1.07 us -> 1.11 us  [by_core(): return jnp.where(core == 0, low, high)]
  transfers between devices with their start and end apart: 3 -> 4, of which waited for: 1 -> 1; matrix products, arithmetic and copies ran while one was open for 2% -> 2% of each run, Pallas kernels for 38% -> 46%
where the time goes in v4:
time: 15.4 us; the launch traced here: 15.3 us
  Pallas kernels  7.04 us (46%)
  starting transfers between devices  5.21 us (34%)
  waiting for transfers between devices  1.32 us (9%)
  other arithmetic  1.12 us (7%)
  local copies, waits for them, and re-layouts  0.47 us (3%)
    pallas_call x1, Pallas kernels, on_device(): pl.pallas_call(inner_kernel, out_shape=(shape((height, GROUP, 3 * width),...  4.11 us
    ppermute x1, starting transfers between devices, on_device(): theirs_in = lax.ppermute(send_in, 'row', swap)  4 us
    pallas_call x1, Pallas kernels, on_device(): pl.pallas_call(prep_kernel, out_shape=(shape(image_tokens.shape, BF16), s...  1.71 us
    ppermute x1, waiting for transfers between devices, on_device(): theirs_edge = lax.ppermute(send_edge, 'row', swap)  1.31 us
    pallas_call x1, Pallas kernels, on_device(): pl.pallas_call(edge_kernel, out_shape=(half_shape, half_shape), in_specs=...  1.23 us
    select_n x4, other arithmetic, by_core(): return jnp.where(core == 0, low, high)  1.11 us
    ppermute x1, starting transfers between devices, on_device(): halo = lax.ppermute(column(0, cols - 1), ('row', 'col'), pairs)  0.66 us
    ppermute x1, starting transfers between devices, on_device(): lax.ppermute(image_tokens, 'row', swap)  0.45 us
  transfers between devices with their start and end apart: 4, of which 1 were waited for; matrix products, arithmetic and copies ran while one was open for 2% of the time, Pallas kernels for 46%

profile of v4, /device:TPU:0, one launch (start us, length us, event | category | flops | bytes accessed | tf_op | source)
XLA Modules:
  0.0 15.3 jit_solution(17463665511775423324)
XLA Ops:
  0.0 0.5 %collective-permute-start = (bf16[32,32,256]{2,1,0:T(8,128)(2,1)}, bf16[32,32,256]{2,1,0:T(8,128)(2,1)S(1)}, u32[]{:S(2)}, u32[]{:S(2)}) collective-permute-start(bf16[32,32,256]{2,1,0:T(8,128)(2,1)} %own_hbm), channel_id=1, source_target_pairs={{0,16},{16,0},{1,17},{17,1},{2,18},{18,2},{3,19},{19,3},{4,20},{20... | collective-permute-start | bytes 1572872 | tf_op jit(solution)/shard_map/ppermute | solution.py:321
  0.5 1.7 %shard_map.100 = (bf16[32,32,256]{2,1,0:T(8,128)(2,1)S(1)}, bf16[256,768]{1,0:T(8,128)(2,1)S(1)}, bf16[256,256]{1,0:T(8,128)(2,1)S(1)}, bf16[512,256]{1,0:T(8,12...) custom-call(bf16[32,32,256]{2,1,0:T(8,128)(2,1)} %own_hbm, ...), custom_call_target="tpu_custom_call" | custom-call | bytes 3145728 | tf_op jit(solution)/shard_map/pallas_call | solution.py:326
  2.2 0.3 %copy.11 = bf16[32,32,256]{2,0,1:T(8,128)(2,1)S(1)} copy(bf16[32,32,256]{2,1,0:T(8,128)(2,1)S(1)} %get-tuple-element.17.own_ref) | data formatting | bytes 1048576 | tf_op jit(solution)/shard_map/pallas_call | solution.py:326
  2.5 0.0 collective-permute-done.other_ref
  2.5 0.2 %fusion = (bf16[32,1,256]{2,1,0:T(2,128)(2,1)S(1)}, bf16[32,1,256]{2,1,0:T(2,128)(2,1)S(1)}, bf16[32,1,256]{2,1,0:T(2,128)(2,1)S(1)}, bf16[32,1,256]{2,1,0:T(2,1...) fusion(bf16[32,32,256]{2,1,0:T(8,128)(2,1)S(1)} %collective-per, ...), kind=kLoop, calls=%fused_computation.21 | loop fusion | bytes 262144 | tf_op jit(solution)/shard_map/slice | solution.py:361
  2.8 0.7 %collective-permute-start.1 = (bf16[64,256]{1,0:T(8,128)(2,1)S(1)}, bf16[64,256]{1,0:T(8,128)(2,1)S(1)}, u32[]{:S(2)}, u32[]{:S(2)}) collective-permute-start(bf16[64,256]{1,0:T(8,128)(2,1)S(1)} %get-tuple-element.53), channel_id=1, source_target_pairs={{16,1},{1,16},{17,2},{2,17},{18,3},{3,18},{19,4},{4,19},{20,5},{5,... | collective-permute-start | bytes 98312 | tf_op jit(solution)/shard_map/ppermute | solution.py:367
  3.5 4.1 %shard_map.101 = (f32[64,8,768]{2,1,0:T(8,128)S(1)}, bf16[32,8,256]{2,1,0:T(8,128)(2,1)S(1)}, bf16[32,8,256]{2,1,0:T(8,128)(2,1)S(1)}) custom-call(bf16[32,32,256]{2,1,0:T(8,128)(2,1)S(1)} %get-tuple-element.17.own_ref, bf16[32,32,256]{2,1,0:T(8,128)(2,1)S(1)} %collective-permute-done.other_ref, bf16[64,256]{1,0:T(8,128)(2,1)S(1)} %pad_maximum_fusion.1.near_ref, ...), custom_call_target="tpu_custom_call" | custom-call | flops 1000000000 | bytes 12582912 | tf_op jit(solution)/shard_map/pallas_call | solution.py:369
  7.6 4.0 %collective-permute-start.2 = (bf16[32,8,256]{2,1,0:T(8,128)(2,1)S(1)}, bf16[32,8,256]{2,1,0:T(8,128)(2,1)S(1)}, u32[]{:S(2)}, u32[]{:S(2)}) collective-permute-start(bf16[32,8,256]{2,1,0:T(8,128)(2,1)S(1)} %get-tuple-element.27), channel_id=1, source_target_pairs={{0,16},{16,0},{1,17},{17,1},{2,18},{18,2},{3,19},{19,3},{4,20},{20... | collective-permute-start | bytes 393224 | tf_op jit(solution)/shard_map/ppermute | solution.py:390
  11.6 0.0 collective-permute-done.1.halo_ref
  11.6 1.2 %shard_map.102 = (bf16[32,8,256]{2,1,0:T(8,128)(2,1)S(1)}, bf16[32,8,256]{2,1,0:T(8,128)(2,1)S(1)}) custom-call(bf16[64,256]{1,0:T(8,128)(2,1)S(1)} %collective-permute-done.1.halo_ref, f32[64,8,768]{2,1,0:T(8,128)S(1)} %get-tuple-element.24.mixed_ref, bf16[256,768]{1,0:T(8,128)(2,1)S(1)} %get-tuple-element.18.w_in_ref, ...), custom_call_target="tpu_custom_call" | custom-call | flops 300000000 | bytes 4194304 | tf_op jit(solution)/shard_map/pallas_call | solution.py:391
  12.8 0.1 collective-permute-start.3
  12.9 0.0 collective-permute-done.2
  12.9 1.3 %collective-permute-done.3 = bf16[32,8,256]{2,1,0:T(8,128)(2,1)S(1)} collective-permute-done((bf16[32,8,256]{2,1,0:T(8,128)(2,1)S(1)}, bf16[32,8,256]{2,1,0:T(8,128)(2,1)S(1)}, u32[]{:S(2)}, u32[]{:S(2)}) %collective-permute-start.3) | collective-permute-done | bytes 131104 | tf_op jit(solution)/shard_map/ppermute | solution.py:406
  14.2 1.0 %maximum_select_fusion = bf16[32,32,256]{2,1,0:T(8,128)(2,1)} fusion(bf16[32,8,256]{2,1,0:T(8,128)(2,1)S(1)} %collective-permute-done.3, bf16[32,8,256]{2,1,0:T(8,128)(2,1)S(1)} %collective-permute-done.2, bf16[32,8,256]{2,1,0:T(8,128)(2,1)S(1)} %get-tuple-element.26, bf16[32,8,256]{2,1,0:T(8,128)(2,1)S(1)} %get-tuple-element.25, pred[]{:T(512)S(6)} %eq.2), kind=kLoop, calls=%fused_computation | loop fusion | flops 4456448 | bytes 1048577 | tf_op jit(solution)/shard_map/jit(_where)/select_n | solution.py:357
  (6 shorter events, 0.1 us)
Async XLA Ops:
  0.0 2.5 %collective-permute-start = (bf16[32,32,256]{2,1,0:T(8,128)(2,1)}, bf16[32,32,256]{2,1,0:T(8,128)(2,1)S(1)}, u32[]{:S(2)}, u32[]{:S(2)}) collective-permute-start(bf16[32,32,256]{2,1,0:T(8,128)(2,1)} %own_hbm), channel_id=1, source_target_pairs={{0,16},{16,0},{1,17},{17,1},{2,18},{18,2},{3,19},{19,3},{4,20},{20... | collective-permute-start | bytes 1572872 | tf_op jit(solution)/shard_map/ppermute | solution.py:321
  2.8 8.8 %collective-permute-start.1 = (bf16[64,256]{1,0:T(8,128)(2,1)S(1)}, bf16[64,256]{1,0:T(8,128)(2,1)S(1)}, u32[]{:S(2)}, u32[]{:S(2)}) collective-permute-start(bf16[64,256]{1,0:T(8,128)(2,1)S(1)} %get-tuple-element.53), channel_id=1, source_target_pairs={{16,1},{1,16},{17,2},{2,17},{18,3},{3,18},{19,4},{4,19},{20,5},{5,... | collective-permute-start | bytes 98312 | tf_op jit(solution)/shard_map/ppermute | solution.py:367
  7.6 5.3 %collective-permute-start.2 = (bf16[32,8,256]{2,1,0:T(8,128)(2,1)S(1)}, bf16[32,8,256]{2,1,0:T(8,128)(2,1)S(1)}, u32[]{:S(2)}, u32[]{:S(2)}) collective-permute-start(bf16[32,8,256]{2,1,0:T(8,128)(2,1)S(1)} %get-tuple-element.27), channel_id=1, source_target_pairs={{0,16},{16,0},{1,17},{17,1},{2,18},{18,2},{3,19},{19,3},{4,20},{20... | collective-permute-start | bytes 393224 | tf_op jit(solution)/shard_map/ppermute | solution.py:390
  12.8 1.4 %collective-permute-start.3 = (bf16[32,8,256]{2,1,0:T(8,128)(2,1)S(1)}, bf16[32,8,256]{2,1,0:T(8,128)(2,1)S(1)}, u32[]{:S(2)}, u32[]{:S(2)}) collective-permute-start(bf16[32,8,256]{2,1,0:T(8,128)(2,1)S(1)} %get-tuple-element.28), channel_id=1, source_target_pairs={{0,16},{16,0},{1,17},{17,1},{2,18},{18,2},{3,19},{19,3},{4,20},{20... | collective-permute-start | bytes 393224 | tf_op jit(solution)/shard_map/ppermute | solution.py:406

commit v5 on v4

--- a/solution.py
+++ b/solution.py
@@ -46,20 +46,33 @@
 CHUNK = 8
 
 
+def pick_columns(block, columns):
+    rows, cols, width = block.shape
+    shape = (rows, rows * cols)
+    place = lax.broadcasted_iota(jnp.int32, shape, 1)
+    row = lax.broadcasted_iota(jnp.int32, shape, 0) * cols
+    chosen = [jnp.where(place == row + column, 1.0, 0.0).astype(BF16) for column in columns]
+    return jnp.dot(
+        jnp.concatenate(chosen, 0), block.reshape(rows * cols, width), preferred_element_type=F32
+    ).astype(BF16)
+
+
 def prep_kernel(
     own_hbm, w_in_hbm, w_out_hbm, fwd_hbm, bwd_hbm, spec_hbm, filt_hbm, gain_hbm, kernel_hbm, bias_hbm,
-    own_ref, w_in_ref, w_out_ref, fwd_ref, bwd_ref, taps_ref, h_ref,
+    own_ref, w_in_ref, w_out_ref, fwd_ref, bwd_ref, taps_ref, h_ref, outer_ref, strips_ref,
     spec_ref, filt_ref, gain_ref, kernel_ref, bias_ref, sems,
 ):
-    rows = own_ref.shape[0]
+    core = lax.axis_index("row")
+    rows, cols, _ = own_ref.shape
+    part = cols // 2
     moves = [
-        (own_hbm, own_ref),
-        (w_in_hbm, w_in_ref),
         (spec_hbm, spec_ref),
         (filt_hbm, filt_ref),
         (gain_hbm, gain_ref),
+        (own_hbm, own_ref),
         (kernel_hbm, kernel_ref),
         (bias_hbm, bias_ref),
+        (w_in_hbm, w_in_ref),
         (fwd_hbm, fwd_ref),
         (bwd_hbm, bwd_ref),
         (w_out_hbm, w_out_ref),
@@ -67,29 +80,45 @@
     copies = [pltpu.make_async_copy(src, dst, sems.at[i]) for i, (src, dst) in enumerate(moves)]
     for copy in copies:
         copy.start()
-    for copy in copies:
+    for copy in copies[:3]:
+        copy.wait()
+    filt = filt_ref[...]
+    h_ref[...] = jnp.dot(spec_ref[0], filt, preferred_element_type=F32) + jnp.dot(
+        spec_ref[1], filt, preferred_element_type=F32
+    )
+    gain = gain_ref[...]
+    h_ref[0:rows, :] = h_ref[0:rows, :] + gain
+    h_ref[2 * rows : 3 * rows, :] = h_ref[2 * rows : 3 * rows, :] + gain
+    copies[3].wait()
+    start = pl.multiple_of(core * part, part)
+    mine = pick_columns(
+        own_ref[:, pl.ds(start, part), :],
+        [core * (part - 1), GROUP - 1 + core, GROUP - core],
+    )
+    outer_ref[...] = mine[:rows]
+    strips_ref[: 2 * rows] = mine[rows:]
+    start = pl.multiple_of((1 - core) * part, part)
+    strips_ref[2 * rows :] = pick_columns(
+        own_ref[:, pl.ds(start, part), :], [core * (part - 1)]
+    )
+    for copy in copies[4:]:
         copy.wait()
     for a in range(3):
         taps_ref[3 * a : 3 * a + 3, :] = kernel_ref[a].astype(F32)
     taps_ref[9, :] = bias_ref[...]
-    filt = filt_ref[...]
-    h_ref[...] = jnp.dot(spec_ref[0], filt, preferred_element_type=F32) + jnp.dot(
-        spec_ref[1], filt, preferred_element_type=F32
-    )
-    gain = gain_ref[...]
-    h_ref[0:rows, :] = h_ref[0:rows, :] + gain
-    h_ref[2 * rows : 3 * rows, :] = h_ref[2 * rows : 3 * rows, :] + gain
-
-
-def edge_terms(tokens, taps, w_in_ref, edge_ref):
-    height = tokens.shape[0]
-    edge_ref[0:8, :] = jnp.zeros((8, edge_ref.shape[1]), F32)
-    edge_ref[8 + height : 16 + height, :] = jnp.zeros((8, edge_ref.shape[1]), F32)
-    edge_ref[8 : 8 + height, :] = jnp.dot(tokens, w_in_ref[...], preferred_element_type=F32)
+
+
+def edge_terms(first, second, core, taps, edge_ref):
+    rows, channels = first.shape
+    height = 2 * rows
+    edge_ref[0:8, :] = jnp.zeros((8, channels), F32)
+    edge_ref[8 + height : 16 + height, :] = jnp.zeros((8, channels), F32)
+    edge_ref[pl.ds(pl.multiple_of(8 + core * rows, 8), rows), :] = first
+    edge_ref[pl.ds(pl.multiple_of(8 + (1 - core) * rows, 8), rows), :] = second
     total = edge_ref[7 : 7 + height, :] * taps[0]
     for a in (1, 2):
         total = total + edge_ref[7 + a : 7 + a + height, :] * taps[a]
-    return total.reshape(height // 8, 8, edge_ref.shape[1])
+    return total.reshape(height // 8, 8, channels)
 
 
 def column_taps(taps_ref, core, on_core0):
@@ -192,16 +221,11 @@
         yield
 
 
-def split_halves(out_ref, core, mine_ref, send_ref):
-    mine_ref[...] = out_ref[core].astype(BF16)
-    send_ref[...] = out_ref[1 - core].astype(BF16)
-
-
 def inner_kernel(
-    own_ref, other_ref, near_ref, far_ref, edge_near_ref,
+    own_ref, other_ref, strips_ref, other_strips_ref,
     w_in_ref, taps_ref, fwd_ref, bwd_ref, w_out_ref, h_ref,
-    edge_mixed_ref, mine_ref, send_ref,
-    p_ref, strip_ref, side_ref, edge_side_ref, mixed_ref, prod_ref, z_ref, out_ref,
+    edge_mixed_ref, out_ref,
+    p_ref, strip_ref, side_ref, edge_side_ref, mixed_ref, prod_ref, z_ref,
 ):
     core = lax.axis_index("row")
     rows, cols, width = own_ref.shape
@@ -212,21 +236,28 @@
     for slot in range(2):
         p_ref[slot, 0] = jnp.zeros((GROUP, 3 * width), F32)
         p_ref[slot, height + 1] = jnp.zeros((GROUP, 3 * width), F32)
-    for row, ref in ((core * rows, own_ref), ((1 - core) * rows, other_ref)):
-        tokens = ref[:, pl.ds(start, part), :].reshape(rows * part, width)
-        got = jnp.dot(tokens, w_in_ref[...], preferred_element_type=F32)
-        got = got.reshape(rows, part, 3 * width)
-        p_ref[core, pl.ds(row + 1, rows)] = got[:, :GROUP]
-        p_ref[1 - core, pl.ds(row + 1, rows)] = got[:, GROUP:]
-
-    side_ref[core] = edge_terms(
-        near_ref[...], column_taps(taps_ref, core, 0), w_in_ref, strip_ref.at[0]
-    )
-    side_ref[1 - core] = edge_terms(
-        far_ref[...], column_taps(taps_ref, core, 2), w_in_ref, strip_ref.at[1]
-    )
+    strips = []
+    for row, ref, strip in (
+        (core * rows, own_ref, strips_ref),
+        ((1 - core) * rows, other_ref, other_strips_ref),
+    ):
+        count = rows * part
+        tokens = ref[:, pl.ds(start, part), :].reshape(count, width)
+        got = jnp.dot(
+            jnp.concatenate([tokens, strip[...]], 0), w_in_ref[...], preferred_element_type=F32
+        )
+        grid = got[:count].reshape(rows, part, 3 * width)
+        p_ref[core, pl.ds(row + 1, rows)] = grid[:, :GROUP]
+        p_ref[1 - core, pl.ds(row + 1, rows)] = grid[:, GROUP:]
+        strips.append(
+            [got[count + j * rows : count + (j + 1) * rows] for j in range(3)]
+        )
+
+    near, edge_near, far = zip(*strips)
+    side_ref[core] = edge_terms(*near, core, column_taps(taps_ref, core, 0), strip_ref.at[0])
+    side_ref[1 - core] = edge_terms(*far, core, column_taps(taps_ref, core, 2), strip_ref.at[1])
     edge_side_ref[1 - core] = edge_terms(
-        edge_near_ref[...], column_taps(taps_ref, core, 2), w_in_ref, strip_ref.at[2]
+        *edge_near, core, column_taps(taps_ref, core, 2), strip_ref.at[2]
     )
     edge_side_ref[core] = jnp.zeros(edge_side_ref.shape[1:], F32)
 
@@ -270,17 +301,18 @@
     for step in edge[done:]:
         for _ in step:
             pass
-    split_halves(out_ref, core, mine_ref, send_ref)
 
 
 def edge_kernel(
-    halo_ref, mixed_ref, w_in_ref, taps_ref, fwd_ref, bwd_ref, w_out_ref, h_ref,
+    halo_ref, mixed_ref, inner_ref, w_in_ref, taps_ref, fwd_ref, bwd_ref, w_out_ref, h_ref,
     mine_ref, send_ref,
     strip_ref, side_ref, prod_ref, z_ref, out_ref,
 ):
     core = lax.axis_index("row")
+    rows, part, width = mine_ref.shape
+    got = jnp.dot(halo_ref[...], w_in_ref[...], preferred_element_type=F32)
     side_ref[...] = edge_terms(
-        halo_ref[...], column_taps(taps_ref, core, 0), w_in_ref, strip_ref
+        got[:rows], got[rows:], 1 - core, column_taps(taps_ref, core, 0), strip_ref
     )
     sub = lax.broadcasted_iota(jnp.int32, (GROUP, LANES), 0)
     at_edge = sub == core * (GROUP - 1)
@@ -297,7 +329,10 @@
         mixed, fwd_ref, bwd_ref, w_out_ref, h_ref, prod_ref, z_ref, put
     ):
         pass
-    split_halves(out_ref, core, mine_ref, send_ref)
+    for ref, half in ((mine_ref, core), (send_ref, 1 - core)):
+        pair = [out_ref[half], inner_ref[half]]
+        ref[:, :GROUP] = jnp.where(core == 0, pair[0], pair[1]).astype(BF16)
+        ref[:, GROUP:] = jnp.where(core == 0, pair[1], pair[0]).astype(BF16)
 
 
 def on_device(image_tokens, w_in, conv_kernel, conv_bias, long_filter, skip_gain, w_out):
@@ -323,7 +358,7 @@
     def keep(array):
         return pltpu.with_memory_space_constraint(array, pltpu.HBM)
 
-    block, w_in_v, w_out_v, fwd_v, bwd_v, taps, spectrum = pl.pallas_call(
+    own, w_in_v, w_out_v, fwd_v, bwd_v, taps, spectrum, outer, strips = pl.pallas_call(
         prep_kernel,
         out_shape=(
             shape(image_tokens.shape, BF16),
@@ -333,9 +368,11 @@
             shape(bwd.shape, BF16),
             shape((16, 3 * width), F32),
             shape((6 * rows, width), F32),
+            shape((rows, width), BF16),
+            shape((3 * rows, width), BF16),
         ),
         in_specs=[hbm] * 10,
-        out_specs=(vmem,) * 7,
+        out_specs=(vmem,) * 9,
         scratch_shapes=[
             pltpu.VMEM(spec.shape, BF16),
             pltpu.VMEM(long_filter.shape, BF16),
@@ -351,26 +388,25 @@
         keep(spec), keep(long_filter), keep(skip_gain[None]), keep(conv_kernel), keep(conv_bias),
     )
 
-    own = block
-
     def by_core(low, high):
         return jnp.where(core == 0, low, high)
 
-    def column(low, high):
-        mine = by_core(own[:, low], own[:, high])
-        theirs = by_core(other[:, low], other[:, high])
-        return jnp.concatenate([by_core(mine, theirs), by_core(theirs, mine)], 0)
+    def column(low):
+        return by_core(other[:, low], other[:, cols - 1 - low])
 
     pairs = []
     for j in range(n_col - 1):
         pairs += [(n_col + j, j + 1), (j + 1, n_col + j)]
-    halo = lax.ppermute(column(0, cols - 1), ("row", "col"), pairs)
-    half_shape = shape((rows, GROUP, width), BF16)
-    edge_mixed, mine_in, send_in = pl.pallas_call(
+    halo = lax.ppermute(jnp.concatenate([outer, column(0)], 0), ("row", "col"), pairs)
+    other_strips = jnp.concatenate([column(GROUP - 1), column(GROUP), column(part)], 0)
+    edge_mixed, inner = pl.pallas_call(
         inner_kernel,
-        out_shape=(shape((height, GROUP, 3 * width), F32), half_shape, half_shape),
-        in_specs=[vmem] * 11,
-        out_specs=(vmem,) * 3,
+        out_shape=(
+            shape((height, GROUP, 3 * width), F32),
+            shape((2, rows, GROUP, width), F32),
+        ),
+        in_specs=[vmem] * 10,
+        out_specs=(vmem,) * 2,
         scratch_shapes=[
             pltpu.VMEM((2, height + 2, GROUP, 3 * width), F32),
             pltpu.VMEM((3, height + 16, 3 * width), F32),
@@ -379,19 +415,15 @@
             pltpu.VMEM((height, GROUP, 3 * width), F32),
             pltpu.VMEM((height * GROUP, width), BF16),
             pltpu.VMEM((2, 2 * rows * GROUP, width), BF16),
-            pltpu.VMEM((2, rows, GROUP, width), F32),
         ],
         compiler_params=limit,
         cost_estimate=pl.CostEstimate(flops=10**9, bytes_accessed=12 * 1024 * 1024, transcendentals=0),
-    )(
-        block, other, column(GROUP - 1, cols - GROUP), column(part, part - 1),
-        column(GROUP, cols - 1 - GROUP), w_in_v, taps, fwd_v, bwd_v, w_out_v, spectrum,
-    )
-    theirs_in = lax.ppermute(send_in, "row", swap)
-    mine_edge, send_edge = pl.pallas_call(
+    )(own, other, strips, other_strips, w_in_v, taps, fwd_v, bwd_v, w_out_v, spectrum)
+    half_shape = shape((rows, part, width), BF16)
+    mine, send = pl.pallas_call(
         edge_kernel,
         out_shape=(half_shape, half_shape),
-        in_specs=[vmem] * 8,
+        in_specs=[vmem] * 9,
         out_specs=(vmem, vmem),
         scratch_shapes=[
             pltpu.VMEM((height + 16, 3 * width), F32),
@@ -402,12 +434,10 @@
         ],
         compiler_params=limit,
         cost_estimate=pl.CostEstimate(flops=3 * 10**8, bytes_accessed=4 * 1024 * 1024, transcendentals=0),
-    )(halo, edge_mixed, w_in_v, taps, fwd_v, bwd_v, w_out_v, spectrum)
-    theirs_edge = lax.ppermute(send_edge, "row", swap)
-    return by_core(
-        jnp.concatenate([mine_edge, mine_in, theirs_in, theirs_edge], 1),
-        jnp.concatenate([theirs_edge, theirs_in, mine_in, mine_edge], 1),
-    )
+    )(halo, edge_mixed, inner, w_in_v, taps, fwd_v, bwd_v, w_out_v, spectrum)
+    theirs = lax.ppermute(send, "row", swap)
+    both = jnp.concatenate([mine, mine], 1)
+    return lax.dynamic_update_slice_in_dim(both, theirs, (1 - core) * part, 1)
 
 
 def solution(mesh):

time: 15.4 us -> 14.8 us (0.961)
  waiting for transfers between devices: 1.32 us -> 0.52 us
  local copies, waits for them, and re-layouts: 0.47 us -> 0.89 us
  other arithmetic: 1.12 us -> 0.88 us
  starting transfers between devices: 5.21 us -> 5.4 us
    select_n x4 -> x3, other arithmetic: 1.11 us -> 0.03 us  [by_core(): return jnp.where(core == 0, low, high)]
    ppermute x3 -> x2, waiting for transfers between devices: 1.32 us -> 0.33 us  [the longest x1 0.33 us: on_device(): theirs = lax.ppermute(send, 'row', swap)]
    concatenate x3, other arithmetic: 0.02 us -> 0.84 us  [the longest x1 0.83 us: on_device(): both = jnp.concatenate([mine, mine], 1)]
    dynamic_update_slice x0 -> x1, local copies, waits for them, and re-layouts: none -> 0.72 us  [on_device(): return lax.dynamic_update_slice_in_dim(both, theirs, (1 - core) * part, 1)]
    pallas_call x1 -> x0, local copies, waits for them, and re-layouts: 0.29 us -> none  [on_device(): pl.pallas_call(prep_kernel, out_shape=(shape(image_tokens.shape, BF16), s...]
    ppermute x3 -> x2, starting transfers between devices: 4.76 us -> 4.95 us  [the longest x1 4.28 us: on_device(): theirs = lax.ppermute(send, 'row', swap)]
    ppermute x1, waiting for transfers between devices: 0.01 us -> 0.19 us  [on_device(): lax.ppermute(image_tokens, 'row', swap)]
    pallas_call x1, Pallas kernels: 1.71 us -> 1.55 us  [on_device(): pl.pallas_call(prep_kernel, out_shape=(shape(image_tokens.shape, BF16), s...]
  transfers between devices with their start and end apart: 4 -> 3, of which waited for: 1 -> 2; matrix products, arithmetic and copies ran while one was open for 2% -> 6% of each run, Pallas kernels for 46% -> 38%
where the time goes in v5:
time: 14.8 us; the launch traced here: 14.7 us
  Pallas kernels  6.91 us (47%)
  starting transfers between devices  5.4 us (36%)
  local copies, waits for them, and re-layouts  0.89 us (6%)
  other arithmetic  0.88 us (6%)
  waiting for transfers between devices  0.52 us (4%)
    ppermute x1, starting transfers between devices, on_device(): theirs = lax.ppermute(send, 'row', swap)  4.28 us
    pallas_call x1, Pallas kernels, on_device(): pl.pallas_call(inner_kernel, out_shape=(shape((height, GROUP, 3 * width),...  4.06 us
    pallas_call x1, Pallas kernels, on_device(): pl.pallas_call(prep_kernel, out_shape=(shape(image_tokens.shape, BF16), s...  1.55 us
    pallas_call x1, Pallas kernels, on_device(): pl.pallas_call(edge_kernel, out_shape=(half_shape, half_shape), in_specs=...  1.29 us
    concatenate x1, other arithmetic, on_device(): both = jnp.concatenate([mine, mine], 1)  0.83 us
    dynamic_update_slice x1, local copies, waits for them, and re-layouts, on_device(): return lax.dynamic_update_slice_in_dim(both, theirs, (1 - core) * part, 1)  0.72 us
    ppermute x1, starting transfers between devices, on_device(): lax.ppermute(jnp.concatenate([outer, column(0)], 0), ('row', 'col'), pairs)  0.66 us
    ppermute x1, starting transfers between devices, on_device(): lax.ppermute(image_tokens, 'row', swap)  0.45 us
  transfers between devices with their start and end apart: 3, of which 2 were waited for; matrix products, arithmetic and copies ran while one was open for 6% of the time, Pallas kernels for 38%

profile of v5, /device:TPU:0, one launch (start us, length us, event | category | flops | bytes accessed | tf_op | source)
XLA Modules:
  0.0 14.7 jit_solution(7989664327296712288)
XLA Ops:
  0.0 0.5 %collective-permute-start = (bf16[32,32,256]{2,1,0:T(8,128)(2,1)}, bf16[32,32,256]{2,1,0:T(8,128)(2,1)S(1)}, u32[]{:S(2)}, u32[]{:S(2)}) collective-permute-start(bf16[32,32,256]{2,1,0:T(8,128)(2,1)} %own_hbm), channel_id=1, source_target_pairs={{0,16},{16,0},{1,17},{17,1},{2,18},{18,2},{3,19},{19,3},{4,20},{20... | collective-permute-start | bytes 1572872 | tf_op jit(solution)/shard_map/ppermute | solution.py:356
  0.5 1.6 %shard_map.100 = (bf16[32,32,256]{2,1,0:T(8,128)(2,1)S(1)}, bf16[256,768]{1,0:T(8,128)(2,1)S(1)}, bf16[256,256]{1,0:T(8,128)(2,1)S(1)}, bf16[512,256]{1,0:T(8,12...) custom-call(bf16[32,32,256]{2,1,0:T(8,128)(2,1)} %own_hbm, ...), custom_call_target="tpu_custom_call" | custom-call | bytes 3145728 | tf_op jit(solution)/shard_map/pallas_call | solution.py:361
  2.0 0.2 %collective-permute-done.other_ref = bf16[32,32,256]{2,1,0:T(8,128)(2,1)S(1)} collective-permute-done((bf16[32,32,256]{2,1,0:T(8,128)(2,1)}, bf16[32,32,256]{2,1,0:T(8,128)(2,1)S(1)}, u32[]{:S(2)}, u32[]{:S(2)}) %collective-permute-start) | collective-permute-done | bytes 524320 | tf_op jit(solution)/shard_map/ppermute | solution.py:356
  2.2 0.2 %fusion.4 = (bf16[32,1,256]{2,1,0:T(2,128)(2,1)S(1)}, bf16[32,1,256]{2,1,0:T(2,128)(2,1)S(1)}, bf16[32,1,256]{2,1,0:T(2,128)(2,1)S(1)}, bf16[32,1,256]{2,1,0:T(2...) fusion(bf16[32,32,256]{2,1,0:T(8,128)(2,1)S(1)} %collective-per, ...), kind=kLoop, calls=%fused_computation.12 | loop fusion | bytes 262144 | tf_op jit(solution)/shard_map/slice | solution.py:395
  2.4 0.7 %collective-permute-start.1 = (bf16[64,256]{1,0:T(8,128)(2,1)S(1)}, bf16[64,256]{1,0:T(8,128)(2,1)S(1)}, u32[]{:S(2)}, u32[]{:S(2)}) collective-permute-start(bf16[64,256]{1,0:T(8,128)(2,1)S(1)} %pad_maximum_fusion.2), channel_id=1, source_target_pairs={{16,1},{1,16},{17,2},{2,17},{18,3},{3,18},{19,4},{4,19},{20,5},{5,... | collective-permute-start | bytes 98312 | tf_op jit(solution)/shard_map/ppermute | solution.py:400
  3.1 4.1 %shard_map.101 = (f32[64,8,768]{2,1,0:T(8,128)S(1)}, f32[2,32,8,256]{3,2,1,0:T(8,128)S(1)}) custom-call(bf16[32,32,256]{2,1,0:T(8,128)(2,1)S(1)} %get-tuple-element.19.own_ref, bf16[32,32,256]{2,1,0:T(8,128)(2,1)S(1)} %collective-permute-done.other_ref, bf16[96,256]{1,0:T(8,128)(2,1)S(1)} %get-tuple-element.20.strips_ref, ...), custom_call_target="tpu_custom_call" | custom-call | flops 1000000000 | bytes 12582912 | tf_op jit(solution)/shard_map/pallas_call | solution.py:402
  7.2 0.0 collective-permute-done.1.halo_ref
  7.2 1.3 %shard_map.102 = (bf16[32,16,256]{2,1,0:T(8,128)(2,1)S(1)}, bf16[32,16,256]{2,1,0:T(8,128)(2,1)S(1)}) custom-call(bf16[64,256]{1,0:T(8,128)(2,1)S(1)} %collective-permute-done.1.halo_ref, f32[64,8,768]{2,1,0:T(8,128)S(1)} %get-tuple-element.27.mixed_ref, f32[2,32,8,256]{3,2,1,0:T(8,128)S(1)} %get-tuple-element.28.inner_ref, ...), custom_call_target="tpu_custom_call" | custom-call | flops 300000000 | bytes 4194304 | tf_op jit(solution)/shard_map/pallas_call | solution.py:423
  8.5 4.3 %collective-permute-start.2 = (bf16[32,16,256]{2,1,0:T(8,128)(2,1)S(1)}, bf16[32,16,256]{2,1,0:T(8,128)(2,1)S(1)}, u32[]{:S(2)}, u32[]{:S(2)}) collective-permute-start(bf16[32,16,256]{2,1,0:T(8,128)(2,1)S(1)} %get-tuple-element.30), channel_id=1, source_target_pairs={{0,16},{16,0},{1,17},{17,1},{2,18},{18,2},{3,19},{19,3},{4,20},{20... | collective-permute-start | bytes 786440 | tf_op jit(solution)/shard_map/ppermute | solution.py:438
  12.8 0.8 %pad_maximum_fusion = bf16[32,32,256]{2,1,0:T(8,128)(2,1)} fusion(bf16[32,16,256]{2,1,0:T(8,128)(2,1)S(1)} %get-tuple-element.29), kind=kLoop, calls=%fused_computation | loop fusion | flops 1048576 | bytes 786432 | tf_op jit(solution)/shard_map/concatenate | solution.py:439
  13.6 0.3 %collective-permute-done.2 = bf16[32,16,256]{2,1,0:T(8,128)(2,1)S(1)} collective-permute-done((bf16[32,16,256]{2,1,0:T(8,128)(2,1)S(1)}, bf16[32,16,256]{2,1,0:T(8,128)(2,1)S(1)}, u32[]{:S(2)}, u32[]{:S(2)}) %collective-permute-start.2) | collective-permute-done | bytes 262176 | tf_op jit(solution)/shard_map/ppermute | solution.py:438
  14.0 0.7 %constant_dynamic-update-slice_fusion = bf16[32,32,256]{2,1,0:T(8,128)(2,1)} fusion(bf16[32,32,256]{2,1,0:T(8,128)(2,1)} %pad_maximum_fusion, bf16[32,16,256]{2,1,0:T(8,128)(2,1)S(1)} %collective-permute-done.2, s32[]{:T(128)S(6)} %select_n.44), kind=kLoop, calls=%fused_computation.11 | loop fusion | bytes 524292 | tf_op jit(solution)/shard_map/dynamic_update_slice | solution.py:440
  (5 shorter events, 0.0 us)
Async XLA Ops:
  0.0 2.2 %collective-permute-start = (bf16[32,32,256]{2,1,0:T(8,128)(2,1)}, bf16[32,32,256]{2,1,0:T(8,128)(2,1)S(1)}, u32[]{:S(2)}, u32[]{:S(2)}) collective-permute-start(bf16[32,32,256]{2,1,0:T(8,128)(2,1)} %own_hbm), channel_id=1, source_target_pairs={{0,16},{16,0},{1,17},{17,1},{2,18},{18,2},{3,19},{19,3},{4,20},{20... | collective-permute-start | bytes 1572872 | tf_op jit(solution)/shard_map/ppermute | solution.py:356
  2.4 4.8 %collective-permute-start.1 = (bf16[64,256]{1,0:T(8,128)(2,1)S(1)}, bf16[64,256]{1,0:T(8,128)(2,1)S(1)}, u32[]{:S(2)}, u32[]{:S(2)}) collective-permute-start(bf16[64,256]{1,0:T(8,128)(2,1)S(1)} %pad_maximum_fusion.2), channel_id=1, source_target_pairs={{16,1},{1,16},{17,2},{2,17},{18,3},{3,18},{19,4},{4,19},{20,5},{5,... | collective-permute-start | bytes 98312 | tf_op jit(solution)/shard_map/ppermute | solution.py:400
  8.5 5.4 %collective-permute-start.2 = (bf16[32,16,256]{2,1,0:T(8,128)(2,1)S(1)}, bf16[32,16,256]{2,1,0:T(8,128)(2,1)S(1)}, u32[]{:S(2)}, u32[]{:S(2)}) collective-permute-start(bf16[32,16,256]{2,1,0:T(8,128)(2,1)S(1)} %get-tuple-element.30), channel_id=1, source_target_pairs={{0,16},{16,0},{1,17},{17,1},{2,18},{18,2},{3,19},{19,3},{4,20},{20... | collective-permute-start | bytes 786440 | tf_op jit(solution)/shard_map/ppermute | solution.py:438

commit v6 on v5

--- a/solution.py
+++ b/solution.py
@@ -57,14 +57,29 @@
     ).astype(BF16)
 
 
+def project(tokens, strips, core, row, w_in_ref, p_ref, strips_ref):
+    rows, part, width = tokens.shape
+    count = rows * part
+    got = jnp.dot(
+        jnp.concatenate([tokens.reshape(count, width), strips], 0),
+        w_in_ref[...],
+        preferred_element_type=F32,
+    )
+    grid = got[:count].reshape(rows, part, 3 * width)
+    p_ref[core, pl.ds(row + 1, rows)] = grid[:, :GROUP]
+    p_ref[1 - core, pl.ds(row + 1, rows)] = grid[:, GROUP:]
+    strips_ref[...] = got[count:]
+
+
 def prep_kernel(
     own_hbm, w_in_hbm, w_out_hbm, fwd_hbm, bwd_hbm, spec_hbm, filt_hbm, gain_hbm, kernel_hbm, bias_hbm,
-    own_ref, w_in_ref, w_out_ref, fwd_ref, bwd_ref, taps_ref, h_ref, outer_ref, strips_ref,
-    spec_ref, filt_ref, gain_ref, kernel_ref, bias_ref, sems,
+    p_ref, strips_ref, w_in_ref, w_out_ref, fwd_ref, bwd_ref, taps_ref, h_ref, outer_ref,
+    own_ref, spec_ref, filt_ref, gain_ref, kernel_ref, bias_ref, sems,
 ):
     core = lax.axis_index("row")
-    rows, cols, _ = own_ref.shape
+    rows, cols, width = own_ref.shape
     part = cols // 2
+    height = 2 * rows
     moves = [
         (spec_hbm, spec_ref),
         (filt_hbm, filt_ref),
@@ -89,6 +104,9 @@
     gain = gain_ref[...]
     h_ref[0:rows, :] = h_ref[0:rows, :] + gain
     h_ref[2 * rows : 3 * rows, :] = h_ref[2 * rows : 3 * rows, :] + gain
+    for slot in range(2):
+        p_ref[slot, 0] = jnp.zeros((GROUP, 3 * width), F32)
+        p_ref[slot, height + 1] = jnp.zeros((GROUP, 3 * width), F32)
     copies[3].wait()
     start = pl.multiple_of(core * part, part)
     mine = pick_columns(
@@ -96,16 +114,19 @@
         [core * (part - 1), GROUP - 1 + core, GROUP - core],
     )
     outer_ref[...] = mine[:rows]
-    strips_ref[: 2 * rows] = mine[rows:]
-    start = pl.multiple_of((1 - core) * part, part)
-    strips_ref[2 * rows :] = pick_columns(
-        own_ref[:, pl.ds(start, part), :], [core * (part - 1)]
-    )
-    for copy in copies[4:]:
+    far = pl.multiple_of((1 - core) * part, part)
+    theirs = pick_columns(own_ref[:, pl.ds(far, part), :], [core * (part - 1)])
+    for copy in copies[4:7]:
         copy.wait()
+    project(
+        own_ref[:, pl.ds(start, part), :], jnp.concatenate([mine[rows:], theirs], 0),
+        core, core * rows, w_in_ref, p_ref, strips_ref,
+    )
     for a in range(3):
         taps_ref[3 * a : 3 * a + 3, :] = kernel_ref[a].astype(F32)
     taps_ref[9, :] = bias_ref[...]
+    for copy in copies[7:]:
+        copy.wait()
 
 
 def edge_terms(first, second, core, taps, edge_ref):
@@ -163,27 +184,24 @@
 
 
 def conv_steps(mixed, fwd_ref, bwd_ref, w_out_ref, h_ref, prod_ref, z_ref, put):
-    height_group, width = prod_ref.shape
-    height = height_group // GROUP
-    rows = height // 2
-    block = rows * GROUP
-    spectra = []
-    for h in range(2):
-        for row in range(h * rows, (h + 1) * rows, 2):
+    block, width = prod_ref.shape[0], prod_ref.shape[1] // 2
+    rows = block // GROUP
+    for row in range(0, rows, 2):
+        for h in range(2):
             for base in range(0, width, LANES):
-                two = [mixed(r, width + base) * mixed(r, 2 * width + base) for r in (row, row + 1)]
-                prod_ref[row * GROUP : (row + 2) * GROUP, base : base + LANES] = jnp.concatenate(
+                two = [
+                    mixed(h * rows + r, width + base) * mixed(h * rows + r, 2 * width + base)
+                    for r in (row, row + 1)
+                ]
+                at = h * width + base
+                prod_ref[row * GROUP : (row + 2) * GROUP, at : at + LANES] = jnp.concatenate(
                     two, 0
                 ).astype(BF16)
-            if row % 8 == 6:
-                yield
-        spectra.append(
-            jnp.dot(
-                fwd_ref[...], prod_ref[h * block : (h + 1) * block], preferred_element_type=F32
-            )
-        )
-        yield
-    low, high = spectra
+        if row % 4 == 2:
+            yield
+    spectra = jnp.dot(fwd_ref[...], prod_ref[...], preferred_element_type=F32)
+    low, high = spectra[:, :width], spectra[:, width:]
+    yield
     for k in range(0, rows, 2):
         parts = [[], [], [], []]
         for s in (k, k + 1):
@@ -198,62 +216,48 @@
             parts[2].append(lr * all_r - li * all_i + hr * near_r - hi * near_i)
             parts[3].append(lr * all_i + li * all_2 + hr * near_i + hi * near_2)
         for j in range(4):
-            at = (j % 2) * block + k * GROUP
-            z_ref[j // 2, at : at + 2 * GROUP, :] = jnp.concatenate(parts[j], 0).astype(BF16)
+            at, lane = (j % 2) * block + k * GROUP, (j // 2) * width
+            z_ref[at : at + 2 * GROUP, lane : lane + width] = jnp.concatenate(parts[j], 0).astype(BF16)
         if k % 4 == 2:
             yield
-    convs = []
+    conv = jnp.dot(bwd_ref[...], z_ref[...], preferred_element_type=F32)
+    yield
+    gated = []
     for h in range(2):
-        convs.append(jnp.dot(bwd_ref[...], z_ref[h], preferred_element_type=F32))
-        yield
-    for h in range(2):
-        gated = []
         for r in range(rows):
             line = [
-                mixed(h * rows + r, base) * convs[h][r * GROUP : (r + 1) * GROUP, base : base + LANES]
+                mixed(h * rows + r, base)
+                * conv[r * GROUP : (r + 1) * GROUP, h * width + base : h * width + base + LANES]
                 for base in range(0, width, LANES)
             ]
             gated.append(jnp.concatenate(line, 1))
-        final = jnp.dot(
-            jnp.concatenate(gated, 0).astype(BF16), w_out_ref[...], preferred_element_type=F32
-        )
-        put(h, final.reshape(rows, GROUP, width))
         yield
+    final = jnp.dot(
+        jnp.concatenate(gated, 0).astype(BF16), w_out_ref[...], preferred_element_type=F32
+    )
+    put(final.reshape(2, rows, GROUP, width))
 
 
 def inner_kernel(
-    own_ref, other_ref, strips_ref, other_strips_ref,
+    _, strips_ref, other_ref, other_strips_ref,
     w_in_ref, taps_ref, fwd_ref, bwd_ref, w_out_ref, h_ref,
-    edge_mixed_ref, out_ref,
-    p_ref, strip_ref, side_ref, edge_side_ref, mixed_ref, prod_ref, z_ref,
+    p_ref, edge_mixed_ref, out_ref,
+    got_strips_ref, strip_ref, side_ref, edge_side_ref, mixed_ref, prod_ref, z_ref,
 ):
     core = lax.axis_index("row")
-    rows, cols, width = own_ref.shape
+    rows, cols, width = other_ref.shape
     part = cols // 2
     height = 2 * rows
     start = pl.multiple_of(core * part, part)
-
-    for slot in range(2):
-        p_ref[slot, 0] = jnp.zeros((GROUP, 3 * width), F32)
-        p_ref[slot, height + 1] = jnp.zeros((GROUP, 3 * width), F32)
-    strips = []
-    for row, ref, strip in (
-        (core * rows, own_ref, strips_ref),
-        ((1 - core) * rows, other_ref, other_strips_ref),
-    ):
-        count = rows * part
-        tokens = ref[:, pl.ds(start, part), :].reshape(count, width)
-        got = jnp.dot(
-            jnp.concatenate([tokens, strip[...]], 0), w_in_ref[...], preferred_element_type=F32
-        )
-        grid = got[:count].reshape(rows, part, 3 * width)
-        p_ref[core, pl.ds(row + 1, rows)] = grid[:, :GROUP]
-        p_ref[1 - core, pl.ds(row + 1, rows)] = grid[:, GROUP:]
-        strips.append(
-            [got[count + j * rows : count + (j + 1) * rows] for j in range(3)]
-        )
-
-    near, edge_near, far = zip(*strips)
+    project(
+        other_ref[:, pl.ds(start, part), :], other_strips_ref[...],
+        core, (1 - core) * rows, w_in_ref, p_ref, got_strips_ref,
+    )
+
+    near, edge_near, far = (
+        [ref[j * rows : (j + 1) * rows, :] for ref in (strips_ref, got_strips_ref)]
+        for j in range(3)
+    )
     side_ref[core] = edge_terms(*near, core, column_taps(taps_ref, core, 0), strip_ref.at[0])
     side_ref[1 - core] = edge_terms(*far, core, column_taps(taps_ref, core, 2), strip_ref.at[1])
     edge_side_ref[1 - core] = edge_terms(
@@ -278,8 +282,8 @@
     def store_edge(row, at, value):
         edge_mixed_ref[row, :, at] = value
 
-    def put(h, final):
-        out_ref[h] = final
+    def put(final):
+        out_ref[...] = final
 
     edge = [
         depthwise_steps(
@@ -322,8 +326,8 @@
         add = jnp.broadcast_to(side_ref[r // 8, r % 8 : r % 8 + 1, at], (GROUP, LANES))
         return mixed_ref[r, :, at] + jnp.where(at_edge, add, 0.0)
 
-    def put(h, final):
-        out_ref[h] = final
+    def put(final):
+        out_ref[...] = final
 
     for _ in conv_steps(
         mixed, fwd_ref, bwd_ref, w_out_ref, h_ref, prod_ref, z_ref, put
@@ -358,10 +362,11 @@
     def keep(array):
         return pltpu.with_memory_space_constraint(array, pltpu.HBM)
 
-    own, w_in_v, w_out_v, fwd_v, bwd_v, taps, spectrum, outer, strips = pl.pallas_call(
+    projected, strips, w_in_v, w_out_v, fwd_v, bwd_v, taps, spectrum, outer = pl.pallas_call(
         prep_kernel,
         out_shape=(
-            shape(image_tokens.shape, BF16),
+            shape((2, height + 2, GROUP, 3 * width), F32),
+            shape((3 * rows, 3 * width), F32),
             shape(w_in.shape, BF16),
             shape(w_out.shape, BF16),
             shape(fwd.shape, BF16),
@@ -369,11 +374,11 @@
             shape((16, 3 * width), F32),
             shape((6 * rows, width), F32),
             shape((rows, width), BF16),
-            shape((3 * rows, width), BF16),
         ),
         in_specs=[hbm] * 10,
         out_specs=(vmem,) * 9,
         scratch_shapes=[
+            pltpu.VMEM(image_tokens.shape, BF16),
             pltpu.VMEM(spec.shape, BF16),
             pltpu.VMEM(long_filter.shape, BF16),
             pltpu.VMEM((1, width), F32),
@@ -399,26 +404,28 @@
         pairs += [(n_col + j, j + 1), (j + 1, n_col + j)]
     halo = lax.ppermute(jnp.concatenate([outer, column(0)], 0), ("row", "col"), pairs)
     other_strips = jnp.concatenate([column(GROUP - 1), column(GROUP), column(part)], 0)
-    edge_mixed, inner = pl.pallas_call(
+    _, edge_mixed, inner = pl.pallas_call(
         inner_kernel,
         out_shape=(
+            shape((2, height + 2, GROUP, 3 * width), F32),
             shape((height, GROUP, 3 * width), F32),
             shape((2, rows, GROUP, width), F32),
         ),
         in_specs=[vmem] * 10,
-        out_specs=(vmem,) * 2,
+        out_specs=(vmem,) * 3,
+        input_output_aliases={0: 0},
         scratch_shapes=[
-            pltpu.VMEM((2, height + 2, GROUP, 3 * width), F32),
+            pltpu.VMEM((3 * rows, 3 * width), F32),
             pltpu.VMEM((3, height + 16, 3 * width), F32),
             pltpu.VMEM((2, height // 8, 8, 3 * width), F32),
             pltpu.VMEM((2, height // 8, 8, 3 * width), F32),
             pltpu.VMEM((height, GROUP, 3 * width), F32),
-            pltpu.VMEM((height * GROUP, width), BF16),
-            pltpu.VMEM((2, 2 * rows * GROUP, width), BF16),
+            pltpu.VMEM((rows * GROUP, 2 * width), BF16),
+            pltpu.VMEM((2 * rows * GROUP, 2 * width), BF16),
         ],
         compiler_params=limit,
         cost_estimate=pl.CostEstimate(flops=10**9, bytes_accessed=12 * 1024 * 1024, transcendentals=0),
-    )(own, other, strips, other_strips, w_in_v, taps, fwd_v, bwd_v, w_out_v, spectrum)
+    )(projected, strips, other, other_strips, w_in_v, taps, fwd_v, bwd_v, w_out_v, spectrum)
     half_shape = shape((rows, part, width), BF16)
     mine, send = pl.pallas_call(
         edge_kernel,
@@ -428,8 +435,8 @@
         scratch_shapes=[
             pltpu.VMEM((height + 16, 3 * width), F32),
             pltpu.VMEM((height // 8, 8, 3 * width), F32),
-            pltpu.VMEM((height * GROUP, width), BF16),
-            pltpu.VMEM((2, 2 * rows * GROUP, width), BF16),
+            pltpu.VMEM((rows * GROUP, 2 * width), BF16),
+            pltpu.VMEM((2 * rows * GROUP, 2 * width), BF16),
             pltpu.VMEM((2, rows, GROUP, width), F32),
         ],
         compiler_params=limit,

time: 14.8 us -> 14.4 us (0.973)
  starting transfers between devices: 5.4 us -> 5.13 us
  waiting for transfers between devices: 0.52 us -> 0.33 us
    ppermute x1, starting transfers between devices: 4.28 us -> 4.02 us  [on_device(): theirs = lax.ppermute(send, 'row', swap)]
    ppermute x1, waiting for transfers between devices: 0.19 us -> 0.01 us  [on_device(): lax.ppermute(image_tokens, 'row', swap)]
  transfers between devices with their start and end apart: 3 -> 3, of which waited for: 2 -> 1; matrix products, arithmetic and copies ran while one was open for 6% -> 6% of each run, Pallas kernels for 38% -> 40%
where the time goes in v6:
time: 14.4 us; the launch traced here: 14.3 us
  Pallas kernels  6.97 us (48%)
  starting transfers between devices  5.13 us (36%)
  local copies, waits for them, and re-layouts  0.89 us (6%)
  other arithmetic  0.88 us (6%)
  waiting for transfers between devices  0.33 us (2%)
    ppermute x1, starting transfers between devices, on_device(): theirs = lax.ppermute(send, 'row', swap)  4.02 us
    pallas_call x1, Pallas kernels, on_device(): pl.pallas_call(inner_kernel, out_shape=(shape((2, height + 2, GROUP, 3 *...  3.72 us
    pallas_call x1, Pallas kernels, on_device(): pl.pallas_call(prep_kernel, out_shape=(shape((2, height + 2, GROUP, 3 * w...  2 us
    pallas_call x1, Pallas kernels, on_device(): pl.pallas_call(edge_kernel, out_shape=(half_shape, half_shape), in_specs=...  1.25 us
    concatenate x1, other arithmetic, on_device(): both = jnp.concatenate([mine, mine], 1)  0.83 us
    dynamic_update_slice x1, local copies, waits for them, and re-layouts, on_device(): return lax.dynamic_update_slice_in_dim(both, theirs, (1 - core) * part, 1)  0.72 us
    ppermute x1, starting transfers between devices, on_device(): lax.ppermute(jnp.concatenate([outer, column(0)], 0), ('row', 'col'), pairs)  0.66 us
    ppermute x1, starting transfers between devices, on_device(): lax.ppermute(image_tokens, 'row', swap)  0.45 us
  transfers between devices with their start and end apart: 3, of which 1 were waited for; matrix products, arithmetic and copies ran while one was open for 6% of the time, Pallas kernels for 40%

profile of v6, /device:TPU:0, one launch (start us, length us, event | category | flops | bytes accessed | tf_op | source)
XLA Modules:
  0.0 14.3 jit_solution(14209881814948798538)
XLA Ops:
  0.0 0.5 %collective-permute-start = (bf16[32,32,256]{2,1,0:T(8,128)(2,1)}, bf16[32,32,256]{2,1,0:T(8,128)(2,1)S(1)}, u32[]{:S(2)}, u32[]{:S(2)}) collective-permute-start(bf16[32,32,256]{2,1,0:T(8,128)(2,1)} %own_hbm), channel_id=1, source_target_pairs={{0,16},{16,0},{1,17},{17,1},{2,18},{18,2},{3,19},{19,3},{4,20},{20... | collective-permute-start | bytes 1572872 | tf_op jit(solution)/shard_map/ppermute | solution.py:360
  0.5 2.0 %shard_map.100 = (f32[2,66,8,768]{3,2,1,0:T(8,128)S(1)}, f32[96,768]{1,0:T(8,128)S(1)}, bf16[256,768]{1,0:T(8,128)(2,1)S(1)}, bf16[256,256]{1,0:T(8,128)(2,1)S(1...) custom-call(bf16[32,32,256]{2,1,0:T(8,128)(2,1)} %own_hbm, ...), custom_call_target="tpu_custom_call" | custom-call | bytes 3145728 | tf_op jit(solution)/shard_map/pallas_call | solution.py:365
  2.5 0.0 collective-permute-done.other_ref
  2.5 0.2 %fusion.4 = (bf16[32,1,256]{2,1,0:T(2,128)(2,1)S(1)}, bf16[32,1,256]{2,1,0:T(2,128)(2,1)S(1)}, bf16[32,1,256]{2,1,0:T(2,128)(2,1)S(1)}, bf16[32,1,256]{2,1,0:T(2...) fusion(bf16[32,32,256]{2,1,0:T(8,128)(2,1)S(1)} %collective-per, ...), kind=kLoop, calls=%fused_computation.12 | loop fusion | bytes 262144 | tf_op jit(solution)/shard_map/slice | solution.py:400
  2.7 0.7 %collective-permute-start.1 = (bf16[64,256]{1,0:T(8,128)(2,1)S(1)}, bf16[64,256]{1,0:T(8,128)(2,1)S(1)}, u32[]{:S(2)}, u32[]{:S(2)}) collective-permute-start(bf16[64,256]{1,0:T(8,128)(2,1)S(1)} %pad_maximum_fusion.2), channel_id=1, source_target_pairs={{16,1},{1,16},{17,2},{2,17},{18,3},{3,18},{19,4},{4,19},{20,5},{5,... | collective-permute-start | bytes 98312 | tf_op jit(solution)/shard_map/ppermute | solution.py:405
  3.4 3.7 %shard_map.101 = (f32[2,66,8,768]{3,2,1,0:T(8,128)S(1)}, f32[64,8,768]{2,1,0:T(8,128)S(1)}, f32[2,32,8,256]{3,2,1,0:T(8,128)S(1)}) custom-call(f32[2,66,8,768]{3,2,1,0:T(8,128)S(1)} %get-tuple-element.19._, f32[96,768]{1,0:T(8,128)S(1)} %get-tuple-element.20.strips_ref, ...), custom_call_target="tpu_custom_call", output_to_operand_aliasing={{0}: (0, {})} | custom-call | flops 1000000000 | bytes 12582912 | tf_op jit(solution)/shard_map/pallas_call | solution.py:407
  7.1 0.0 collective-permute-done.1.halo_ref
  7.1 1.2 %shard_map.102 = (bf16[32,16,256]{2,1,0:T(8,128)(2,1)S(1)}, bf16[32,16,256]{2,1,0:T(8,128)(2,1)S(1)}) custom-call(bf16[64,256]{1,0:T(8,128)(2,1)S(1)} %collective-permute-done.1.halo_ref, f32[64,8,768]{2,1,0:T(8,128)S(1)} %get-tuple-element.27.mixed_ref, f32[2,32,8,256]{3,2,1,0:T(8,128)S(1)} %get-tuple-element.28.inner_ref, ...), custom_call_target="tpu_custom_call" | custom-call | flops 300000000 | bytes 4194304 | tf_op jit(solution)/shard_map/pallas_call | solution.py:430
  8.4 4.0 %collective-permute-start.2 = (bf16[32,16,256]{2,1,0:T(8,128)(2,1)S(1)}, bf16[32,16,256]{2,1,0:T(8,128)(2,1)S(1)}, u32[]{:S(2)}, u32[]{:S(2)}) collective-permute-start(bf16[32,16,256]{2,1,0:T(8,128)(2,1)S(1)} %get-tuple-element.30), channel_id=1, source_target_pairs={{0,16},{16,0},{1,17},{17,1},{2,18},{18,2},{3,19},{19,3},{4,20},{20... | collective-permute-start | bytes 786440 | tf_op jit(solution)/shard_map/ppermute | solution.py:445
  12.4 0.8 %pad_maximum_fusion = bf16[32,32,256]{2,1,0:T(8,128)(2,1)} fusion(bf16[32,16,256]{2,1,0:T(8,128)(2,1)S(1)} %get-tuple-element.29), kind=kLoop, calls=%fused_computation | loop fusion | flops 1048576 | bytes 786432 | tf_op jit(solution)/shard_map/concatenate | solution.py:446
  13.3 0.3 %collective-permute-done.2 = bf16[32,16,256]{2,1,0:T(8,128)(2,1)S(1)} collective-permute-done((bf16[32,16,256]{2,1,0:T(8,128)(2,1)S(1)}, bf16[32,16,256]{2,1,0:T(8,128)(2,1)S(1)}, u32[]{:S(2)}, u32[]{:S(2)}) %collective-permute-start.2) | collective-permute-done | bytes 262176 | tf_op jit(solution)/shard_map/ppermute | solution.py:445
  13.6 0.7 %constant_dynamic-update-slice_fusion = bf16[32,32,256]{2,1,0:T(8,128)(2,1)} fusion(bf16[32,32,256]{2,1,0:T(8,128)(2,1)} %pad_maximum_fusion, bf16[32,16,256]{2,1,0:T(8,128)(2,1)S(1)} %collective-permute-done.2, s32[]{:T(128)S(6)} %select_n.44), kind=kLoop, calls=%fused_computation.11 | loop fusion | bytes 524292 | tf_op jit(solution)/shard_map/dynamic_update_slice | solution.py:447
  (5 shorter events, 0.0 us)
Async XLA Ops:
  0.0 2.5 %collective-permute-start = (bf16[32,32,256]{2,1,0:T(8,128)(2,1)}, bf16[32,32,256]{2,1,0:T(8,128)(2,1)S(1)}, u32[]{:S(2)}, u32[]{:S(2)}) collective-permute-start(bf16[32,32,256]{2,1,0:T(8,128)(2,1)} %own_hbm), channel_id=1, source_target_pairs={{0,16},{16,0},{1,17},{17,1},{2,18},{18,2},{3,19},{19,3},{4,20},{20... | collective-permute-start | bytes 1572872 | tf_op jit(solution)/shard_map/ppermute | solution.py:360
  2.7 4.5 %collective-permute-start.1 = (bf16[64,256]{1,0:T(8,128)(2,1)S(1)}, bf16[64,256]{1,0:T(8,128)(2,1)S(1)}, u32[]{:S(2)}, u32[]{:S(2)}) collective-permute-start(bf16[64,256]{1,0:T(8,128)(2,1)S(1)} %pad_maximum_fusion.2), channel_id=1, source_target_pairs={{16,1},{1,16},{17,2},{2,17},{18,3},{3,18},{19,4},{4,19},{20,5},{5,... | collective-permute-start | bytes 98312 | tf_op jit(solution)/shard_map/ppermute | solution.py:405
  8.4 5.2 %collective-permute-start.2 = (bf16[32,16,256]{2,1,0:T(8,128)(2,1)S(1)}, bf16[32,16,256]{2,1,0:T(8,128)(2,1)S(1)}, u32[]{:S(2)}, u32[]{:S(2)}) collective-permute-start(bf16[32,16,256]{2,1,0:T(8,128)(2,1)S(1)} %get-tuple-element.30), channel_id=1, source_target_pairs={{0,16},{16,0},{1,17},{17,1},{2,18},{18,2},{3,19},{19,3},{4,20},{20... | collective-permute-start | bytes 786440 | tf_op jit(solution)/shard_map/ppermute | solution.py:445

commit v7 on v6

--- a/solution.py
+++ b/solution.py
@@ -44,36 +44,52 @@
 LANES = 128
 GROUP = 8
 CHUNK = 8
-
-
-def pick_columns(block, columns):
+PITCH = 24
+FIRST = 8
+
+
+def pick_column(block, column):
     rows, cols, width = block.shape
     shape = (rows, rows * cols)
     place = lax.broadcasted_iota(jnp.int32, shape, 1)
-    row = lax.broadcasted_iota(jnp.int32, shape, 0) * cols
-    chosen = [jnp.where(place == row + column, 1.0, 0.0).astype(BF16) for column in columns]
+    wanted = lax.broadcasted_iota(jnp.int32, shape, 0) * cols + column
     return jnp.dot(
-        jnp.concatenate(chosen, 0), block.reshape(rows * cols, width), preferred_element_type=F32
+        jnp.where(place == wanted, 1.0, 0.0).astype(BF16),
+        block.reshape(rows * cols, width),
+        preferred_element_type=F32,
     ).astype(BF16)
 
 
-def project(tokens, strips, core, row, w_in_ref, p_ref, strips_ref):
+def row_place(row, column):
+    return row * PITCH + FIRST + column
+
+
+def project(tokens, strip, core, row, w_in_ref, p_ref):
     rows, part, width = tokens.shape
     count = rows * part
     got = jnp.dot(
-        jnp.concatenate([tokens.reshape(count, width), strips], 0),
+        jnp.concatenate([tokens.reshape(count, width), strip], 0),
         w_in_ref[...],
         preferred_element_type=F32,
     )
-    grid = got[:count].reshape(rows, part, 3 * width)
-    p_ref[core, pl.ds(row + 1, rows)] = grid[:, :GROUP]
-    p_ref[1 - core, pl.ds(row + 1, rows)] = grid[:, GROUP:]
-    strips_ref[...] = got[count:]
+    for t in range(3 * width // LANES):
+        at = slice(t * LANES, (t + 1) * LANES)
+        for r in range(rows):
+            place = pl.multiple_of(row_place(row + r + 1, 0), GROUP)
+            p_ref[t, pl.ds(place, part), :] = got[r * part : (r + 1) * part, at]
+        for r in range(0, rows, GROUP):
+            beside = got[count + r : count + r + GROUP, at]
+            for column, value in (
+                (-1, jnp.where(core == 1, beside, 0.0)),
+                (part, jnp.where(core == 0, beside, 0.0)),
+            ):
+                place = row_place(row + r + 1, column)
+                p_ref[t, pl.ds(place, GROUP, stride=PITCH), :] = value
 
 
 def prep_kernel(
     own_hbm, w_in_hbm, w_out_hbm, fwd_hbm, bwd_hbm, spec_hbm, filt_hbm, gain_hbm, kernel_hbm, bias_hbm,
-    p_ref, strips_ref, w_in_ref, w_out_ref, fwd_ref, bwd_ref, taps_ref, h_ref, outer_ref,
+    p_ref, w_in_ref, w_out_ref, fwd_ref, bwd_ref, taps_ref, h_ref, outer_ref,
     own_ref, spec_ref, filt_ref, gain_ref, kernel_ref, bias_ref, sems,
 ):
     core = lax.axis_index("row")
@@ -104,24 +120,18 @@
     gain = gain_ref[...]
     h_ref[0:rows, :] = h_ref[0:rows, :] + gain
     h_ref[2 * rows : 3 * rows, :] = h_ref[2 * rows : 3 * rows, :] + gain
-    for slot in range(2):
-        p_ref[slot, 0] = jnp.zeros((GROUP, 3 * width), F32)
-        p_ref[slot, height + 1] = jnp.zeros((GROUP, 3 * width), F32)
+    for t in range(p_ref.shape[0]):
+        for row in (0, height + 1):
+            p_ref[t, row * PITCH : row * PITCH + PITCH + GROUP, :] = jnp.zeros((PITCH + GROUP, LANES), F32)
     copies[3].wait()
     start = pl.multiple_of(core * part, part)
-    mine = pick_columns(
-        own_ref[:, pl.ds(start, part), :],
-        [core * (part - 1), GROUP - 1 + core, GROUP - core],
-    )
-    outer_ref[...] = mine[:rows]
     far = pl.multiple_of((1 - core) * part, part)
-    theirs = pick_columns(own_ref[:, pl.ds(far, part), :], [core * (part - 1)])
+    inner_edge = core * (part - 1)
+    outer_ref[...] = pick_column(own_ref[:, pl.ds(start, part), :], inner_edge)
+    beside = pick_column(own_ref[:, pl.ds(far, part), :], inner_edge)
     for copy in copies[4:7]:
         copy.wait()
-    project(
-        own_ref[:, pl.ds(start, part), :], jnp.concatenate([mine[rows:], theirs], 0),
-        core, core * rows, w_in_ref, p_ref, strips_ref,
-    )
+    project(own_ref[:, pl.ds(start, part), :], beside, core, core * rows, w_in_ref, p_ref)
     for a in range(3):
         taps_ref[3 * a : 3 * a + 3, :] = kernel_ref[a].astype(F32)
     taps_ref[9, :] = bias_ref[...]
@@ -154,33 +164,42 @@
     ]
 
 
-def depthwise_steps(load, side_ref, taps_ref, chunk, store, bases):
-    sub = lax.broadcasted_iota(jnp.int32, (GROUP, LANES), 0)
-    is_first = sub == 0
-    is_last = sub == GROUP - 1
+def depthwise_steps(p_ref, first, taps_ref, chunk, store, bases):
     for base in bases:
         at = slice(base, base + LANES)
         tap = [
+            jnp.broadcast_to(taps_ref[k : k + 1, at], (GROUP, LANES)) for k in range(10)
+        ]
+        loaded = [
             [
-                jnp.broadcast_to(taps_ref[3 * a + b : 3 * a + b + 1, at], (GROUP, LANES))
+                p_ref[
+                    base // LANES,
+                    pl.ds(row_place(chunk * CHUNK + r, first + b - 1), GROUP, stride=2),
+                    :,
+                ]
                 for b in range(3)
             ]
-            for a in range(3)
+            for r in range(CHUNK + 2)
         ]
-        bias = jnp.broadcast_to(taps_ref[9:10, at], (GROUP, LANES))
-        loaded = [load(chunk * CHUNK + r, at) for r in range(CHUNK + 2)]
         for r in range(CHUNK):
-            u = [
-                loaded[r] * tap[0][b] + loaded[r + 1] * tap[1][b] + loaded[r + 2] * tap[2][b]
-                for b in range(3)
-            ]
-            west = jnp.broadcast_to(side_ref[0, chunk, r : r + 1, at], (GROUP, LANES))
-            east = jnp.broadcast_to(side_ref[1, chunk, r : r + 1, at], (GROUP, LANES))
-            value = u[1] + bias
-            value = value + jnp.where(is_first, west, pltpu.roll(u[0], 1, 0))
-            value = value + jnp.where(is_last, east, pltpu.roll(u[2], GROUP - 1, 0))
+            value = tap[9]
+            for a in range(3):
+                row = loaded[r + a]
+                value = value + (
+                    row[0] * tap[3 * a] + row[1] * tap[3 * a + 1] + row[2] * tap[3 * a + 2]
+                )
             store(chunk * CHUNK + r, at, value)
         yield
+
+
+def interleave(out_ref, final, first):
+    _, rows, _, width = final.shape
+    for h in range(2):
+        for t in range(width // LANES):
+            for r in range(rows):
+                out_ref[h, t, pl.ds(r * 2 * GROUP + first, GROUP, stride=2), :] = final[
+                    h, r, :, t * LANES : (t + 1) * LANES
+                ]
 
 
 def conv_steps(mixed, fwd_ref, bwd_ref, w_out_ref, h_ref, prod_ref, z_ref, put):
@@ -239,10 +258,10 @@
 
 
 def inner_kernel(
-    _, strips_ref, other_ref, other_strips_ref,
+    _, other_ref, other_strip_ref,
     w_in_ref, taps_ref, fwd_ref, bwd_ref, w_out_ref, h_ref,
     p_ref, edge_mixed_ref, out_ref,
-    got_strips_ref, strip_ref, side_ref, edge_side_ref, mixed_ref, prod_ref, z_ref,
+    mixed_ref, prod_ref, z_ref,
 ):
     core = lax.axis_index("row")
     rows, cols, width = other_ref.shape
@@ -250,28 +269,16 @@
     height = 2 * rows
     start = pl.multiple_of(core * part, part)
     project(
-        other_ref[:, pl.ds(start, part), :], other_strips_ref[...],
-        core, (1 - core) * rows, w_in_ref, p_ref, got_strips_ref,
-    )
-
-    near, edge_near, far = (
-        [ref[j * rows : (j + 1) * rows, :] for ref in (strips_ref, got_strips_ref)]
-        for j in range(3)
-    )
-    side_ref[core] = edge_terms(*near, core, column_taps(taps_ref, core, 0), strip_ref.at[0])
-    side_ref[1 - core] = edge_terms(*far, core, column_taps(taps_ref, core, 2), strip_ref.at[1])
-    edge_side_ref[1 - core] = edge_terms(
-        *edge_near, core, column_taps(taps_ref, core, 2), strip_ref.at[2]
-    )
-    edge_side_ref[core] = jnp.zeros(edge_side_ref.shape[1:], F32)
+        other_ref[:, pl.ds(start, part), :], other_strip_ref[...],
+        core, (1 - core) * rows, w_in_ref, p_ref,
+    )
 
     def store_inner(row, at, value):
         mixed_ref[row, :, at] = value
 
     def inner_chunk(i, carry):
         steps = depthwise_steps(
-            lambda row, at: p_ref[1, row, :, at], side_ref, taps_ref, i, store_inner,
-            range(0, 3 * width, LANES),
+            p_ref, 1 - core, taps_ref, i, store_inner, range(0, 3 * width, LANES)
         )
         for _ in steps:
             pass
@@ -283,12 +290,10 @@
         edge_mixed_ref[row, :, at] = value
 
     def put(final):
-        out_ref[...] = final
+        interleave(out_ref, final, 1 - core)
 
     edge = [
-        depthwise_steps(
-            lambda row, at: p_ref[0, row, :, at], edge_side_ref, taps_ref, i, store_edge, [base]
-        )
+        depthwise_steps(p_ref, core, taps_ref, i, store_edge, [base])
         for i in range(height // CHUNK)
         for base in range(0, 3 * width, LANES)
     ]
@@ -308,9 +313,9 @@
 
 
 def edge_kernel(
-    halo_ref, mixed_ref, inner_ref, w_in_ref, taps_ref, fwd_ref, bwd_ref, w_out_ref, h_ref,
-    mine_ref, send_ref,
-    strip_ref, side_ref, prod_ref, z_ref, out_ref,
+    _, halo_ref, mixed_ref, w_in_ref, taps_ref, fwd_ref, bwd_ref, w_out_ref, h_ref,
+    out_ref, mine_ref, send_ref,
+    strip_ref, side_ref, prod_ref, z_ref,
 ):
     core = lax.axis_index("row")
     rows, part, width = mine_ref.shape
@@ -327,16 +332,17 @@
         return mixed_ref[r, :, at] + jnp.where(at_edge, add, 0.0)
 
     def put(final):
-        out_ref[...] = final
+        interleave(out_ref, final, core)
 
     for _ in conv_steps(
         mixed, fwd_ref, bwd_ref, w_out_ref, h_ref, prod_ref, z_ref, put
     ):
         pass
     for ref, half in ((mine_ref, core), (send_ref, 1 - core)):
-        pair = [out_ref[half], inner_ref[half]]
-        ref[:, :GROUP] = jnp.where(core == 0, pair[0], pair[1]).astype(BF16)
-        ref[:, GROUP:] = jnp.where(core == 0, pair[1], pair[0]).astype(BF16)
+        for t in range(width // LANES):
+            ref[:, :, t * LANES : (t + 1) * LANES] = (
+                out_ref[half, t].reshape(rows, part, LANES).astype(BF16)
+            )
 
 
 def on_device(image_tokens, w_in, conv_kernel, conv_bias, long_filter, skip_gain, w_out):
@@ -354,6 +360,9 @@
     shape = jax.ShapeDtypeStruct
     limit = pltpu.CompilerParams(vmem_limit_bytes=24 * 1024 * 1024)
 
+    p_shape = shape((3 * width // LANES, (height + 2) * PITCH + GROUP, LANES), F32)
+    out_shape = shape((2, width // LANES, rows * part, LANES), F32)
+
     swap = [(0, 1), (1, 0)]
     rowmajor = Layout((0, 1, 2))
     image_tokens = with_layout_constraint(image_tokens, rowmajor)
@@ -362,11 +371,10 @@
     def keep(array):
         return pltpu.with_memory_space_constraint(array, pltpu.HBM)
 
-    projected, strips, w_in_v, w_out_v, fwd_v, bwd_v, taps, spectrum, outer = pl.pallas_call(
+    projected, w_in_v, w_out_v, fwd_v, bwd_v, taps, spectrum, outer = pl.pallas_call(
         prep_kernel,
         out_shape=(
-            shape((2, height + 2, GROUP, 3 * width), F32),
-            shape((3 * rows, 3 * width), F32),
+            p_shape,
             shape(w_in.shape, BF16),
             shape(w_out.shape, BF16),
             shape(fwd.shape, BF16),
@@ -376,7 +384,7 @@
             shape((rows, width), BF16),
         ),
         in_specs=[hbm] * 10,
-        out_specs=(vmem,) * 9,
+        out_specs=(vmem,) * 8,
         scratch_shapes=[
             pltpu.VMEM(image_tokens.shape, BF16),
             pltpu.VMEM(spec.shape, BF16),
@@ -403,45 +411,36 @@
     for j in range(n_col - 1):
         pairs += [(n_col + j, j + 1), (j + 1, n_col + j)]
     halo = lax.ppermute(jnp.concatenate([outer, column(0)], 0), ("row", "col"), pairs)
-    other_strips = jnp.concatenate([column(GROUP - 1), column(GROUP), column(part)], 0)
     _, edge_mixed, inner = pl.pallas_call(
         inner_kernel,
-        out_shape=(
-            shape((2, height + 2, GROUP, 3 * width), F32),
-            shape((height, GROUP, 3 * width), F32),
-            shape((2, rows, GROUP, width), F32),
-        ),
-        in_specs=[vmem] * 10,
+        out_shape=(p_shape, shape((height, GROUP, 3 * width), F32), out_shape),
+        in_specs=[vmem] * 9,
         out_specs=(vmem,) * 3,
         input_output_aliases={0: 0},
         scratch_shapes=[
-            pltpu.VMEM((3 * rows, 3 * width), F32),
-            pltpu.VMEM((3, height + 16, 3 * width), F32),
-            pltpu.VMEM((2, height // 8, 8, 3 * width), F32),
-            pltpu.VMEM((2, height // 8, 8, 3 * width), F32),
             pltpu.VMEM((height, GROUP, 3 * width), F32),
             pltpu.VMEM((rows * GROUP, 2 * width), BF16),
             pltpu.VMEM((2 * rows * GROUP, 2 * width), BF16),
         ],
         compiler_params=limit,
         cost_estimate=pl.CostEstimate(flops=10**9, bytes_accessed=12 * 1024 * 1024, transcendentals=0),
-    )(projected, strips, other, other_strips, w_in_v, taps, fwd_v, bwd_v, w_out_v, spectrum)
+    )(projected, other, column(part), w_in_v, taps, fwd_v, bwd_v, w_out_v, spectrum)
     half_shape = shape((rows, part, width), BF16)
-    mine, send = pl.pallas_call(
+    _, mine, send = pl.pallas_call(
         edge_kernel,
-        out_shape=(half_shape, half_shape),
+        out_shape=(out_shape, half_shape, half_shape),
         in_specs=[vmem] * 9,
-        out_specs=(vmem, vmem),
+        out_specs=(vmem,) * 3,
+        input_output_aliases={0: 0},
         scratch_shapes=[
             pltpu.VMEM((height + 16, 3 * width), F32),
             pltpu.VMEM((height // 8, 8, 3 * width), F32),
             pltpu.VMEM((rows * GROUP, 2 * width), BF16),
             pltpu.VMEM((2 * rows * GROUP, 2 * width), BF16),
-            pltpu.VMEM((2, rows, GROUP, width), F32),
         ],
         compiler_params=limit,
         cost_estimate=pl.CostEstimate(flops=3 * 10**8, bytes_accessed=4 * 1024 * 1024, transcendentals=0),
-    )(halo, edge_mixed, inner, w_in_v, taps, fwd_v, bwd_v, w_out_v, spectrum)
+    )(inner, halo, edge_mixed, w_in_v, taps, fwd_v, bwd_v, w_out_v, spectrum)
     theirs = lax.ppermute(send, "row", swap)
     both = jnp.concatenate([mine, mine], 1)
     return lax.dynamic_update_slice_in_dim(both, theirs, (1 - core) * part, 1)

time: 14.4 us -> 14.1 us (0.979)
  Pallas kernels: 6.97 us -> 6.7 us
    pallas_call x3, Pallas kernels: 6.97 us -> 6.7 us  [the longest x1 3.34 us: on_device(): pl.pallas_call(inner_kernel, out_shape=(p_shape, shape((height, GROUP, 3...]
  transfers between devices with their start and end apart: 3 -> 3, of which waited for: 1 -> 1; matrix products, arithmetic and copies ran while one was open for 6% -> 6% of each run, Pallas kernels for 40% -> 38%
where the time goes in v7:
time: 14.1 us; the launch traced here: 13.9 us
  Pallas kernels  6.7 us (48%)
  starting transfers between devices  5.15 us (37%)
  other arithmetic  0.86 us (6%)
  local copies, waits for them, and re-layouts  0.83 us (6%)
  waiting for transfers between devices  0.33 us (2%)
    ppermute x1, starting transfers between devices, on_device(): theirs = lax.ppermute(send, 'row', swap)  4.04 us
    pallas_call x1, Pallas kernels, on_device(): pl.pallas_call(inner_kernel, out_shape=(p_shape, shape((height, GROUP, 3...  3.34 us
    pallas_call x1, Pallas kernels, on_device(): pl.pallas_call(prep_kernel, out_shape=(p_shape, shape(w_in.shape, BF16),...  1.98 us
    pallas_call x1, Pallas kernels, on_device(): pl.pallas_call(edge_kernel, out_shape=(out_shape, half_shape, half_shape)...  1.37 us
    concatenate x1, other arithmetic, on_device(): both = jnp.concatenate([mine, mine], 1)  0.83 us
    dynamic_update_slice x1, local copies, waits for them, and re-layouts, on_device(): return lax.dynamic_update_slice_in_dim(both, theirs, (1 - core) * part, 1)  0.72 us
    ppermute x1, starting transfers between devices, on_device(): lax.ppermute(jnp.concatenate([outer, column(0)], 0), ('row', 'col'), pairs)  0.66 us
    ppermute x1, starting transfers between devices, on_device(): lax.ppermute(image_tokens, 'row', swap)  0.45 us
  transfers between devices with their start and end apart: 3, of which 1 were waited for; matrix products, arithmetic and copies ran while one was open for 6% of the time, Pallas kernels for 38%

profile of v7, /device:TPU:0, one launch (start us, length us, event | category | flops | bytes accessed | tf_op | source)
XLA Modules:
  0.0 13.9 jit_solution(16658741214598248000)
XLA Ops:
  0.0 0.5 %collective-permute-start = (bf16[32,32,256]{2,1,0:T(8,128)(2,1)}, bf16[32,32,256]{2,1,0:T(8,128)(2,1)S(1)}, u32[]{:S(2)}, u32[]{:S(2)}) collective-permute-start(bf16[32,32,256]{2,1,0:T(8,128)(2,1)} %own_hbm), channel_id=1, source_target_pairs={{0,16},{16,0},{1,17},{17,1},{2,18},{18,2},{3,19},{19,3},{4,20},{20... | collective-permute-start | bytes 1572872 | tf_op jit(solution)/shard_map/ppermute | solution.py:369
  0.5 2.0 %shard_map.100 = (f32[6,1592,128]{2,1,0:T(8,128)S(1)}, bf16[256,768]{1,0:T(8,128)(2,1)S(1)}, bf16[256,256]{1,0:T(8,128)(2,1)S(1)}, bf16[512,256]{1,0:T(8,128)(2,...) custom-call(bf16[32,32,256]{2,1,0:T(8,128)(2,1)} %own_hbm, ...), custom_call_target="tpu_custom_call" | custom-call | bytes 3145728 | tf_op jit(solution)/shard_map/pallas_call | solution.py:374
  2.4 0.0 collective-permute-done.other_ref
  2.5 0.1 fusion.2
  2.6 0.7 %collective-permute-start.1 = (bf16[64,256]{1,0:T(8,128)(2,1)S(1)}, bf16[64,256]{1,0:T(8,128)(2,1)S(1)}, u32[]{:S(2)}, u32[]{:S(2)}) collective-permute-start(bf16[64,256]{1,0:T(8,128)(2,1)S(1)} %pad_maximum_fusion.1), channel_id=1, source_target_pairs={{16,1},{1,16},{17,2},{2,17},{18,3},{3,18},{19,4},{4,19},{20,5},{5,... | collective-permute-start | bytes 98312 | tf_op jit(solution)/shard_map/ppermute | solution.py:413
  3.3 3.3 %shard_map.101 = (f32[6,1592,128]{2,1,0:T(8,128)S(1)}, f32[64,8,768]{2,1,0:T(8,128)S(1)}, f32[2,2,512,128]{3,2,1,0:T(8,128)S(1)}) custom-call(f32[6,1592,128]{2,1,0:T(8,128)S(1)} %get-tuple-element.17._, bf16[32,32,256]{2,1,0:T(8,128)(2,1)S(1)} %collective-permute-done.other_ref, ...), custom_call_target="tpu_custom_call", output_to_operand_aliasing={{0}: (0, {})} | custom-call | flops 1000000000 | bytes 12582912 | tf_op jit(solution)/shard_map/pallas_call | solution.py:414
  6.6 0.0 collective-permute-done.1.halo_ref
  6.6 1.4 %shard_map.102 = (f32[2,2,512,128]{3,2,1,0:T(8,128)S(1)}, bf16[32,16,256]{2,1,0:T(8,128)(2,1)S(1)}, bf16[32,16,256]{2,1,0:T(8,128)(2,1)S(1)}) custom-call(f32[2,2,512,128]{3,2,1,0:T(8,128)S(1)} %get-tuple-element.24._, bf16[64,256]{1,0:T(8,128)(2,1)S(1)} %collective-permute-done.1.halo_ref, ...), custom_call_target="tpu_custom_call", output_to_operand_aliasing={{0}: (0, {})} | custom-call | flops 300000000 | bytes 4194304 | tf_op jit(solution)/shard_map/pallas_call | solution.py:429
  8.0 4.0 %collective-permute-start.2 = (bf16[32,16,256]{2,1,0:T(8,128)(2,1)S(1)}, bf16[32,16,256]{2,1,0:T(8,128)(2,1)S(1)}, u32[]{:S(2)}, u32[]{:S(2)}) collective-permute-start(bf16[32,16,256]{2,1,0:T(8,128)(2,1)S(1)} %get-tuple-element.28), channel_id=1, source_target_pairs={{0,16},{16,0},{1,17},{17,1},{2,18},{18,2},{3,19},{19,3},{4,20},{20... | collective-permute-start | bytes 786440 | tf_op jit(solution)/shard_map/ppermute | solution.py:444
  12.1 0.8 %pad_maximum_fusion = bf16[32,32,256]{2,1,0:T(8,128)(2,1)} fusion(bf16[32,16,256]{2,1,0:T(8,128)(2,1)S(1)} %get-tuple-element.27), kind=kLoop, calls=%fused_computation | loop fusion | flops 1048576 | bytes 786432 | tf_op jit(solution)/shard_map/concatenate | solution.py:445
  12.9 0.3 %collective-permute-done.2 = bf16[32,16,256]{2,1,0:T(8,128)(2,1)S(1)} collective-permute-done((bf16[32,16,256]{2,1,0:T(8,128)(2,1)S(1)}, bf16[32,16,256]{2,1,0:T(8,128)(2,1)S(1)}, u32[]{:S(2)}, u32[]{:S(2)}) %collective-permute-start.2) | collective-permute-done | bytes 262176 | tf_op jit(solution)/shard_map/ppermute | solution.py:444
  13.2 0.7 %constant_dynamic-update-slice_fusion = bf16[32,32,256]{2,1,0:T(8,128)(2,1)} fusion(bf16[32,32,256]{2,1,0:T(8,128)(2,1)} %pad_maximum_fusion, bf16[32,16,256]{2,1,0:T(8,128)(2,1)S(1)} %collective-permute-done.2, s32[]{:T(128)S(6)} %select_n.25), kind=kLoop, calls=%fused_computation.6 | loop fusion | bytes 524292 | tf_op jit(solution)/shard_map/dynamic_update_slice | solution.py:446
  (3 shorter events, 0.0 us)
Async XLA Ops:
  0.0 2.4 %collective-permute-start = (bf16[32,32,256]{2,1,0:T(8,128)(2,1)}, bf16[32,32,256]{2,1,0:T(8,128)(2,1)S(1)}, u32[]{:S(2)}, u32[]{:S(2)}) collective-permute-start(bf16[32,32,256]{2,1,0:T(8,128)(2,1)} %own_hbm), channel_id=1, source_target_pairs={{0,16},{16,0},{1,17},{17,1},{2,18},{18,2},{3,19},{19,3},{4,20},{20... | collective-permute-start | bytes 1572872 | tf_op jit(solution)/shard_map/ppermute | solution.py:369
  2.6 4.0 %collective-permute-start.1 = (bf16[64,256]{1,0:T(8,128)(2,1)S(1)}, bf16[64,256]{1,0:T(8,128)(2,1)S(1)}, u32[]{:S(2)}, u32[]{:S(2)}) collective-permute-start(bf16[64,256]{1,0:T(8,128)(2,1)S(1)} %pad_maximum_fusion.1), channel_id=1, source_target_pairs={{16,1},{1,16},{17,2},{2,17},{18,3},{3,18},{19,4},{4,19},{20,5},{5,... | collective-permute-start | bytes 98312 | tf_op jit(solution)/shard_map/ppermute | solution.py:413
  8.0 5.2 %collective-permute-start.2 = (bf16[32,16,256]{2,1,0:T(8,128)(2,1)S(1)}, bf16[32,16,256]{2,1,0:T(8,128)(2,1)S(1)}, u32[]{:S(2)}, u32[]{:S(2)}) collective-permute-start(bf16[32,16,256]{2,1,0:T(8,128)(2,1)S(1)} %get-tuple-element.28), channel_id=1, source_target_pairs={{0,16},{16,0},{1,17},{17,1},{2,18},{18,2},{3,19},{19,3},{4,20},{20... | collective-permute-start | bytes 786440 | tf_op jit(solution)/shard_map/ppermute | solution.py:444

commit v8 on v7

--- a/solution.py
+++ b/solution.py
@@ -64,7 +64,7 @@
     return row * PITCH + FIRST + column
 
 
-def project(tokens, strip, core, row, w_in_ref, p_ref):
+def project(tokens, strip, core, w_in_ref, p_ref):
     rows, part, width = tokens.shape
     count = rows * part
     got = jnp.dot(
@@ -74,17 +74,34 @@
     )
     for t in range(3 * width // LANES):
         at = slice(t * LANES, (t + 1) * LANES)
+        for row in (0, rows + 1):
+            place = row * PITCH
+            p_ref[t, place : place + PITCH + GROUP, :] = jnp.zeros((PITCH + GROUP, LANES), F32)
         for r in range(rows):
-            place = pl.multiple_of(row_place(row + r + 1, 0), GROUP)
-            p_ref[t, pl.ds(place, part), :] = got[r * part : (r + 1) * part, at]
+            place = row_place(r + 1, 0)
+            p_ref[t, place : place + part, :] = got[r * part : (r + 1) * part, at]
         for r in range(0, rows, GROUP):
             beside = got[count + r : count + r + GROUP, at]
             for column, value in (
                 (-1, jnp.where(core == 1, beside, 0.0)),
                 (part, jnp.where(core == 0, beside, 0.0)),
             ):
-                place = row_place(row + r + 1, column)
+                place = row_place(r + 1, column)
                 p_ref[t, pl.ds(place, GROUP, stride=PITCH), :] = value
+
+
+def copy_row(from_ref, from_row, to_ref, to_row, part):
+    sub = lax.broadcasted_iota(jnp.int32, (GROUP, LANES), 0)
+    for t in range(from_ref.shape[0]):
+        for place in range(0, FIRST + part + GROUP, GROUP):
+            source = pl.ds(pl.multiple_of(from_row * PITCH + place, GROUP), GROUP)
+            target = pl.ds(pl.multiple_of(to_row * PITCH + place, GROUP), GROUP)
+            value = from_ref[t, source, :]
+            if place < FIRST:
+                value = jnp.where(sub == GROUP - 1, value, to_ref[t, target, :])
+            elif place >= FIRST + part:
+                value = jnp.where(sub == 0, value, to_ref[t, target, :])
+            to_ref[t, target, :] = value
 
 
 def prep_kernel(
@@ -95,15 +112,14 @@
     core = lax.axis_index("row")
     rows, cols, width = own_ref.shape
     part = cols // 2
-    height = 2 * rows
     moves = [
+        (own_hbm, own_ref),
+        (w_in_hbm, w_in_ref),
         (spec_hbm, spec_ref),
         (filt_hbm, filt_ref),
         (gain_hbm, gain_ref),
-        (own_hbm, own_ref),
         (kernel_hbm, kernel_ref),
         (bias_hbm, bias_ref),
-        (w_in_hbm, w_in_ref),
         (fwd_hbm, fwd_ref),
         (bwd_hbm, bwd_ref),
         (w_out_hbm, w_out_ref),
@@ -111,27 +127,23 @@
     copies = [pltpu.make_async_copy(src, dst, sems.at[i]) for i, (src, dst) in enumerate(moves)]
     for copy in copies:
         copy.start()
-    for copy in copies[:3]:
-        copy.wait()
-    filt = filt_ref[...]
-    h_ref[...] = jnp.dot(spec_ref[0], filt, preferred_element_type=F32) + jnp.dot(
-        spec_ref[1], filt, preferred_element_type=F32
-    )
-    gain = gain_ref[...]
-    h_ref[0:rows, :] = h_ref[0:rows, :] + gain
-    h_ref[2 * rows : 3 * rows, :] = h_ref[2 * rows : 3 * rows, :] + gain
-    for t in range(p_ref.shape[0]):
-        for row in (0, height + 1):
-            p_ref[t, row * PITCH : row * PITCH + PITCH + GROUP, :] = jnp.zeros((PITCH + GROUP, LANES), F32)
-    copies[3].wait()
+    copies[0].wait()
     start = pl.multiple_of(core * part, part)
     far = pl.multiple_of((1 - core) * part, part)
     inner_edge = core * (part - 1)
     outer_ref[...] = pick_column(own_ref[:, pl.ds(start, part), :], inner_edge)
     beside = pick_column(own_ref[:, pl.ds(far, part), :], inner_edge)
-    for copy in copies[4:7]:
+    for copy in copies[1:7]:
         copy.wait()
-    project(own_ref[:, pl.ds(start, part), :], beside, core, core * rows, w_in_ref, p_ref)
+    project(own_ref[:, pl.ds(start, part), :], beside, core, w_in_ref, p_ref)
+    filt = filt_ref[...]
+    gain = gain_ref[...]
+    spectrum = jnp.dot(spec_ref[0], filt, preferred_element_type=F32) + jnp.dot(
+        spec_ref[1], filt, preferred_element_type=F32
+    )
+    for j in range(6):
+        part_j = spectrum[j * rows : (j + 1) * rows]
+        h_ref[j * rows : (j + 1) * rows, :] = part_j + gain if j in (0, 2) else part_j
     for a in range(3):
         taps_ref[3 * a : 3 * a + 3, :] = kernel_ref[a].astype(F32)
     taps_ref[9, :] = bias_ref[...]
@@ -139,17 +151,21 @@
         copy.wait()
 
 
-def edge_terms(first, second, core, taps, edge_ref):
+def edge_terms(first, second, core, taps, edge_ref, side_ref):
     rows, channels = first.shape
-    height = 2 * rows
-    edge_ref[0:8, :] = jnp.zeros((8, channels), F32)
-    edge_ref[8 + height : 16 + height, :] = jnp.zeros((8, channels), F32)
-    edge_ref[pl.ds(pl.multiple_of(8 + core * rows, 8), rows), :] = first
-    edge_ref[pl.ds(pl.multiple_of(8 + (1 - core) * rows, 8), rows), :] = second
-    total = edge_ref[7 : 7 + height, :] * taps[0]
-    for a in (1, 2):
-        total = total + edge_ref[7 + a : 7 + a + height, :] * taps[a]
-    return total.reshape(height // 8, 8, channels)
+    for t in range(channels // LANES):
+        at = slice(t * LANES, (t + 1) * LANES)
+        edge_ref[t, 0:8, :] = jnp.zeros((8, LANES), F32)
+        edge_ref[t, 4 * rows : 4 * rows + 8, :] = jnp.zeros((8, LANES), F32)
+        for r in range(0, rows, 8):
+            for row, half in ((core * rows, first), ((1 - core) * rows, second)):
+                place = pl.ds(2 * (row + r + 1), 8, stride=2)
+                edge_ref[t, place, :] = half[r : r + 8, at]
+        for r in range(0, 2 * rows, 8):
+            total = edge_ref[t, pl.ds(2 * r, 8, stride=2), :] * taps[0][:, at]
+            for a in (1, 2):
+                total = total + edge_ref[t, pl.ds(2 * (r + a), 8, stride=2), :] * taps[a][:, at]
+            side_ref[r // 8, :, at] = total
 
 
 def column_taps(taps_ref, core, on_core0):
@@ -261,55 +277,64 @@
     _, other_ref, other_strip_ref,
     w_in_ref, taps_ref, fwd_ref, bwd_ref, w_out_ref, h_ref,
     p_ref, edge_mixed_ref, out_ref,
-    mixed_ref, prod_ref, z_ref,
+    q_ref, mixed_ref, prod_ref, z_ref,
 ):
     core = lax.axis_index("row")
     rows, cols, width = other_ref.shape
     part = cols // 2
     height = 2 * rows
     start = pl.multiple_of(core * part, part)
-    project(
-        other_ref[:, pl.ds(start, part), :], other_strip_ref[...],
-        core, (1 - core) * rows, w_in_ref, p_ref,
-    )
-
-    def store_inner(row, at, value):
-        mixed_ref[row, :, at] = value
+    channels = range(0, 3 * width, LANES)
+    n_chunk = rows // CHUNK
+
+    def store_in(ref, row0):
+        def store(row, at, value):
+            ref[row0 + row, :, at] = value
+
+        return store
+
+    own_at, other_at = core * rows, (1 - core) * rows
+
+    def inner(ref, row0, chunk):
+        return depthwise_steps(ref, 1 - core, taps_ref, chunk, store_in(mixed_ref, row0), channels)
+
+    def edge(ref, row0, chunk):
+        return depthwise_steps(ref, core, taps_ref, chunk, store_in(edge_mixed_ref, row0), channels)
+
+    for i in range(n_chunk - 1):
+        for _ in inner(p_ref, own_at, core + i):
+            pass
+    project(other_ref[:, pl.ds(start, part), :], other_strip_ref[...], core, w_in_ref, q_ref)
+    copy_row(q_ref, 1 + core * (rows - 1), p_ref, (1 - core) * (rows + 1), part)
+    copy_row(p_ref, rows - core * (rows - 1), q_ref, core * (rows + 1), part)
+    for _ in inner(p_ref, own_at, (1 - core) * (n_chunk - 1)):
+        pass
 
     def inner_chunk(i, carry):
-        steps = depthwise_steps(
-            p_ref, 1 - core, taps_ref, i, store_inner, range(0, 3 * width, LANES)
-        )
-        for _ in steps:
+        for _ in inner(q_ref, other_at, i):
             pass
         return carry
 
-    lax.fori_loop(0, height // CHUNK, inner_chunk, 0)
-
-    def store_edge(row, at, value):
-        edge_mixed_ref[row, :, at] = value
+    lax.fori_loop(0, n_chunk, inner_chunk, 0)
 
     def put(final):
         interleave(out_ref, final, 1 - core)
 
-    edge = [
-        depthwise_steps(p_ref, core, taps_ref, i, store_edge, [base])
-        for i in range(height // CHUNK)
-        for base in range(0, 3 * width, LANES)
-    ]
+    def edge_all():
+        for ref, row0 in ((p_ref, own_at), (q_ref, other_at)):
+            for i in range(n_chunk):
+                yield from edge(ref, row0, i)
+
+    steps = edge_all()
     conv = conv_steps(
         lambda r, base: mixed_ref[r, :, base : base + LANES],
         fwd_ref, bwd_ref, w_out_ref, h_ref, prod_ref, z_ref, put,
     )
-    done = 0
     for _ in conv:
-        for step in edge[done : done + 2]:
-            for _ in step:
-                pass
-        done += 2
-    for step in edge[done:]:
-        for _ in step:
-            pass
+        for _ in range(2):
+            next(steps, None)
+    for _ in steps:
+        pass
 
 
 def edge_kernel(
@@ -320,8 +345,8 @@
     core = lax.axis_index("row")
     rows, part, width = mine_ref.shape
     got = jnp.dot(halo_ref[...], w_in_ref[...], preferred_element_type=F32)
-    side_ref[...] = edge_terms(
-        got[:rows], got[rows:], 1 - core, column_taps(taps_ref, core, 0), strip_ref
+    edge_terms(
+        got[:rows], got[rows:], 1 - core, column_taps(taps_ref, core, 0), strip_ref, side_ref
     )
     sub = lax.broadcasted_iota(jnp.int32, (GROUP, LANES), 0)
     at_edge = sub == core * (GROUP - 1)
@@ -360,7 +385,7 @@
     shape = jax.ShapeDtypeStruct
     limit = pltpu.CompilerParams(vmem_limit_bytes=24 * 1024 * 1024)
 
-    p_shape = shape((3 * width // LANES, (height + 2) * PITCH + GROUP, LANES), F32)
+    p_shape = shape((3 * width // LANES, (rows + 2) * PITCH + GROUP, LANES), F32)
     out_shape = shape((2, width // LANES, rows * part, LANES), F32)
 
     swap = [(0, 1), (1, 0)]
@@ -418,6 +443,7 @@
         out_specs=(vmem,) * 3,
         input_output_aliases={0: 0},
         scratch_shapes=[
+            pltpu.VMEM(p_shape.shape, F32),
             pltpu.VMEM((height, GROUP, 3 * width), F32),
             pltpu.VMEM((rows * GROUP, 2 * width), BF16),
             pltpu.VMEM((2 * rows * GROUP, 2 * width), BF16),
@@ -433,7 +459,7 @@
         out_specs=(vmem,) * 3,
         input_output_aliases={0: 0},
         scratch_shapes=[
-            pltpu.VMEM((height + 16, 3 * width), F32),
+            pltpu.VMEM((3 * width // LANES, 2 * height + 8, LANES), F32),
             pltpu.VMEM((height // 8, 8, 3 * width), F32),
             pltpu.VMEM((rows * GROUP, 2 * width), BF16),
             pltpu.VMEM((2 * rows * GROUP, 2 * width), BF16),

time: 14.1 us -> 13.9 us (0.986)
  Pallas kernels: 6.7 us -> 6.33 us
  starting transfers between devices: 5.15 us -> 5.34 us
    pallas_call x1, Pallas kernels: 1.98 us -> 1.79 us  [on_device(): pl.pallas_call(prep_kernel, out_shape=(p_shape, shape(w_in.shape, BF16),...]
    ppermute x1, starting transfers between devices: 4.04 us -> 4.22 us  [on_device(): theirs = lax.ppermute(send, 'row', swap)]
    pallas_call x1, Pallas kernels: 3.34 us -> 3.16 us  [on_device(): pl.pallas_call(inner_kernel, out_shape=(p_shape, shape((height, GROUP, 3...]
  transfers between devices with their start and end apart: 3 -> 3, of which waited for: 1 -> 1; matrix products, arithmetic and copies ran while one was open for 6% -> 6% of each run, Pallas kernels for 38% -> 36%
where the time goes in v8:
time: 13.9 us; the launch traced here: 13.8 us
  Pallas kernels  6.33 us (46%)
  starting transfers between devices  5.34 us (38%)
  other arithmetic  0.86 us (6%)
  local copies, waits for them, and re-layouts  0.83 us (6%)
  waiting for transfers between devices  0.33 us (2%)
    ppermute x1, starting transfers between devices, on_device(): theirs = lax.ppermute(send, 'row', swap)  4.22 us
    pallas_call x1, Pallas kernels, on_device(): pl.pallas_call(inner_kernel, out_shape=(p_shape, shape((height, GROUP, 3...  3.16 us
    pallas_call x1, Pallas kernels, on_device(): pl.pallas_call(prep_kernel, out_shape=(p_shape, shape(w_in.shape, BF16),...  1.79 us
    pallas_call x1, Pallas kernels, on_device(): pl.pallas_call(edge_kernel, out_shape=(out_shape, half_shape, half_shape)...  1.37 us
    concatenate x1, other arithmetic, on_device(): both = jnp.concatenate([mine, mine], 1)  0.83 us
    dynamic_update_slice x1, local copies, waits for them, and re-layouts, on_device(): return lax.dynamic_update_slice_in_dim(both, theirs, (1 - core) * part, 1)  0.72 us
    ppermute x1, starting transfers between devices, on_device(): lax.ppermute(jnp.concatenate([outer, column(0)], 0), ('row', 'col'), pairs)  0.66 us
    ppermute x1, starting transfers between devices, on_device(): lax.ppermute(image_tokens, 'row', swap)  0.45 us
  transfers between devices with their start and end apart: 3, of which 1 were waited for; matrix products, arithmetic and copies ran while one was open for 6% of the time, Pallas kernels for 36%

profile of v8, /device:TPU:0, one launch (start us, length us, event | category | flops | bytes accessed | tf_op | source)
XLA Modules:
  0.0 13.8 jit_solution(11358613509081847659)
XLA Ops:
  0.0 0.5 %collective-permute-start = (bf16[32,32,256]{2,1,0:T(8,128)(2,1)}, bf16[32,32,256]{2,1,0:T(8,128)(2,1)S(1)}, u32[]{:S(2)}, u32[]{:S(2)}) collective-permute-start(bf16[32,32,256]{2,1,0:T(8,128)(2,1)} %own_hbm), channel_id=1, source_target_pairs={{0,16},{16,0},{1,17},{17,1},{2,18},{18,2},{3,19},{19,3},{4,20},{20... | collective-permute-start | bytes 1572872 | tf_op jit(solution)/shard_map/ppermute | solution.py:394
  0.5 1.8 %shard_map.100 = (f32[6,824,128]{2,1,0:T(8,128)S(1)}, bf16[256,768]{1,0:T(8,128)(2,1)S(1)}, bf16[256,256]{1,0:T(8,128)(2,1)S(1)}, bf16[512,256]{1,0:T(8,128)(2,1...) custom-call(bf16[32,32,256]{2,1,0:T(8,128)(2,1)} %own_hbm, ...), custom_call_target="tpu_custom_call" | custom-call | bytes 3145728 | tf_op jit(solution)/shard_map/pallas_call | solution.py:399
  2.3 0.0 collective-permute-done.other_ref
  2.3 0.1 fusion.2
  2.4 0.7 %collective-permute-start.1 = (bf16[64,256]{1,0:T(8,128)(2,1)S(1)}, bf16[64,256]{1,0:T(8,128)(2,1)S(1)}, u32[]{:S(2)}, u32[]{:S(2)}) collective-permute-start(bf16[64,256]{1,0:T(8,128)(2,1)S(1)} %pad_maximum_fusion.1), channel_id=1, source_target_pairs={{16,1},{1,16},{17,2},{2,17},{18,3},{3,18},{19,4},{4,19},{20,5},{5,... | collective-permute-start | bytes 98312 | tf_op jit(solution)/shard_map/ppermute | solution.py:438
  3.1 3.2 %shard_map.101 = (f32[6,824,128]{2,1,0:T(8,128)S(1)}, f32[64,8,768]{2,1,0:T(8,128)S(1)}, f32[2,2,512,128]{3,2,1,0:T(8,128)S(1)}) custom-call(f32[6,824,128]{2,1,0:T(8,128)S(1)} %get-tuple-element.17._, bf16[32,32,256]{2,1,0:T(8,128)(2,1)S(1)} %collective-permute-done.other_ref, ...), custom_call_target="tpu_custom_call", output_to_operand_aliasing={{0}: (0, {})} | custom-call | flops 1000000000 | bytes 12582912 | tf_op jit(solution)/shard_map/pallas_call | solution.py:439
  6.3 0.0 collective-permute-done.1.halo_ref
  6.3 1.4 %shard_map.102 = (f32[2,2,512,128]{3,2,1,0:T(8,128)S(1)}, bf16[32,16,256]{2,1,0:T(8,128)(2,1)S(1)}, bf16[32,16,256]{2,1,0:T(8,128)(2,1)S(1)}) custom-call(f32[2,2,512,128]{3,2,1,0:T(8,128)S(1)} %get-tuple-element.24._, bf16[64,256]{1,0:T(8,128)(2,1)S(1)} %collective-permute-done.1.halo_ref, ...), custom_call_target="tpu_custom_call", output_to_operand_aliasing={{0}: (0, {})} | custom-call | flops 300000000 | bytes 4194304 | tf_op jit(solution)/shard_map/pallas_call | solution.py:455
  7.7 4.2 %collective-permute-start.2 = (bf16[32,16,256]{2,1,0:T(8,128)(2,1)S(1)}, bf16[32,16,256]{2,1,0:T(8,128)(2,1)S(1)}, u32[]{:S(2)}, u32[]{:S(2)}) collective-permute-start(bf16[32,16,256]{2,1,0:T(8,128)(2,1)S(1)} %get-tuple-element.28), channel_id=1, source_target_pairs={{0,16},{16,0},{1,17},{17,1},{2,18},{18,2},{3,19},{19,3},{4,20},{20... | collective-permute-start | bytes 786440 | tf_op jit(solution)/shard_map/ppermute | solution.py:470
  11.9 0.8 %pad_maximum_fusion = bf16[32,32,256]{2,1,0:T(8,128)(2,1)} fusion(bf16[32,16,256]{2,1,0:T(8,128)(2,1)S(1)} %get-tuple-element.27), kind=kLoop, calls=%fused_computation | loop fusion | flops 1048576 | bytes 786432 | tf_op jit(solution)/shard_map/concatenate | solution.py:471
  12.7 0.3 %collective-permute-done.2 = bf16[32,16,256]{2,1,0:T(8,128)(2,1)S(1)} collective-permute-done((bf16[32,16,256]{2,1,0:T(8,128)(2,1)S(1)}, bf16[32,16,256]{2,1,0:T(8,128)(2,1)S(1)}, u32[]{:S(2)}, u32[]{:S(2)}) %collective-permute-start.2) | collective-permute-done | bytes 262176 | tf_op jit(solution)/shard_map/ppermute | solution.py:470
  13.0 0.7 %constant_dynamic-update-slice_fusion = bf16[32,32,256]{2,1,0:T(8,128)(2,1)} fusion(bf16[32,32,256]{2,1,0:T(8,128)(2,1)} %pad_maximum_fusion, bf16[32,16,256]{2,1,0:T(8,128)(2,1)S(1)} %collective-permute-done.2, s32[]{:T(128)S(6)} %select_n.25), kind=kLoop, calls=%fused_computation.6 | loop fusion | bytes 524292 | tf_op jit(solution)/shard_map/dynamic_update_slice | solution.py:472
  (3 shorter events, 0.0 us)
Async XLA Ops:
  0.0 2.3 %collective-permute-start = (bf16[32,32,256]{2,1,0:T(8,128)(2,1)}, bf16[32,32,256]{2,1,0:T(8,128)(2,1)S(1)}, u32[]{:S(2)}, u32[]{:S(2)}) collective-permute-start(bf16[32,32,256]{2,1,0:T(8,128)(2,1)} %own_hbm), channel_id=1, source_target_pairs={{0,16},{16,0},{1,17},{17,1},{2,18},{18,2},{3,19},{19,3},{4,20},{20... | collective-permute-start | bytes 1572872 | tf_op jit(solution)/shard_map/ppermute | solution.py:394
  2.4 3.9 %collective-permute-start.1 = (bf16[64,256]{1,0:T(8,128)(2,1)S(1)}, bf16[64,256]{1,0:T(8,128)(2,1)S(1)}, u32[]{:S(2)}, u32[]{:S(2)}) collective-permute-start(bf16[64,256]{1,0:T(8,128)(2,1)S(1)} %pad_maximum_fusion.1), channel_id=1, source_target_pairs={{16,1},{1,16},{17,2},{2,17},{18,3},{3,18},{19,4},{4,19},{20,5},{5,... | collective-permute-start | bytes 98312 | tf_op jit(solution)/shard_map/ppermute | solution.py:438
  7.7 5.4 %collective-permute-start.2 = (bf16[32,16,256]{2,1,0:T(8,128)(2,1)S(1)}, bf16[32,16,256]{2,1,0:T(8,128)(2,1)S(1)}, u32[]{:S(2)}, u32[]{:S(2)}) collective-permute-start(bf16[32,16,256]{2,1,0:T(8,128)(2,1)S(1)} %get-tuple-element.28), channel_id=1, source_target_pairs={{0,16},{16,0},{1,17},{17,1},{2,18},{18,2},{3,19},{19,3},{4,20},{20... | collective-permute-start | bytes 786440 | tf_op jit(solution)/shard_map/ppermute | solution.py:470

commit v9 on v8

--- a/solution.py
+++ b/solution.py
@@ -43,7 +43,7 @@
 
 LANES = 128
 GROUP = 8
-CHUNK = 8
+CHUNK = 16
 PITCH = 24
 FIRST = 8
 
@@ -67,11 +67,8 @@
 def project(tokens, strip, core, w_in_ref, p_ref):
     rows, part, width = tokens.shape
     count = rows * part
-    got = jnp.dot(
-        jnp.concatenate([tokens.reshape(count, width), strip], 0),
-        w_in_ref[...],
-        preferred_element_type=F32,
-    )
+    got = jnp.dot(tokens.reshape(count, width), w_in_ref[...], preferred_element_type=F32)
+    got_strip = jnp.dot(strip, w_in_ref[...], preferred_element_type=F32)
     for t in range(3 * width // LANES):
         at = slice(t * LANES, (t + 1) * LANES)
         for row in (0, rows + 1):
@@ -81,7 +78,7 @@
             place = row_place(r + 1, 0)
             p_ref[t, place : place + part, :] = got[r * part : (r + 1) * part, at]
         for r in range(0, rows, GROUP):
-            beside = got[count + r : count + r + GROUP, at]
+            beside = got_strip[r : r + GROUP, at]
             for column, value in (
                 (-1, jnp.where(core == 1, beside, 0.0)),
                 (part, jnp.where(core == 0, beside, 0.0)),
@@ -219,57 +216,72 @@
 
 
 def conv_steps(mixed, fwd_ref, bwd_ref, w_out_ref, h_ref, prod_ref, z_ref, put):
-    block, width = prod_ref.shape[0], prod_ref.shape[1] // 2
+    streams, block, _ = prod_ref.shape
     rows = block // GROUP
-    for row in range(0, rows, 2):
-        for h in range(2):
-            for base in range(0, width, LANES):
+    width = streams * LANES
+
+    def products(n):
+        base = n * LANES
+        for row in range(0, rows, 2):
+            for h in range(2):
                 two = [
                     mixed(h * rows + r, width + base) * mixed(h * rows + r, 2 * width + base)
                     for r in (row, row + 1)
                 ]
-                at = h * width + base
-                prod_ref[row * GROUP : (row + 2) * GROUP, at : at + LANES] = jnp.concatenate(
-                    two, 0
+                prod_ref[n, row * GROUP : (row + 2) * GROUP, h * LANES : (h + 1) * LANES] = (
+                    jnp.concatenate(two, 0).astype(BF16)
+                )
+        return jnp.dot(fwd_ref[...], prod_ref[n], preferred_element_type=F32)
+
+    def filtered(n, spectra):
+        base = n * LANES
+        low, high = spectra[:, :LANES], spectra[:, LANES:]
+        for k in range(0, rows, 2):
+            parts = [[], [], [], []]
+            for s in (k, k + 1):
+                near_r, near_i, near_2, all_r, all_i, all_2 = (
+                    jnp.broadcast_to(
+                        h_ref[j * rows + s : j * rows + s + 1, base : base + LANES], (GROUP, LANES)
+                    )
+                    for j in range(6)
+                )
+                re = slice(s * GROUP, (s + 1) * GROUP)
+                im = slice(block + s * GROUP, block + (s + 1) * GROUP)
+                lr, li, hr, hi = low[re], low[im], high[re], high[im]
+                parts[0].append(lr * near_r - li * near_i)
+                parts[1].append(lr * near_i + li * near_2)
+                parts[2].append(lr * all_r - li * all_i + hr * near_r - hi * near_i)
+                parts[3].append(lr * all_i + li * all_2 + hr * near_i + hi * near_2)
+            for j in range(4):
+                at, lane = (j % 2) * block + k * GROUP, (j // 2) * LANES
+                z_ref[n, at : at + 2 * GROUP, lane : lane + LANES] = jnp.concatenate(
+                    parts[j], 0
                 ).astype(BF16)
-        if row % 4 == 2:
-            yield
-    spectra = jnp.dot(fwd_ref[...], prod_ref[...], preferred_element_type=F32)
-    low, high = spectra[:, :width], spectra[:, width:]
-    yield
-    for k in range(0, rows, 2):
-        parts = [[], [], [], []]
-        for s in (k, k + 1):
-            near_r, near_i, near_2, all_r, all_i, all_2 = (
-                jnp.broadcast_to(h_ref[j * rows + s : j * rows + s + 1, :], (GROUP, width))
-                for j in range(6)
-            )
-            re, im = slice(s * GROUP, (s + 1) * GROUP), slice(block + s * GROUP, block + (s + 1) * GROUP)
-            lr, li, hr, hi = low[re], low[im], high[re], high[im]
-            parts[0].append(lr * near_r - li * near_i)
-            parts[1].append(lr * near_i + li * near_2)
-            parts[2].append(lr * all_r - li * all_i + hr * near_r - hi * near_i)
-            parts[3].append(lr * all_i + li * all_2 + hr * near_i + hi * near_2)
-        for j in range(4):
-            at, lane = (j % 2) * block + k * GROUP, (j // 2) * width
-            z_ref[at : at + 2 * GROUP, lane : lane + width] = jnp.concatenate(parts[j], 0).astype(BF16)
-        if k % 4 == 2:
-            yield
-    conv = jnp.dot(bwd_ref[...], z_ref[...], preferred_element_type=F32)
-    yield
-    gated = []
-    for h in range(2):
-        for r in range(rows):
-            line = [
-                mixed(h * rows + r, base)
-                * conv[r * GROUP : (r + 1) * GROUP, h * width + base : h * width + base + LANES]
-                for base in range(0, width, LANES)
-            ]
-            gated.append(jnp.concatenate(line, 1))
+        return jnp.dot(bwd_ref[...], z_ref[n], preferred_element_type=F32)
+
+    def gated(n, conv):
+        line = [
+            mixed(h * rows + r, n * LANES)
+            * conv[r * GROUP : (r + 1) * GROUP, h * LANES : (h + 1) * LANES]
+            for h in range(2)
+            for r in range(rows)
+        ]
+        return jnp.concatenate(line, 0).astype(BF16)
+
+    spectra = []
+    for n in range(streams):
+        spectra.append(products(n))
+        yield
+    convs = []
+    for n in range(streams):
+        convs.append(filtered(n, spectra[n]))
         yield
     final = jnp.dot(
-        jnp.concatenate(gated, 0).astype(BF16), w_out_ref[...], preferred_element_type=F32
-    )
+        jnp.concatenate([gated(n, convs[n]) for n in range(streams)], 1),
+        w_out_ref[...],
+        preferred_element_type=F32,
+    )
+    yield
     put(final.reshape(2, rows, GROUP, width))
 
 
@@ -331,7 +343,7 @@
         fwd_ref, bwd_ref, w_out_ref, h_ref, prod_ref, z_ref, put,
     )
     for _ in conv:
-        for _ in range(2):
+        for _ in range(5):
             next(steps, None)
     for _ in steps:
         pass
@@ -445,8 +457,8 @@
         scratch_shapes=[
             pltpu.VMEM(p_shape.shape, F32),
             pltpu.VMEM((height, GROUP, 3 * width), F32),
-            pltpu.VMEM((rows * GROUP, 2 * width), BF16),
-            pltpu.VMEM((2 * rows * GROUP, 2 * width), BF16),
+            pltpu.VMEM((width // LANES, rows * GROUP, 2 * LANES), BF16),
+            pltpu.VMEM((width // LANES, 2 * rows * GROUP, 2 * LANES), BF16),
         ],
         compiler_params=limit,
         cost_estimate=pl.CostEstimate(flops=10**9, bytes_accessed=12 * 1024 * 1024, transcendentals=0),
@@ -461,8 +473,8 @@
         scratch_shapes=[
             pltpu.VMEM((3 * width // LANES, 2 * height + 8, LANES), F32),
             pltpu.VMEM((height // 8, 8, 3 * width), F32),
-            pltpu.VMEM((rows * GROUP, 2 * width), BF16),
-            pltpu.VMEM((2 * rows * GROUP, 2 * width), BF16),
+            pltpu.VMEM((width // LANES, rows * GROUP, 2 * LANES), BF16),
+            pltpu.VMEM((width // LANES, 2 * rows * GROUP, 2 * LANES), BF16),
         ],
         compiler_params=limit,
         cost_estimate=pl.CostEstimate(flops=3 * 10**8, bytes_accessed=4 * 1024 * 1024, transcendentals=0),

time: 13.9 us -> 13.8 us (level)
    pallas_call x1, Pallas kernels: 3.16 us -> 3.02 us  [on_device(): pl.pallas_call(inner_kernel, out_shape=(p_shape, shape((height, GROUP, 3...]
  transfers between devices with their start and end apart: 3 -> 3, of which waited for: 1 -> 1; matrix products, arithmetic and copies ran while one was open for 6% -> 6% of each run, Pallas kernels for 36% -> 35%
where the time goes in v9:
time: 13.8 us; the launch traced here: 13.7 us
  Pallas kernels  6.26 us (45%)
  starting transfers between devices  5.34 us (39%)
  other arithmetic  0.86 us (6%)
  local copies, waits for them, and re-layouts  0.83 us (6%)
  waiting for transfers between devices  0.33 us (2%)
    ppermute x1, starting transfers between devices, on_device(): theirs = lax.ppermute(send, 'row', swap)  4.22 us
    pallas_call x1, Pallas kernels, on_device(): pl.pallas_call(inner_kernel, out_shape=(p_shape, shape((height, GROUP, 3...  3.02 us
    pallas_call x1, Pallas kernels, on_device(): pl.pallas_call(prep_kernel, out_shape=(p_shape, shape(w_in.shape, BF16),...  1.81 us
    pallas_call x1, Pallas kernels, on_device(): pl.pallas_call(edge_kernel, out_shape=(out_shape, half_shape, half_shape)...  1.43 us
    concatenate x1, other arithmetic, on_device(): both = jnp.concatenate([mine, mine], 1)  0.83 us
    dynamic_update_slice x1, local copies, waits for them, and re-layouts, on_device(): return lax.dynamic_update_slice_in_dim(both, theirs, (1 - core) * part, 1)  0.72 us
    ppermute x1, starting transfers between devices, on_device(): lax.ppermute(jnp.concatenate([outer, column(0)], 0), ('row', 'col'), pairs)  0.66 us
    ppermute x1, starting transfers between devices, on_device(): lax.ppermute(image_tokens, 'row', swap)  0.45 us
  transfers between devices with their start and end apart: 3, of which 1 were waited for; matrix products, arithmetic and copies ran while one was open for 6% of the time, Pallas kernels for 35%

profile of v9, /device:TPU:0, one launch (start us, length us, event | category | flops | bytes accessed | tf_op | source)
XLA Modules:
  0.0 13.7 jit_solution(7063597893739277654)
XLA Ops:
  0.0 0.5 %collective-permute-start = (bf16[32,32,256]{2,1,0:T(8,128)(2,1)}, bf16[32,32,256]{2,1,0:T(8,128)(2,1)S(1)}, u32[]{:S(2)}, u32[]{:S(2)}) collective-permute-start(bf16[32,32,256]{2,1,0:T(8,128)(2,1)} %own_hbm), channel_id=1, source_target_pairs={{0,16},{16,0},{1,17},{17,1},{2,18},{18,2},{3,19},{19,3},{4,20},{20... | collective-permute-start | bytes 1572872 | tf_op jit(solution)/shard_map/ppermute | solution.py:406
  0.5 1.8 %shard_map.100 = (f32[6,824,128]{2,1,0:T(8,128)S(1)}, bf16[256,768]{1,0:T(8,128)(2,1)S(1)}, bf16[256,256]{1,0:T(8,128)(2,1)S(1)}, bf16[512,256]{1,0:T(8,128)(2,1...) custom-call(bf16[32,32,256]{2,1,0:T(8,128)(2,1)} %own_hbm, ...), custom_call_target="tpu_custom_call" | custom-call | bytes 3145728 | tf_op jit(solution)/shard_map/pallas_call | solution.py:411
  2.3 0.0 collective-permute-done.other_ref
  2.3 0.1 fusion.2
  2.4 0.7 %collective-permute-start.1 = (bf16[64,256]{1,0:T(8,128)(2,1)S(1)}, bf16[64,256]{1,0:T(8,128)(2,1)S(1)}, u32[]{:S(2)}, u32[]{:S(2)}) collective-permute-start(bf16[64,256]{1,0:T(8,128)(2,1)S(1)} %pad_maximum_fusion.1), channel_id=1, source_target_pairs={{16,1},{1,16},{17,2},{2,17},{18,3},{3,18},{19,4},{4,19},{20,5},{5,... | collective-permute-start | bytes 98312 | tf_op jit(solution)/shard_map/ppermute | solution.py:450
  3.1 3.0 %shard_map.101 = (f32[6,824,128]{2,1,0:T(8,128)S(1)}, f32[64,8,768]{2,1,0:T(8,128)S(1)}, f32[2,2,512,128]{3,2,1,0:T(8,128)S(1)}) custom-call(f32[6,824,128]{2,1,0:T(8,128)S(1)} %get-tuple-element.17._, bf16[32,32,256]{2,1,0:T(8,128)(2,1)S(1)} %collective-permute-done.other_ref, ...), custom_call_target="tpu_custom_call", output_to_operand_aliasing={{0}: (0, {})} | custom-call | flops 1000000000 | bytes 12582912 | tf_op jit(solution)/shard_map/pallas_call | solution.py:451
  6.1 0.0 collective-permute-done.1.halo_ref
  6.1 1.4 %shard_map.102 = (f32[2,2,512,128]{3,2,1,0:T(8,128)S(1)}, bf16[32,16,256]{2,1,0:T(8,128)(2,1)S(1)}, bf16[32,16,256]{2,1,0:T(8,128)(2,1)S(1)}) custom-call(f32[2,2,512,128]{3,2,1,0:T(8,128)S(1)} %get-tuple-element.24._, bf16[64,256]{1,0:T(8,128)(2,1)S(1)} %collective-permute-done.1.halo_ref, ...), custom_call_target="tpu_custom_call", output_to_operand_aliasing={{0}: (0, {})} | custom-call | flops 300000000 | bytes 4194304 | tf_op jit(solution)/shard_map/pallas_call | solution.py:467
  7.6 4.2 %collective-permute-start.2 = (bf16[32,16,256]{2,1,0:T(8,128)(2,1)S(1)}, bf16[32,16,256]{2,1,0:T(8,128)(2,1)S(1)}, u32[]{:S(2)}, u32[]{:S(2)}) collective-permute-start(bf16[32,16,256]{2,1,0:T(8,128)(2,1)S(1)} %get-tuple-element.28), channel_id=1, source_target_pairs={{0,16},{16,0},{1,17},{17,1},{2,18},{18,2},{3,19},{19,3},{4,20},{20... | collective-permute-start | bytes 786440 | tf_op jit(solution)/shard_map/ppermute | solution.py:482
  11.8 0.8 %pad_maximum_fusion = bf16[32,32,256]{2,1,0:T(8,128)(2,1)} fusion(bf16[32,16,256]{2,1,0:T(8,128)(2,1)S(1)} %get-tuple-element.27), kind=kLoop, calls=%fused_computation | loop fusion | flops 1048576 | bytes 786432 | tf_op jit(solution)/shard_map/concatenate | solution.py:483
  12.6 0.3 %collective-permute-done.2 = bf16[32,16,256]{2,1,0:T(8,128)(2,1)S(1)} collective-permute-done((bf16[32,16,256]{2,1,0:T(8,128)(2,1)S(1)}, bf16[32,16,256]{2,1,0:T(8,128)(2,1)S(1)}, u32[]{:S(2)}, u32[]{:S(2)}) %collective-permute-start.2) | collective-permute-done | bytes 262176 | tf_op jit(solution)/shard_map/ppermute | solution.py:482
  13.0 0.7 %constant_dynamic-update-slice_fusion = bf16[32,32,256]{2,1,0:T(8,128)(2,1)} fusion(bf16[32,32,256]{2,1,0:T(8,128)(2,1)} %pad_maximum_fusion, bf16[32,16,256]{2,1,0:T(8,128)(2,1)S(1)} %collective-permute-done.2, s32[]{:T(128)S(6)} %select_n.25), kind=kLoop, calls=%fused_computation.6 | loop fusion | bytes 524292 | tf_op jit(solution)/shard_map/dynamic_update_slice | solution.py:484
  (3 shorter events, 0.0 us)
Async XLA Ops:
  0.0 2.3 %collective-permute-start = (bf16[32,32,256]{2,1,0:T(8,128)(2,1)}, bf16[32,32,256]{2,1,0:T(8,128)(2,1)S(1)}, u32[]{:S(2)}, u32[]{:S(2)}) collective-permute-start(bf16[32,32,256]{2,1,0:T(8,128)(2,1)} %own_hbm), channel_id=1, source_target_pairs={{0,16},{16,0},{1,17},{17,1},{2,18},{18,2},{3,19},{19,3},{4,20},{20... | collective-permute-start | bytes 1572872 | tf_op jit(solution)/shard_map/ppermute | solution.py:406
  2.4 3.7 %collective-permute-start.1 = (bf16[64,256]{1,0:T(8,128)(2,1)S(1)}, bf16[64,256]{1,0:T(8,128)(2,1)S(1)}, u32[]{:S(2)}, u32[]{:S(2)}) collective-permute-start(bf16[64,256]{1,0:T(8,128)(2,1)S(1)} %pad_maximum_fusion.1), channel_id=1, source_target_pairs={{16,1},{1,16},{17,2},{2,17},{18,3},{3,18},{19,4},{4,19},{20,5},{5,... | collective-permute-start | bytes 98312 | tf_op jit(solution)/shard_map/ppermute | solution.py:450
  7.6 5.4 %collective-permute-start.2 = (bf16[32,16,256]{2,1,0:T(8,128)(2,1)S(1)}, bf16[32,16,256]{2,1,0:T(8,128)(2,1)S(1)}, u32[]{:S(2)}, u32[]{:S(2)}) collective-permute-start(bf16[32,16,256]{2,1,0:T(8,128)(2,1)S(1)} %get-tuple-element.28), channel_id=1, source_target_pairs={{0,16},{16,0},{1,17},{17,1},{2,18},{18,2},{3,19},{19,3},{4,20},{20... | collective-permute-start | bytes 786440 | tf_op jit(solution)/shard_map/ppermute | solution.py:482

commit v10 on v9

--- a/solution.py
+++ b/solution.py
@@ -148,7 +148,7 @@
         copy.wait()
 
 
-def edge_terms(first, second, core, taps, edge_ref, side_ref):
+def add_edge_terms(first, second, core, taps, edge_ref, mixed_ref, column):
     rows, channels = first.shape
     for t in range(channels // LANES):
         at = slice(t * LANES, (t + 1) * LANES)
@@ -159,10 +159,11 @@
                 place = pl.ds(2 * (row + r + 1), 8, stride=2)
                 edge_ref[t, place, :] = half[r : r + 8, at]
         for r in range(0, 2 * rows, 8):
-            total = edge_ref[t, pl.ds(2 * r, 8, stride=2), :] * taps[0][:, at]
-            for a in (1, 2):
+            place = pl.ds(r * GROUP + column, 8, stride=GROUP)
+            total = mixed_ref[t, place, :]
+            for a in range(3):
                 total = total + edge_ref[t, pl.ds(2 * (r + a), 8, stride=2), :] * taps[a][:, at]
-            side_ref[r // 8, :, at] = total
+            mixed_ref[t, place, :] = total
 
 
 def column_taps(taps_ref, core, on_core0):
@@ -216,35 +217,39 @@
 
 
 def conv_steps(mixed, fwd_ref, bwd_ref, w_out_ref, h_ref, prod_ref, z_ref, put):
-    streams, block, _ = prod_ref.shape
+    streams, block, lanes = prod_ref.shape
+    lanes = lanes // 2
     rows = block // GROUP
-    width = streams * LANES
+    width = streams * lanes
 
     def products(n):
-        base = n * LANES
         for row in range(0, rows, 2):
             for h in range(2):
-                two = [
-                    mixed(h * rows + r, width + base) * mixed(h * rows + r, 2 * width + base)
-                    for r in (row, row + 1)
-                ]
-                prod_ref[n, row * GROUP : (row + 2) * GROUP, h * LANES : (h + 1) * LANES] = (
-                    jnp.concatenate(two, 0).astype(BF16)
-                )
+                for base in range(n * lanes, (n + 1) * lanes, LANES):
+                    two = [
+                        mixed(h * rows + r, width + base) * mixed(h * rows + r, 2 * width + base)
+                        for r in (row, row + 1)
+                    ]
+                    at = h * lanes + base - n * lanes
+                    prod_ref[n, row * GROUP : (row + 2) * GROUP, at : at + LANES] = (
+                        jnp.concatenate(two, 0).astype(BF16)
+                    )
         return jnp.dot(fwd_ref[...], prod_ref[n], preferred_element_type=F32)
 
     def filtered(n, spectra):
-        base = n * LANES
-        low, high = spectra[:, :LANES], spectra[:, LANES:]
+        channels = slice(n * lanes, (n + 1) * lanes)
+        low, high = spectra[:, :lanes], spectra[:, lanes:]
+
+        def response(j, s):
+            place = j * rows + s
+            return jnp.broadcast_to(h_ref[place : place + 1, channels], (GROUP, lanes))
+
         for k in range(0, rows, 2):
             parts = [[], [], [], []]
             for s in (k, k + 1):
-                near_r, near_i, near_2, all_r, all_i, all_2 = (
-                    jnp.broadcast_to(
-                        h_ref[j * rows + s : j * rows + s + 1, base : base + LANES], (GROUP, LANES)
-                    )
-                    for j in range(6)
-                )
+                near_r, near_i = response(0, s), response(1, s)
+                all_r, all_i = response(3, s), response(4, s)
+                near_2, all_2 = (response(2, s), response(5, s)) if s == 0 else (near_r, all_r)
                 re = slice(s * GROUP, (s + 1) * GROUP)
                 im = slice(block + s * GROUP, block + (s + 1) * GROUP)
                 lr, li, hr, hi = low[re], low[im], high[re], high[im]
@@ -253,20 +258,23 @@
                 parts[2].append(lr * all_r - li * all_i + hr * near_r - hi * near_i)
                 parts[3].append(lr * all_i + li * all_2 + hr * near_i + hi * near_2)
             for j in range(4):
-                at, lane = (j % 2) * block + k * GROUP, (j // 2) * LANES
-                z_ref[n, at : at + 2 * GROUP, lane : lane + LANES] = jnp.concatenate(
+                at, lane = (j % 2) * block + k * GROUP, (j // 2) * lanes
+                z_ref[n, at : at + 2 * GROUP, lane : lane + lanes] = jnp.concatenate(
                     parts[j], 0
                 ).astype(BF16)
         return jnp.dot(bwd_ref[...], z_ref[n], preferred_element_type=F32)
 
     def gated(n, conv):
-        line = [
-            mixed(h * rows + r, n * LANES)
-            * conv[r * GROUP : (r + 1) * GROUP, h * LANES : (h + 1) * LANES]
-            for h in range(2)
-            for r in range(rows)
-        ]
-        return jnp.concatenate(line, 0).astype(BF16)
+        columns = []
+        for base in range(0, lanes, LANES):
+            line = [
+                mixed(h * rows + r, n * lanes + base)
+                * conv[r * GROUP : (r + 1) * GROUP, h * lanes + base : h * lanes + base + LANES]
+                for h in range(2)
+                for r in range(rows)
+            ]
+            columns.append(jnp.concatenate(line, 0).astype(BF16))
+        return columns
 
     spectra = []
     for n in range(streams):
@@ -277,7 +285,7 @@
         convs.append(filtered(n, spectra[n]))
         yield
     final = jnp.dot(
-        jnp.concatenate([gated(n, convs[n]) for n in range(streams)], 1),
+        jnp.concatenate([c for n in range(streams) for c in gated(n, convs[n])], 1),
         w_out_ref[...],
         preferred_element_type=F32,
     )
@@ -301,7 +309,8 @@
 
     def store_in(ref, row0):
         def store(row, at, value):
-            ref[row0 + row, :, at] = value
+            place = pl.ds(pl.multiple_of((row0 + row) * GROUP, GROUP), GROUP)
+            ref[at.start // LANES, place, :] = value
 
         return store
 
@@ -339,7 +348,7 @@
 
     steps = edge_all()
     conv = conv_steps(
-        lambda r, base: mixed_ref[r, :, base : base + LANES],
+        lambda r, base: mixed_ref[base // LANES, r * GROUP : (r + 1) * GROUP, :],
         fwd_ref, bwd_ref, w_out_ref, h_ref, prod_ref, z_ref, put,
     )
     for _ in conv:
@@ -350,23 +359,20 @@
 
 
 def edge_kernel(
-    _, halo_ref, mixed_ref, w_in_ref, taps_ref, fwd_ref, bwd_ref, w_out_ref, h_ref,
-    out_ref, mine_ref, send_ref,
-    strip_ref, side_ref, prod_ref, z_ref,
+    _, __, halo_ref, w_in_ref, taps_ref, fwd_ref, bwd_ref, w_out_ref, h_ref,
+    out_ref, mixed_ref, mine_ref, send_ref,
+    strip_ref, prod_ref, z_ref,
 ):
     core = lax.axis_index("row")
     rows, part, width = mine_ref.shape
     got = jnp.dot(halo_ref[...], w_in_ref[...], preferred_element_type=F32)
-    edge_terms(
-        got[:rows], got[rows:], 1 - core, column_taps(taps_ref, core, 0), strip_ref, side_ref
-    )
-    sub = lax.broadcasted_iota(jnp.int32, (GROUP, LANES), 0)
-    at_edge = sub == core * (GROUP - 1)
+    add_edge_terms(
+        got[:rows], got[rows:], 1 - core, column_taps(taps_ref, core, 0), strip_ref,
+        mixed_ref, core * (GROUP - 1),
+    )
 
     def mixed(r, base):
-        at = slice(base, base + LANES)
-        add = jnp.broadcast_to(side_ref[r // 8, r % 8 : r % 8 + 1, at], (GROUP, LANES))
-        return mixed_ref[r, :, at] + jnp.where(at_edge, add, 0.0)
+        return mixed_ref[base // LANES, r * GROUP : (r + 1) * GROUP, :]
 
     def put(final):
         interleave(out_ref, final, core)
@@ -399,6 +405,7 @@
 
     p_shape = shape((3 * width // LANES, (rows + 2) * PITCH + GROUP, LANES), F32)
     out_shape = shape((2, width // LANES, rows * part, LANES), F32)
+    mixed_shape = shape((3 * width // LANES, height * GROUP, LANES), F32)
 
     swap = [(0, 1), (1, 0)]
     rowmajor = Layout((0, 1, 2))
@@ -450,13 +457,13 @@
     halo = lax.ppermute(jnp.concatenate([outer, column(0)], 0), ("row", "col"), pairs)
     _, edge_mixed, inner = pl.pallas_call(
         inner_kernel,
-        out_shape=(p_shape, shape((height, GROUP, 3 * width), F32), out_shape),
+        out_shape=(p_shape, mixed_shape, out_shape),
         in_specs=[vmem] * 9,
         out_specs=(vmem,) * 3,
         input_output_aliases={0: 0},
         scratch_shapes=[
             pltpu.VMEM(p_shape.shape, F32),
-            pltpu.VMEM((height, GROUP, 3 * width), F32),
+            pltpu.VMEM(mixed_shape.shape, F32),
             pltpu.VMEM((width // LANES, rows * GROUP, 2 * LANES), BF16),
             pltpu.VMEM((width // LANES, 2 * rows * GROUP, 2 * LANES), BF16),
         ],
@@ -464,21 +471,20 @@
         cost_estimate=pl.CostEstimate(flops=10**9, bytes_accessed=12 * 1024 * 1024, transcendentals=0),
     )(projected, other, column(part), w_in_v, taps, fwd_v, bwd_v, w_out_v, spectrum)
     half_shape = shape((rows, part, width), BF16)
-    _, mine, send = pl.pallas_call(
+    _, _, mine, send = pl.pallas_call(
         edge_kernel,
-        out_shape=(out_shape, half_shape, half_shape),
+        out_shape=(out_shape, mixed_shape, half_shape, half_shape),
         in_specs=[vmem] * 9,
-        out_specs=(vmem,) * 3,
-        input_output_aliases={0: 0},
+        out_specs=(vmem,) * 4,
+        input_output_aliases={0: 0, 1: 1},
         scratch_shapes=[
             pltpu.VMEM((3 * width // LANES, 2 * height + 8, LANES), F32),
-            pltpu.VMEM((height // 8, 8, 3 * width), F32),
-            pltpu.VMEM((width // LANES, rows * GROUP, 2 * LANES), BF16),
-            pltpu.VMEM((width // LANES, 2 * rows * GROUP, 2 * LANES), BF16),
+            pltpu.VMEM((1, rows * GROUP, 2 * width), BF16),
+            pltpu.VMEM((1, 2 * rows * GROUP, 2 * width), BF16),
         ],
         compiler_params=limit,
         cost_estimate=pl.CostEstimate(flops=3 * 10**8, bytes_accessed=4 * 1024 * 1024, transcendentals=0),
-    )(inner, halo, edge_mixed, w_in_v, taps, fwd_v, bwd_v, w_out_v, spectrum)
+    )(inner, edge_mixed, halo, w_in_v, taps, fwd_v, bwd_v, w_out_v, spectrum)
     theirs = lax.ppermute(send, "row", swap)
     both = jnp.concatenate([mine, mine], 1)
     return lax.dynamic_update_slice_in_dim(both, theirs, (1 - core) * part, 1)

time: 13.8 us -> 13.8 us (level)
  transfers between devices with their start and end apart: 3 -> 3, of which waited for: 1 -> 1; matrix products, arithmetic and copies ran while one was open for 6% -> 6% of each run, Pallas kernels for 35% -> 36%
where the time goes in v10:
time: 13.8 us; the launch traced here: 13.6 us
  Pallas kernels  6.2 us (45%)
  starting transfers between devices  5.34 us (39%)
  other arithmetic  0.86 us (6%)
  local copies, waits for them, and re-layouts  0.83 us (6%)
  waiting for transfers between devices  0.33 us (2%)
    ppermute x1, starting transfers between devices, on_device(): theirs = lax.ppermute(send, 'row', swap)  4.22 us
    pallas_call x1, Pallas kernels, on_device(): pl.pallas_call(inner_kernel, out_shape=(p_shape, mixed_shape, out_shape),...  3.03 us
    pallas_call x1, Pallas kernels, on_device(): pl.pallas_call(prep_kernel, out_shape=(p_shape, shape(w_in.shape, BF16),...  1.81 us
    pallas_call x1, Pallas kernels, on_device(): pl.pallas_call(edge_kernel, out_shape=(out_shape, mixed_shape, half_shape...  1.36 us
    concatenate x1, other arithmetic, on_device(): both = jnp.concatenate([mine, mine], 1)  0.83 us
    dynamic_update_slice x1, local copies, waits for them, and re-layouts, on_device(): return lax.dynamic_update_slice_in_dim(both, theirs, (1 - core) * part, 1)  0.72 us
    ppermute x1, starting transfers between devices, on_device(): lax.ppermute(jnp.concatenate([outer, column(0)], 0), ('row', 'col'), pairs)  0.66 us
    ppermute x1, starting transfers between devices, on_device(): lax.ppermute(image_tokens, 'row', swap)  0.45 us
  transfers between devices with their start and end apart: 3, of which 1 were waited for; matrix products, arithmetic and copies ran while one was open for 6% of the time, Pallas kernels for 36%

profile of v10, /device:TPU:0, one launch (start us, length us, event | category | flops | bytes accessed | tf_op | source)
XLA Modules:
  0.0 13.6 jit_solution(17275068960833689752)
XLA Ops:
  0.0 0.5 %collective-permute-start = (bf16[32,32,256]{2,1,0:T(8,128)(2,1)}, bf16[32,32,256]{2,1,0:T(8,128)(2,1)S(1)}, u32[]{:S(2)}, u32[]{:S(2)}) collective-permute-start(bf16[32,32,256]{2,1,0:T(8,128)(2,1)} %own_hbm), channel_id=1, source_target_pairs={{0,16},{16,0},{1,17},{17,1},{2,18},{18,2},{3,19},{19,3},{4,20},{20... | collective-permute-start | bytes 1572872 | tf_op jit(solution)/shard_map/ppermute | solution.py:413
  0.5 1.8 %shard_map.100 = (f32[6,824,128]{2,1,0:T(8,128)S(1)}, bf16[256,768]{1,0:T(8,128)(2,1)S(1)}, bf16[256,256]{1,0:T(8,128)(2,1)S(1)}, bf16[512,256]{1,0:T(8,128)(2,1...) custom-call(bf16[32,32,256]{2,1,0:T(8,128)(2,1)} %own_hbm, ...), custom_call_target="tpu_custom_call" | custom-call | bytes 3145728 | tf_op jit(solution)/shard_map/pallas_call | solution.py:418
  2.3 0.0 collective-permute-done.other_ref
  2.3 0.1 fusion.2
  2.4 0.7 %collective-permute-start.1 = (bf16[64,256]{1,0:T(8,128)(2,1)S(1)}, bf16[64,256]{1,0:T(8,128)(2,1)S(1)}, u32[]{:S(2)}, u32[]{:S(2)}) collective-permute-start(bf16[64,256]{1,0:T(8,128)(2,1)S(1)} %pad_maximum_fusion.1), channel_id=1, source_target_pairs={{16,1},{1,16},{17,2},{2,17},{18,3},{3,18},{19,4},{4,19},{20,5},{5,... | collective-permute-start | bytes 98312 | tf_op jit(solution)/shard_map/ppermute | solution.py:457
  3.1 3.0 %shard_map.101 = (f32[6,824,128]{2,1,0:T(8,128)S(1)}, f32[6,512,128]{2,1,0:T(8,128)S(1)}, f32[2,2,512,128]{3,2,1,0:T(8,128)S(1)}) custom-call(f32[6,824,128]{2,1,0:T(8,128)S(1)} %get-tuple-element.17._, bf16[32,32,256]{2,1,0:T(8,128)(2,1)S(1)} %collective-permute-done.other_ref, ...), custom_call_target="tpu_custom_call", output_to_operand_aliasing={{0}: (0, {})} | custom-call | flops 1000000000 | bytes 12582912 | tf_op jit(solution)/shard_map/pallas_call | solution.py:458
  6.2 0.0 collective-permute-done.1.halo_ref
  6.2 1.4 %shard_map.102 = (f32[2,2,512,128]{3,2,1,0:T(8,128)S(1)}, f32[6,512,128]{2,1,0:T(8,128)S(1)}, bf16[32,16,256]{2,1,0:T(8,128)(2,1)S(1)}, bf16[32,16,256]{2,1,0:T(8,128)(2,1)S(1)}) custom-call(f32[2,2,512,128]{3,2,1,0:T(8,128)S(1)} %get-tuple-element.24._, f32[6,512,128]{2,1,0:T(8,128)S(1)} %get-tuple-element.25.__, ...), custom_call_target="tpu_custom_call", output_to_operand_aliasing={{0}: (0, {}), {1}: (1, {})} | custom-call | flops 300000000 | bytes 4194304 | tf_op jit(solution)/shard_map/pallas_call | solution.py:474
  7.5 4.2 %collective-permute-start.2 = (bf16[32,16,256]{2,1,0:T(8,128)(2,1)S(1)}, bf16[32,16,256]{2,1,0:T(8,128)(2,1)S(1)}, u32[]{:S(2)}, u32[]{:S(2)}) collective-permute-start(bf16[32,16,256]{2,1,0:T(8,128)(2,1)S(1)} %get-tuple-element.28), channel_id=1, source_target_pairs={{0,16},{16,0},{1,17},{17,1},{2,18},{18,2},{3,19},{19,3},{4,20},{20... | collective-permute-start | bytes 786440 | tf_op jit(solution)/shard_map/ppermute | solution.py:488
  11.8 0.8 %pad_maximum_fusion = bf16[32,32,256]{2,1,0:T(8,128)(2,1)} fusion(bf16[32,16,256]{2,1,0:T(8,128)(2,1)S(1)} %get-tuple-element.27), kind=kLoop, calls=%fused_computation | loop fusion | flops 1048576 | bytes 786432 | tf_op jit(solution)/shard_map/concatenate | solution.py:489
  12.6 0.3 %collective-permute-done.2 = bf16[32,16,256]{2,1,0:T(8,128)(2,1)S(1)} collective-permute-done((bf16[32,16,256]{2,1,0:T(8,128)(2,1)S(1)}, bf16[32,16,256]{2,1,0:T(8,128)(2,1)S(1)}, u32[]{:S(2)}, u32[]{:S(2)}) %collective-permute-start.2) | collective-permute-done | bytes 262176 | tf_op jit(solution)/shard_map/ppermute | solution.py:488
  12.9 0.7 %constant_dynamic-update-slice_fusion = bf16[32,32,256]{2,1,0:T(8,128)(2,1)} fusion(bf16[32,32,256]{2,1,0:T(8,128)(2,1)} %pad_maximum_fusion, bf16[32,16,256]{2,1,0:T(8,128)(2,1)S(1)} %collective-permute-done.2, s32[]{:T(128)S(6)} %select_n.25), kind=kLoop, calls=%fused_computation.6 | loop fusion | bytes 524292 | tf_op jit(solution)/shard_map/dynamic_update_slice | solution.py:490
  (3 shorter events, 0.0 us)
Async XLA Ops:
  0.0 2.3 %collective-permute-start = (bf16[32,32,256]{2,1,0:T(8,128)(2,1)}, bf16[32,32,256]{2,1,0:T(8,128)(2,1)S(1)}, u32[]{:S(2)}, u32[]{:S(2)}) collective-permute-start(bf16[32,32,256]{2,1,0:T(8,128)(2,1)} %own_hbm), channel_id=1, source_target_pairs={{0,16},{16,0},{1,17},{17,1},{2,18},{18,2},{3,19},{19,3},{4,20},{20... | collective-permute-start | bytes 1572872 | tf_op jit(solution)/shard_map/ppermute | solution.py:413
  2.4 3.7 %collective-permute-start.1 = (bf16[64,256]{1,0:T(8,128)(2,1)S(1)}, bf16[64,256]{1,0:T(8,128)(2,1)S(1)}, u32[]{:S(2)}, u32[]{:S(2)}) collective-permute-start(bf16[64,256]{1,0:T(8,128)(2,1)S(1)} %pad_maximum_fusion.1), channel_id=1, source_target_pairs={{16,1},{1,16},{17,2},{2,17},{18,3},{3,18},{19,4},{4,19},{20,5},{5,... | collective-permute-start | bytes 98312 | tf_op jit(solution)/shard_map/ppermute | solution.py:457
  7.5 5.4 %collective-permute-start.2 = (bf16[32,16,256]{2,1,0:T(8,128)(2,1)S(1)}, bf16[32,16,256]{2,1,0:T(8,128)(2,1)S(1)}, u32[]{:S(2)}, u32[]{:S(2)}) collective-permute-start(bf16[32,16,256]{2,1,0:T(8,128)(2,1)S(1)} %get-tuple-element.28), channel_id=1, source_target_pairs={{0,16},{16,0},{1,17},{17,1},{2,18},{18,2},{3,19},{19,3},{4,20},{20... | collective-permute-start | bytes 786440 | tf_op jit(solution)/shard_map/ppermute | solution.py:488

commit v11 on v10

--- a/solution.py
+++ b/solution.py
@@ -216,6 +216,17 @@
                 ]
 
 
+def tall_dot(left, right, pieces):
+    size = left.shape[0] // pieces
+    return jnp.concatenate(
+        [
+            jnp.dot(left[i * size : (i + 1) * size], right, preferred_element_type=F32)
+            for i in range(pieces)
+        ],
+        0,
+    )
+
+
 def conv_steps(mixed, fwd_ref, bwd_ref, w_out_ref, h_ref, prod_ref, z_ref, put):
     streams, block, lanes = prod_ref.shape
     lanes = lanes // 2
@@ -234,7 +245,7 @@
                     prod_ref[n, row * GROUP : (row + 2) * GROUP, at : at + LANES] = (
                         jnp.concatenate(two, 0).astype(BF16)
                     )
-        return jnp.dot(fwd_ref[...], prod_ref[n], preferred_element_type=F32)
+        return tall_dot(fwd_ref, prod_ref[n], 2 * streams)
 
     def filtered(n, spectra):
         channels = slice(n * lanes, (n + 1) * lanes)
@@ -262,7 +273,7 @@
                 z_ref[n, at : at + 2 * GROUP, lane : lane + lanes] = jnp.concatenate(
                     parts[j], 0
                 ).astype(BF16)
-        return jnp.dot(bwd_ref[...], z_ref[n], preferred_element_type=F32)
+        return tall_dot(bwd_ref, z_ref[n], 2)
 
     def gated(n, conv):
         columns = []
@@ -284,10 +295,8 @@
     for n in range(streams):
         convs.append(filtered(n, spectra[n]))
         yield
-    final = jnp.dot(
-        jnp.concatenate([c for n in range(streams) for c in gated(n, convs[n])], 1),
-        w_out_ref[...],
-        preferred_element_type=F32,
+    final = tall_dot(
+        jnp.concatenate([c for n in range(streams) for c in gated(n, convs[n])], 1), w_out_ref[...], 4
     )
     yield
     put(final.reshape(2, rows, GROUP, width))

time: 13.8 us -> 13.8 us (level)
  transfers between devices with their start and end apart: 3 -> 3, of which waited for: 1 -> 1; matrix products, arithmetic and copies ran while one was open for 6% -> 6% of each run, Pallas kernels for 36% -> 35%
where the time goes in v11:
time: 13.8 us; the launch traced here: 13.6 us
  Pallas kernels  6.2 us (45%)
  starting transfers between devices  5.33 us (39%)
  other arithmetic  0.86 us (6%)
  local copies, waits for them, and re-layouts  0.83 us (6%)
  waiting for transfers between devices  0.33 us (2%)
    ppermute x1, starting transfers between devices, on_device(): theirs = lax.ppermute(send, 'row', swap)  4.21 us
    pallas_call x1, Pallas kernels, on_device(): pl.pallas_call(inner_kernel, out_shape=(p_shape, mixed_shape, out_shape),...  3 us
    pallas_call x1, Pallas kernels, on_device(): pl.pallas_call(prep_kernel, out_shape=(p_shape, shape(w_in.shape, BF16),...  1.81 us
    pallas_call x1, Pallas kernels, on_device(): pl.pallas_call(edge_kernel, out_shape=(out_shape, mixed_shape, half_shape...  1.39 us
    concatenate x1, other arithmetic, on_device(): both = jnp.concatenate([mine, mine], 1)  0.83 us
    dynamic_update_slice x1, local copies, waits for them, and re-layouts, on_device(): return lax.dynamic_update_slice_in_dim(both, theirs, (1 - core) * part, 1)  0.72 us
    ppermute x1, starting transfers between devices, on_device(): lax.ppermute(jnp.concatenate([outer, column(0)], 0), ('row', 'col'), pairs)  0.66 us
    ppermute x1, starting transfers between devices, on_device(): lax.ppermute(image_tokens, 'row', swap)  0.45 us
  transfers between devices with their start and end apart: 3, of which 1 were waited for; matrix products, arithmetic and copies ran while one was open for 6% of the time, Pallas kernels for 35%

profile of v11, /device:TPU:0, one launch (start us, length us, event | category | flops | bytes accessed | tf_op | source)
XLA Modules:
  0.0 13.6 jit_solution(14268605873792603293)
XLA Ops:
  0.0 0.5 %collective-permute-start = (bf16[32,32,256]{2,1,0:T(8,128)(2,1)}, bf16[32,32,256]{2,1,0:T(8,128)(2,1)S(1)}, u32[]{:S(2)}, u32[]{:S(2)}) collective-permute-start(bf16[32,32,256]{2,1,0:T(8,128)(2,1)} %own_hbm), channel_id=1, source_target_pairs={{0,16},{16,0},{1,17},{17,1},{2,18},{18,2},{3,19},{19,3},{4,20},{20... | collective-permute-start | bytes 1572872 | tf_op jit(solution)/shard_map/ppermute | solution.py:422
  0.5 1.8 %shard_map.100 = (f32[6,824,128]{2,1,0:T(8,128)S(1)}, bf16[256,768]{1,0:T(8,128)(2,1)S(1)}, bf16[256,256]{1,0:T(8,128)(2,1)S(1)}, bf16[512,256]{1,0:T(8,128)(2,1...) custom-call(bf16[32,32,256]{2,1,0:T(8,128)(2,1)} %own_hbm, ...), custom_call_target="tpu_custom_call" | custom-call | bytes 3145728 | tf_op jit(solution)/shard_map/pallas_call | solution.py:427
  2.3 0.0 collective-permute-done.other_ref
  2.3 0.1 fusion.2
  2.4 0.7 %collective-permute-start.1 = (bf16[64,256]{1,0:T(8,128)(2,1)S(1)}, bf16[64,256]{1,0:T(8,128)(2,1)S(1)}, u32[]{:S(2)}, u32[]{:S(2)}) collective-permute-start(bf16[64,256]{1,0:T(8,128)(2,1)S(1)} %pad_maximum_fusion.1), channel_id=1, source_target_pairs={{16,1},{1,16},{17,2},{2,17},{18,3},{3,18},{19,4},{4,19},{20,5},{5,... | collective-permute-start | bytes 98312 | tf_op jit(solution)/shard_map/ppermute | solution.py:466
  3.1 3.0 %shard_map.101 = (f32[6,824,128]{2,1,0:T(8,128)S(1)}, f32[6,512,128]{2,1,0:T(8,128)S(1)}, f32[2,2,512,128]{3,2,1,0:T(8,128)S(1)}) custom-call(f32[6,824,128]{2,1,0:T(8,128)S(1)} %get-tuple-element.17._, bf16[32,32,256]{2,1,0:T(8,128)(2,1)S(1)} %collective-permute-done.other_ref, ...), custom_call_target="tpu_custom_call", output_to_operand_aliasing={{0}: (0, {})} | custom-call | flops 1000000000 | bytes 12582912 | tf_op jit(solution)/shard_map/pallas_call | solution.py:467
  6.1 0.0 collective-permute-done.1.halo_ref
  6.1 1.4 %shard_map.102 = (f32[2,2,512,128]{3,2,1,0:T(8,128)S(1)}, f32[6,512,128]{2,1,0:T(8,128)S(1)}, bf16[32,16,256]{2,1,0:T(8,128)(2,1)S(1)}, bf16[32,16,256]{2,1,0:T(8,128)(2,1)S(1)}) custom-call(f32[2,2,512,128]{3,2,1,0:T(8,128)S(1)} %get-tuple-element.24._, f32[6,512,128]{2,1,0:T(8,128)S(1)} %get-tuple-element.25.__, ...), custom_call_target="tpu_custom_call", output_to_operand_aliasing={{0}: (0, {}), {1}: (1, {})} | custom-call | flops 300000000 | bytes 4194304 | tf_op jit(solution)/shard_map/pallas_call | solution.py:483
  7.5 4.2 %collective-permute-start.2 = (bf16[32,16,256]{2,1,0:T(8,128)(2,1)S(1)}, bf16[32,16,256]{2,1,0:T(8,128)(2,1)S(1)}, u32[]{:S(2)}, u32[]{:S(2)}) collective-permute-start(bf16[32,16,256]{2,1,0:T(8,128)(2,1)S(1)} %get-tuple-element.28), channel_id=1, source_target_pairs={{0,16},{16,0},{1,17},{17,1},{2,18},{18,2},{3,19},{19,3},{4,20},{20... | collective-permute-start | bytes 786440 | tf_op jit(solution)/shard_map/ppermute | solution.py:497
  11.7 0.8 %pad_maximum_fusion = bf16[32,32,256]{2,1,0:T(8,128)(2,1)} fusion(bf16[32,16,256]{2,1,0:T(8,128)(2,1)S(1)} %get-tuple-element.27), kind=kLoop, calls=%fused_computation | loop fusion | flops 1048576 | bytes 786432 | tf_op jit(solution)/shard_map/concatenate | solution.py:498
  12.6 0.3 %collective-permute-done.2 = bf16[32,16,256]{2,1,0:T(8,128)(2,1)S(1)} collective-permute-done((bf16[32,16,256]{2,1,0:T(8,128)(2,1)S(1)}, bf16[32,16,256]{2,1,0:T(8,128)(2,1)S(1)}, u32[]{:S(2)}, u32[]{:S(2)}) %collective-permute-start.2) | collective-permute-done | bytes 262176 | tf_op jit(solution)/shard_map/ppermute | solution.py:497
  12.9 0.7 %constant_dynamic-update-slice_fusion = bf16[32,32,256]{2,1,0:T(8,128)(2,1)} fusion(bf16[32,32,256]{2,1,0:T(8,128)(2,1)} %pad_maximum_fusion, bf16[32,16,256]{2,1,0:T(8,128)(2,1)S(1)} %collective-permute-done.2, s32[]{:T(128)S(6)} %select_n.25), kind=kLoop, calls=%fused_computation.6 | loop fusion | bytes 524292 | tf_op jit(solution)/shard_map/dynamic_update_slice | solution.py:499
  (3 shorter events, 0.0 us)
Async XLA Ops:
  0.0 2.3 %collective-permute-start = (bf16[32,32,256]{2,1,0:T(8,128)(2,1)}, bf16[32,32,256]{2,1,0:T(8,128)(2,1)S(1)}, u32[]{:S(2)}, u32[]{:S(2)}) collective-permute-start(bf16[32,32,256]{2,1,0:T(8,128)(2,1)} %own_hbm), channel_id=1, source_target_pairs={{0,16},{16,0},{1,17},{17,1},{2,18},{18,2},{3,19},{19,3},{4,20},{20... | collective-permute-start | bytes 1572872 | tf_op jit(solution)/shard_map/ppermute | solution.py:422
  2.4 3.7 %collective-permute-start.1 = (bf16[64,256]{1,0:T(8,128)(2,1)S(1)}, bf16[64,256]{1,0:T(8,128)(2,1)S(1)}, u32[]{:S(2)}, u32[]{:S(2)}) collective-permute-start(bf16[64,256]{1,0:T(8,128)(2,1)S(1)} %pad_maximum_fusion.1), channel_id=1, source_target_pairs={{16,1},{1,16},{17,2},{2,17},{18,3},{3,18},{19,4},{4,19},{20,5},{5,... | collective-permute-start | bytes 98312 | tf_op jit(solution)/shard_map/ppermute | solution.py:466
  7.5 5.4 %collective-permute-start.2 = (bf16[32,16,256]{2,1,0:T(8,128)(2,1)S(1)}, bf16[32,16,256]{2,1,0:T(8,128)(2,1)S(1)}, u32[]{:S(2)}, u32[]{:S(2)}) collective-permute-start(bf16[32,16,256]{2,1,0:T(8,128)(2,1)S(1)} %get-tuple-element.28), channel_id=1, source_target_pairs={{0,16},{16,0},{1,17},{17,1},{2,18},{18,2},{3,19},{19,3},{4,20},{20... | collective-permute-start | bytes 786440 | tf_op jit(solution)/shard_map/ppermute | solution.py:497

commit v12 on v10

--- a/solution.py
+++ b/solution.py
@@ -140,7 +140,8 @@
     )
     for j in range(6):
         part_j = spectrum[j * rows : (j + 1) * rows]
-        h_ref[j * rows : (j + 1) * rows, :] = part_j + gain if j in (0, 2) else part_j
+        part_j = part_j + gain if j in (0, 2) else part_j
+        h_ref[j * rows // 8 : (j + 1) * rows // 8] = part_j.reshape(rows // 8, 8, width)
     for a in range(3):
         taps_ref[3 * a : 3 * a + 3, :] = kernel_ref[a].astype(F32)
     taps_ref[9, :] = bias_ref[...]
@@ -241,8 +242,8 @@
         low, high = spectra[:, :lanes], spectra[:, lanes:]
 
         def response(j, s):
-            place = j * rows + s
-            return jnp.broadcast_to(h_ref[place : place + 1, channels], (GROUP, lanes))
+            place = j * rows // 8 + s // 8
+            return jnp.broadcast_to(h_ref[place, s % 8 : s % 8 + 1, channels], (GROUP, lanes))
 
         for k in range(0, rows, 2):
             parts = [[], [], [], []]
@@ -293,6 +294,82 @@
     put(final.reshape(2, rows, GROUP, width))
 
 
+def conv_loops(mixed_ref, fwd_ref, bwd_ref, w_out_ref, h_ref, prod_ref, s_ref, z_ref, c_ref, g_ref):
+    block, width = prod_ref.shape[0], prod_ref.shape[1] // 2
+    rows = block // GROUP
+    bases = range(0, width, LANES)
+
+    def mixed(row, base):
+        return mixed_ref[base // LANES, pl.ds(pl.multiple_of(row * GROUP, GROUP), GROUP), :]
+
+    def pair_place(first, step):
+        return pl.ds(pl.multiple_of((first + step) * GROUP, 2 * GROUP), 2 * GROUP)
+
+    def products(i, carry):
+        for row in range(0, 8, 2):
+            for h in range(2):
+                for base in bases:
+                    two = [
+                        mixed(h * rows + 8 * i + r, width + base)
+                        * mixed(h * rows + 8 * i + r, 2 * width + base)
+                        for r in (row, row + 1)
+                    ]
+                    at = h * width + base
+                    prod_ref[pair_place(8 * i, row), at : at + LANES] = jnp.concatenate(
+                        two, 0
+                    ).astype(BF16)
+        return carry
+
+    lax.fori_loop(0, rows // 8, products, 0)
+    s_ref[...] = jnp.dot(fwd_ref[...], prod_ref[...], preferred_element_type=F32)
+
+    def filtered(i, carry):
+        for k in range(0, 8, 2):
+            parts = [[], [], [], []]
+            for s in (k, k + 1):
+                near_r, near_i, near_2, all_r, all_i, all_2 = (
+                    jnp.broadcast_to(h_ref[j * (rows // 8) + i, s : s + 1, :], (GROUP, width))
+                    for j in range(6)
+                )
+                re = pl.ds(pl.multiple_of((8 * i + s) * GROUP, GROUP), GROUP)
+                im = pl.ds(pl.multiple_of(block + (8 * i + s) * GROUP, GROUP), GROUP)
+                lr, hr = s_ref[re, :width], s_ref[re, width:]
+                li, hi = s_ref[im, :width], s_ref[im, width:]
+                parts[0].append(lr * near_r - li * near_i)
+                parts[1].append(lr * near_i + li * near_2)
+                parts[2].append(lr * all_r - li * all_i + hr * near_r - hi * near_i)
+                parts[3].append(lr * all_i + li * all_2 + hr * near_i + hi * near_2)
+            for j in range(4):
+                lane = (j // 2) * width
+                z_ref[pair_place((j % 2) * rows + 8 * i, k), lane : lane + width] = (
+                    jnp.concatenate(parts[j], 0).astype(BF16)
+                )
+        return carry
+
+    lax.fori_loop(0, rows // 8, filtered, 0)
+    c_ref[...] = jnp.dot(bwd_ref[...], z_ref[...], preferred_element_type=F32)
+
+    def gated(i, carry):
+        for row in range(0, 8, 2):
+            for h in range(2):
+                for base in bases:
+                    two = [
+                        mixed(h * rows + 8 * i + r, base)
+                        * c_ref[
+                            pl.ds(pl.multiple_of((8 * i + r) * GROUP, GROUP), GROUP),
+                            h * width + base : h * width + base + LANES,
+                        ]
+                        for r in (row, row + 1)
+                    ]
+                    g_ref[pair_place(h * rows + 8 * i, row), base : base + LANES] = jnp.concatenate(
+                        two, 0
+                    ).astype(BF16)
+        return carry
+
+    lax.fori_loop(0, rows // 8, gated, 0)
+    return jnp.dot(g_ref[...], w_out_ref[...], preferred_element_type=F32)
+
+
 def inner_kernel(
     _, other_ref, other_strip_ref,
     w_in_ref, taps_ref, fwd_ref, bwd_ref, w_out_ref, h_ref,
@@ -361,7 +438,7 @@
 def edge_kernel(
     _, __, halo_ref, w_in_ref, taps_ref, fwd_ref, bwd_ref, w_out_ref, h_ref,
     out_ref, mixed_ref, mine_ref, send_ref,
-    strip_ref, prod_ref, z_ref,
+    strip_ref, prod_ref, s_ref, z_ref, c_ref, g_ref,
 ):
     core = lax.axis_index("row")
     rows, part, width = mine_ref.shape
@@ -371,21 +448,21 @@
         mixed_ref, core * (GROUP - 1),
     )
 
-    def mixed(r, base):
-        return mixed_ref[base // LANES, r * GROUP : (r + 1) * GROUP, :]
-
-    def put(final):
-        interleave(out_ref, final, core)
-
-    for _ in conv_steps(
-        mixed, fwd_ref, bwd_ref, w_out_ref, h_ref, prod_ref, z_ref, put
-    ):
-        pass
-    for ref, half in ((mine_ref, core), (send_ref, 1 - core)):
-        for t in range(width // LANES):
-            ref[:, :, t * LANES : (t + 1) * LANES] = (
-                out_ref[half, t].reshape(rows, part, LANES).astype(BF16)
-            )
+    final = conv_loops(
+        mixed_ref, fwd_ref, bwd_ref, w_out_ref, h_ref, prod_ref, s_ref, z_ref, c_ref, g_ref
+    )
+    interleave(out_ref, final.reshape(2, rows, GROUP, width), core)
+
+    def finish(i, carry):
+        for ref, half in ((mine_ref, core), (send_ref, 1 - core)):
+            for t in range(width // LANES):
+                place = pl.ds(pl.multiple_of(8 * i * part, 8 * part), 8 * part)
+                ref[pl.ds(8 * i, 8), :, t * LANES : (t + 1) * LANES] = (
+                    out_ref[half, t, place, :].reshape(8, part, LANES).astype(BF16)
+                )
+        return carry
+
+    lax.fori_loop(0, rows // 8, finish, 0)
 
 
 def on_device(image_tokens, w_in, conv_kernel, conv_bias, long_filter, skip_gain, w_out):
@@ -424,7 +501,7 @@
             shape(fwd.shape, BF16),
             shape(bwd.shape, BF16),
             shape((16, 3 * width), F32),
-            shape((6 * rows, width), F32),
+            shape((6 * rows // 8, 8, width), F32),
             shape((rows, width), BF16),
         ),
         in_specs=[hbm] * 10,
@@ -479,8 +556,11 @@
         input_output_aliases={0: 0, 1: 1},
         scratch_shapes=[
             pltpu.VMEM((3 * width // LANES, 2 * height + 8, LANES), F32),
-            pltpu.VMEM((1, rows * GROUP, 2 * width), BF16),
-            pltpu.VMEM((1, 2 * rows * GROUP, 2 * width), BF16),
+            pltpu.VMEM((rows * GROUP, 2 * width), BF16),
+            pltpu.VMEM((2 * rows * GROUP, 2 * width), F32),
+            pltpu.VMEM((2 * rows * GROUP, 2 * width), BF16),
+            pltpu.VMEM((rows * GROUP, 2 * width), F32),
+            pltpu.VMEM((2 * rows * GROUP, width), BF16),
         ],
         compiler_params=limit,
         cost_estimate=pl.CostEstimate(flops=3 * 10**8, bytes_accessed=4 * 1024 * 1024, transcendentals=0),

time: 13.8 us -> 14.1 us (1.022)
  Pallas kernels: 6.2 us -> 6.54 us
    pallas_call x1, Pallas kernels: 1.36 us -> 1.7 us  [on_device(): pl.pallas_call(edge_kernel, out_shape=(out_shape, mixed_shape, half_shape...]
  transfers between devices with their start and end apart: 3 -> 3, of which waited for: 1 -> 1; matrix products, arithmetic and copies ran while one was open for 6% -> 6% of each run, Pallas kernels for 36% -> 35%
where the time goes in v12:
time: 14.1 us; the launch traced here: 14 us
  Pallas kernels  6.54 us (46%)
  starting transfers between devices  5.33 us (38%)
  other arithmetic  0.86 us (6%)
  local copies, waits for them, and re-layouts  0.83 us (6%)
  waiting for transfers between devices  0.33 us (2%)
    ppermute x1, starting transfers between devices, on_device(): theirs = lax.ppermute(send, 'row', swap)  4.21 us
    pallas_call x1, Pallas kernels, on_device(): pl.pallas_call(inner_kernel, out_shape=(p_shape, mixed_shape, out_shape),...  3.03 us
    pallas_call x1, Pallas kernels, on_device(): pl.pallas_call(prep_kernel, out_shape=(p_shape, shape(w_in.shape, BF16),...  1.81 us
    pallas_call x1, Pallas kernels, on_device(): pl.pallas_call(edge_kernel, out_shape=(out_shape, mixed_shape, half_shape...  1.7 us
    concatenate x1, other arithmetic, on_device(): both = jnp.concatenate([mine, mine], 1)  0.83 us
    dynamic_update_slice x1, local copies, waits for them, and re-layouts, on_device(): return lax.dynamic_update_slice_in_dim(both, theirs, (1 - core) * part, 1)  0.72 us
    ppermute x1, starting transfers between devices, on_device(): lax.ppermute(jnp.concatenate([outer, column(0)], 0), ('row', 'col'), pairs)  0.66 us
    ppermute x1, starting transfers between devices, on_device(): lax.ppermute(image_tokens, 'row', swap)  0.45 us
  transfers between devices with their start and end apart: 3, of which 1 were waited for; matrix products, arithmetic and copies ran while one was open for 6% of the time, Pallas kernels for 35%

profile of v12, /device:TPU:0, one launch (start us, length us, event | category | flops | bytes accessed | tf_op | source)
XLA Modules:
  0.0 14.0 jit_solution(2066992899413198022)
XLA Ops:
  0.0 0.5 %collective-permute-start = (bf16[32,32,256]{2,1,0:T(8,128)(2,1)}, bf16[32,32,256]{2,1,0:T(8,128)(2,1)S(1)}, u32[]{:S(2)}, u32[]{:S(2)}) collective-permute-start(bf16[32,32,256]{2,1,0:T(8,128)(2,1)} %own_hbm), channel_id=1, source_target_pairs={{0,16},{16,0},{1,17},{17,1},{2,18},{18,2},{3,19},{19,3},{4,20},{20... | collective-permute-start | bytes 1572872 | tf_op jit(solution)/shard_map/ppermute | solution.py:490
  0.5 1.8 %shard_map.100 = (f32[6,824,128]{2,1,0:T(8,128)S(1)}, bf16[256,768]{1,0:T(8,128)(2,1)S(1)}, bf16[256,256]{1,0:T(8,128)(2,1)S(1)}, bf16[512,256]{1,0:T(8,128)(2,1...) custom-call(bf16[32,32,256]{2,1,0:T(8,128)(2,1)} %own_hbm, ...), custom_call_target="tpu_custom_call" | custom-call | bytes 3145728 | tf_op jit(solution)/shard_map/pallas_call | solution.py:495
  2.3 0.0 collective-permute-done.other_ref
  2.3 0.1 fusion.2
  2.4 0.7 %collective-permute-start.1 = (bf16[64,256]{1,0:T(8,128)(2,1)S(1)}, bf16[64,256]{1,0:T(8,128)(2,1)S(1)}, u32[]{:S(2)}, u32[]{:S(2)}) collective-permute-start(bf16[64,256]{1,0:T(8,128)(2,1)S(1)} %pad_maximum_fusion.1), channel_id=1, source_target_pairs={{16,1},{1,16},{17,2},{2,17},{18,3},{3,18},{19,4},{4,19},{20,5},{5,... | collective-permute-start | bytes 98312 | tf_op jit(solution)/shard_map/ppermute | solution.py:534
  3.1 3.0 %shard_map.101 = (f32[6,824,128]{2,1,0:T(8,128)S(1)}, f32[6,512,128]{2,1,0:T(8,128)S(1)}, f32[2,2,512,128]{3,2,1,0:T(8,128)S(1)}) custom-call(f32[6,824,128]{2,1,0:T(8,128)S(1)} %get-tuple-element.17._, bf16[32,32,256]{2,1,0:T(8,128)(2,1)S(1)} %collective-permute-done.other_ref, ...), custom_call_target="tpu_custom_call", output_to_operand_aliasing={{0}: (0, {})} | custom-call | flops 1000000000 | bytes 12582912 | tf_op jit(solution)/shard_map/pallas_call | solution.py:535
  6.2 0.0 collective-permute-done.1.halo_ref
  6.2 1.7 %shard_map.102 = (f32[2,2,512,128]{3,2,1,0:T(8,128)S(1)}, f32[6,512,128]{2,1,0:T(8,128)S(1)}, bf16[32,16,256]{2,1,0:T(8,128)(2,1)S(1)}, bf16[32,16,256]{2,1,0:T(8,128)(2,1)S(1)}) custom-call(f32[2,2,512,128]{3,2,1,0:T(8,128)S(1)} %get-tuple-element.24._, f32[6,512,128]{2,1,0:T(8,128)S(1)} %get-tuple-element.25.__, ...), custom_call_target="tpu_custom_call", output_to_operand_aliasing={{0}: (0, {}), {1}: (1, {})} | custom-call | flops 300000000 | bytes 4194304 | tf_op jit(solution)/shard_map/pallas_call | solution.py:551
  7.9 4.2 %collective-permute-start.2 = (bf16[32,16,256]{2,1,0:T(8,128)(2,1)S(1)}, bf16[32,16,256]{2,1,0:T(8,128)(2,1)S(1)}, u32[]{:S(2)}, u32[]{:S(2)}) collective-permute-start(bf16[32,16,256]{2,1,0:T(8,128)(2,1)S(1)} %get-tuple-element.28), channel_id=1, source_target_pairs={{0,16},{16,0},{1,17},{17,1},{2,18},{18,2},{3,19},{19,3},{4,20},{20... | collective-permute-start | bytes 786440 | tf_op jit(solution)/shard_map/ppermute | solution.py:568
  12.1 0.8 %pad_maximum_fusion = bf16[32,32,256]{2,1,0:T(8,128)(2,1)} fusion(bf16[32,16,256]{2,1,0:T(8,128)(2,1)S(1)} %get-tuple-element.27), kind=kLoop, calls=%fused_computation | loop fusion | flops 1048576 | bytes 786432 | tf_op jit(solution)/shard_map/concatenate | solution.py:569
  12.9 0.3 %collective-permute-done.2 = bf16[32,16,256]{2,1,0:T(8,128)(2,1)S(1)} collective-permute-done((bf16[32,16,256]{2,1,0:T(8,128)(2,1)S(1)}, bf16[32,16,256]{2,1,0:T(8,128)(2,1)S(1)}, u32[]{:S(2)}, u32[]{:S(2)}) %collective-permute-start.2) | collective-permute-done | bytes 262176 | tf_op jit(solution)/shard_map/ppermute | solution.py:568
  13.2 0.7 %constant_dynamic-update-slice_fusion = bf16[32,32,256]{2,1,0:T(8,128)(2,1)} fusion(bf16[32,32,256]{2,1,0:T(8,128)(2,1)} %pad_maximum_fusion, bf16[32,16,256]{2,1,0:T(8,128)(2,1)S(1)} %collective-permute-done.2, s32[]{:T(128)S(6)} %select_n.25), kind=kLoop, calls=%fused_computation.6 | loop fusion | bytes 524292 | tf_op jit(solution)/shard_map/dynamic_update_slice | solution.py:570
  (3 shorter events, 0.0 us)
Async XLA Ops:
  0.0 2.3 %collective-permute-start = (bf16[32,32,256]{2,1,0:T(8,128)(2,1)}, bf16[32,32,256]{2,1,0:T(8,128)(2,1)S(1)}, u32[]{:S(2)}, u32[]{:S(2)}) collective-permute-start(bf16[32,32,256]{2,1,0:T(8,128)(2,1)} %own_hbm), channel_id=1, source_target_pairs={{0,16},{16,0},{1,17},{17,1},{2,18},{18,2},{3,19},{19,3},{4,20},{20... | collective-permute-start | bytes 1572872 | tf_op jit(solution)/shard_map/ppermute | solution.py:490
  2.4 3.7 %collective-permute-start.1 = (bf16[64,256]{1,0:T(8,128)(2,1)S(1)}, bf16[64,256]{1,0:T(8,128)(2,1)S(1)}, u32[]{:S(2)}, u32[]{:S(2)}) collective-permute-start(bf16[64,256]{1,0:T(8,128)(2,1)S(1)} %pad_maximum_fusion.1), channel_id=1, source_target_pairs={{16,1},{1,16},{17,2},{2,17},{18,3},{3,18},{19,4},{4,19},{20,5},{5,... | collective-permute-start | bytes 98312 | tf_op jit(solution)/shard_map/ppermute | solution.py:534
  7.9 5.4 %collective-permute-start.2 = (bf16[32,16,256]{2,1,0:T(8,128)(2,1)S(1)}, bf16[32,16,256]{2,1,0:T(8,128)(2,1)S(1)}, u32[]{:S(2)}, u32[]{:S(2)}) collective-permute-start(bf16[32,16,256]{2,1,0:T(8,128)(2,1)S(1)} %get-tuple-element.28), channel_id=1, source_target_pairs={{0,16},{16,0},{1,17},{17,1},{2,18},{18,2},{3,19},{19,3},{4,20},{20... | collective-permute-start | bytes 786440 | tf_op jit(solution)/shard_map/ppermute | solution.py:568

commit v13 on v10

--- a/solution.py
+++ b/solution.py
@@ -138,9 +138,13 @@
     spectrum = jnp.dot(spec_ref[0], filt, preferred_element_type=F32) + jnp.dot(
         spec_ref[1], filt, preferred_element_type=F32
     )
-    for j in range(6):
-        part_j = spectrum[j * rows : (j + 1) * rows]
-        h_ref[j * rows : (j + 1) * rows, :] = part_j + gain if j in (0, 2) else part_j
+    pieces = [spectrum[j * rows : (j + 1) * rows] for j in range(6)]
+    near = [pieces[0] + gain, pieces[1], pieces[2] + gain]
+    for j in range(3):
+        h_ref[0, j] = near[j]
+        h_ref[0, 3 + j] = jnp.zeros((rows, width), F32)
+        h_ref[1, j] = pieces[3 + j]
+        h_ref[1, 3 + j] = near[j]
     for a in range(3):
         taps_ref[3 * a : 3 * a + 3, :] = kernel_ref[a].astype(F32)
     taps_ref[9, :] = bias_ref[...]
@@ -241,8 +245,7 @@
         low, high = spectra[:, :lanes], spectra[:, lanes:]
 
         def response(j, s):
-            place = j * rows + s
-            return jnp.broadcast_to(h_ref[place : place + 1, channels], (GROUP, lanes))
+            return jnp.broadcast_to(h_ref[j // 3, j % 3, s : s + 1, channels], (GROUP, lanes))
 
         for k in range(0, rows, 2):
             parts = [[], [], [], []]
@@ -358,13 +361,53 @@
         pass
 
 
+def finish_half(half, core, s_ref, mixed_ref, bwd_ref, w_out_ref, h_ref, z_ref, out_ref, to_ref):
+    rows, part, width = to_ref.shape
+    block = rows * GROUP
+    for k in range(0, rows, 2):
+        parts = [[], []]
+        for s in (k, k + 1):
+
+            def response(j):
+                return jnp.broadcast_to(h_ref[half, j, s : s + 1, :], (GROUP, width))
+
+            upper_r, upper_i, lower_r, lower_i = (response(j) for j in (0, 1, 3, 4))
+            upper_2, lower_2 = (response(2), response(5)) if s == 0 else (upper_r, lower_r)
+            re = slice(s * GROUP, (s + 1) * GROUP)
+            im = slice(block + s * GROUP, block + (s + 1) * GROUP)
+            lr, hr = s_ref[re, :width], s_ref[re, width:]
+            li, hi = s_ref[im, :width], s_ref[im, width:]
+            parts[0].append(lr * upper_r - li * upper_i + hr * lower_r - hi * lower_i)
+            parts[1].append(lr * upper_i + li * upper_2 + hr * lower_i + hi * lower_2)
+        for j in range(2):
+            at = j * block + k * GROUP
+            z_ref[at : at + 2 * GROUP, :] = jnp.concatenate(parts[j], 0).astype(BF16)
+    conv = jnp.dot(bwd_ref[...], z_ref[...], preferred_element_type=F32)
+    columns = []
+    for t in range(width // LANES):
+        line = [
+            mixed_ref[t, pl.ds(pl.multiple_of((half * rows + r) * GROUP, GROUP), GROUP), :]
+            * conv[r * GROUP : (r + 1) * GROUP, t * LANES : (t + 1) * LANES]
+            for r in range(rows)
+        ]
+        columns.append(jnp.concatenate(line, 0).astype(BF16))
+    final = jnp.dot(jnp.concatenate(columns, 1), w_out_ref[...], preferred_element_type=F32)
+    for t in range(width // LANES):
+        at = slice(t * LANES, (t + 1) * LANES)
+        for r in range(rows):
+            out_ref[half, t, pl.ds(r * part + core, GROUP, stride=2), :] = final[
+                r * GROUP : (r + 1) * GROUP, at
+            ]
+        to_ref[:, :, at] = out_ref[half, t].reshape(rows, part, LANES).astype(BF16)
+
+
 def edge_kernel(
     _, __, halo_ref, w_in_ref, taps_ref, fwd_ref, bwd_ref, w_out_ref, h_ref,
-    out_ref, mixed_ref, mine_ref, send_ref,
+    out_ref, mixed_ref, s_ref, send_ref,
     strip_ref, prod_ref, z_ref,
 ):
     core = lax.axis_index("row")
-    rows, part, width = mine_ref.shape
+    rows, part, width = send_ref.shape
     got = jnp.dot(halo_ref[...], w_in_ref[...], preferred_element_type=F32)
     add_edge_terms(
         got[:rows], got[rows:], 1 - core, column_taps(taps_ref, core, 0), strip_ref,
@@ -374,18 +417,30 @@
     def mixed(r, base):
         return mixed_ref[base // LANES, r * GROUP : (r + 1) * GROUP, :]
 
-    def put(final):
-        interleave(out_ref, final, core)
-
-    for _ in conv_steps(
-        mixed, fwd_ref, bwd_ref, w_out_ref, h_ref, prod_ref, z_ref, put
-    ):
-        pass
-    for ref, half in ((mine_ref, core), (send_ref, 1 - core)):
-        for t in range(width // LANES):
-            ref[:, :, t * LANES : (t + 1) * LANES] = (
-                out_ref[half, t].reshape(rows, part, LANES).astype(BF16)
-            )
+    for row in range(0, rows, 2):
+        for h in range(2):
+            for base in range(0, width, LANES):
+                two = [
+                    mixed(h * rows + r, width + base) * mixed(h * rows + r, 2 * width + base)
+                    for r in (row, row + 1)
+                ]
+                at = h * width + base
+                prod_ref[row * GROUP : (row + 2) * GROUP, at : at + LANES] = jnp.concatenate(
+                    two, 0
+                ).astype(BF16)
+    s_ref[...] = jnp.dot(fwd_ref[...], prod_ref[...], preferred_element_type=F32)
+    finish_half(
+        1 - core, core, s_ref, mixed_ref, bwd_ref, w_out_ref, h_ref, z_ref, out_ref, send_ref
+    )
+
+
+def own_kernel(
+    _, mixed_ref, s_ref, bwd_ref, w_out_ref, h_ref,
+    out_ref, mine_ref,
+    z_ref,
+):
+    core = lax.axis_index("row")
+    finish_half(core, core, s_ref, mixed_ref, bwd_ref, w_out_ref, h_ref, z_ref, out_ref, mine_ref)
 
 
 def on_device(image_tokens, w_in, conv_kernel, conv_bias, long_filter, skip_gain, w_out):
@@ -424,7 +479,7 @@
             shape(fwd.shape, BF16),
             shape(bwd.shape, BF16),
             shape((16, 3 * width), F32),
-            shape((6 * rows, width), F32),
+            shape((2, 6, rows, width), F32),
             shape((rows, width), BF16),
         ),
         in_specs=[hbm] * 10,
@@ -471,21 +526,33 @@
         cost_estimate=pl.CostEstimate(flops=10**9, bytes_accessed=12 * 1024 * 1024, transcendentals=0),
     )(projected, other, column(part), w_in_v, taps, fwd_v, bwd_v, w_out_v, spectrum)
     half_shape = shape((rows, part, width), BF16)
-    _, _, mine, send = pl.pallas_call(
+    s_shape = shape((2 * rows * GROUP, 2 * width), F32)
+    z_scratch = pltpu.VMEM((2 * rows * GROUP, width), BF16)
+    out, edge_mixed, transforms_edge, send = pl.pallas_call(
         edge_kernel,
-        out_shape=(out_shape, mixed_shape, half_shape, half_shape),
+        out_shape=(out_shape, mixed_shape, s_shape, half_shape),
         in_specs=[vmem] * 9,
         out_specs=(vmem,) * 4,
         input_output_aliases={0: 0, 1: 1},
         scratch_shapes=[
             pltpu.VMEM((3 * width // LANES, 2 * height + 8, LANES), F32),
-            pltpu.VMEM((1, rows * GROUP, 2 * width), BF16),
-            pltpu.VMEM((1, 2 * rows * GROUP, 2 * width), BF16),
+            pltpu.VMEM((rows * GROUP, 2 * width), BF16),
+            z_scratch,
         ],
         compiler_params=limit,
         cost_estimate=pl.CostEstimate(flops=3 * 10**8, bytes_accessed=4 * 1024 * 1024, transcendentals=0),
     )(inner, edge_mixed, halo, w_in_v, taps, fwd_v, bwd_v, w_out_v, spectrum)
     theirs = lax.ppermute(send, "row", swap)
+    _, mine = pl.pallas_call(
+        own_kernel,
+        out_shape=(out_shape, half_shape),
+        in_specs=[vmem] * 6,
+        out_specs=(vmem,) * 2,
+        input_output_aliases={0: 0},
+        scratch_shapes=[z_scratch],
+        compiler_params=limit,
+        cost_estimate=pl.CostEstimate(flops=10**8, bytes_accessed=2 * 1024 * 1024, transcendentals=0),
+    )(out, edge_mixed, transforms_edge, bwd_v, w_out_v, spectrum)
     both = jnp.concatenate([mine, mine], 1)
     return lax.dynamic_update_slice_in_dim(both, theirs, (1 - core) * part, 1)
 

time: 13.8 us -> 19.5 us (1.41)
  local copies, waits for them, and re-layouts: 0.83 us -> 5.79 us
  Pallas kernels: 6.2 us -> 7.21 us
  waiting for transfers between devices: 0.33 us -> 0.01 us
    unnamed x0 -> x8, local copies, waits for them, and re-layouts: none -> 4.02 us
    pallas_call x1 -> x2, Pallas kernels: 1.36 us -> 2.39 us  [the longest x1 1.86 us: on_device(): pl.pallas_call(edge_kernel, out_shape=(out_shape, mixed_shape, s_shape, h...]
    dynamic_update_slice x1, local copies, waits for them, and re-layouts: 0.72 us -> 1.67 us  [on_device(): return lax.dynamic_update_slice_in_dim(both, theirs, (1 - core) * part, 1)]
    ppermute x1, waiting for transfers between devices: 0.33 us -> 0.01 us  [on_device(): theirs = lax.ppermute(send, 'row', swap)]
  transfers between devices with their start and end apart: 3 -> 3, of which waited for: 1 -> 0; matrix products, arithmetic and copies ran while one was open for 6% -> 4% of each run, Pallas kernels for 36% -> 28%
where the time goes in v13:
time: 19.5 us; the launch traced here: 19.2 us
  Pallas kernels  7.21 us (37%)
  local copies, waits for them, and re-layouts  5.79 us (30%)
  starting transfers between devices  5.25 us (27%)
  other arithmetic  0.86 us (4%)
    ppermute x1, starting transfers between devices, on_device(): theirs = lax.ppermute(send, 'row', swap)  4.14 us
    unnamed x8, local copies, waits for them, and re-layouts  4.02 us
    pallas_call x1, Pallas kernels, on_device(): pl.pallas_call(inner_kernel, out_shape=(p_shape, mixed_shape, out_shape),...  3 us
    pallas_call x1, Pallas kernels, on_device(): pl.pallas_call(edge_kernel, out_shape=(out_shape, mixed_shape, s_shape, h...  1.86 us
    pallas_call x1, Pallas kernels, on_device(): pl.pallas_call(prep_kernel, out_shape=(p_shape, shape(w_in.shape, BF16),...  1.81 us
    dynamic_update_slice x1, local copies, waits for them, and re-layouts, on_device(): return lax.dynamic_update_slice_in_dim(both, theirs, (1 - core) * part, 1)  1.67 us
    concatenate x1, other arithmetic, on_device(): both = jnp.concatenate([mine, mine], 1)  0.84 us
    ppermute x1, starting transfers between devices, on_device(): lax.ppermute(jnp.concatenate([outer, column(0)], 0), ('row', 'col'), pairs)  0.66 us
  transfers between devices with their start and end apart: 3, of which 0 were waited for; matrix products, arithmetic and copies ran while one was open for 4% of the time, Pallas kernels for 28%

profile of v13, /device:TPU:0, one launch (start us, length us, event | category | flops | bytes accessed | tf_op | source)
XLA Modules:
  0.0 19.2 jit_solution(11816859091741661529)
XLA Ops:
  0.0 0.5 %collective-permute-start = (bf16[32,32,256]{2,1,0:T(8,128)(2,1)}, bf16[32,32,256]{2,1,0:T(8,128)(2,1)S(1)}, u32[]{:S(2)}, u32[]{:S(2)}) collective-permute-start(bf16[32,32,256]{2,1,0:T(8,128)(2,1)} %own_hbm), channel_id=1, source_target_pairs={{0,16},{16,0},{1,17},{17,1},{2,18},{18,2},{3,19},{19,3},{4,20},{20... | collective-permute-start | bytes 1572872 | tf_op jit(solution)/shard_map/ppermute | solution.py:468
  0.5 1.8 %shard_map.100 = (f32[6,824,128]{2,1,0:T(8,128)S(1)}, bf16[256,768]{1,0:T(8,128)(2,1)S(1)}, bf16[256,256]{1,0:T(8,128)(2,1)S(1)}, bf16[512,256]{1,0:T(8,128)(2,1...) custom-call(bf16[32,32,256]{2,1,0:T(8,128)(2,1)} %own_hbm, ...), custom_call_target="tpu_custom_call" | custom-call | bytes 3145728 | tf_op jit(solution)/shard_map/pallas_call | solution.py:473
  2.3 0.0 collective-permute-done.other_ref
  2.3 0.1 fusion.2
  2.4 0.0 copy-start.2
  2.4 0.8 %copy-done.2 = bf16[32,32,256]{2,1,0:T(8,128)(2,1)} copy-done((bf16[32,32,256]{2,1,0:T(8,128)(2,1)}, bf16[32,32,256]{2,1,0:T(8,128)(2,1)S(1)}, u32[]{:S(2)}) %copy-start.2) | copy-done | bytes 524312
  3.2 0.7 %collective-permute-start.1 = (bf16[64,256]{1,0:T(8,128)(2,1)S(1)}, bf16[64,256]{1,0:T(8,128)(2,1)S(1)}, u32[]{:S(2)}, u32[]{:S(2)}) collective-permute-start(bf16[64,256]{1,0:T(8,128)(2,1)S(1)} %pad_maximum_fusion.1), channel_id=1, source_target_pairs={{16,1},{1,16},{17,2},{2,17},{18,3},{3,18},{19,4},{4,19},{20,5},{5,... | collective-permute-start | bytes 98312 | tf_op jit(solution)/shard_map/ppermute | solution.py:512
  3.9 0.0 copy-start.3
  3.9 1.0 %copy-done.3 = bf16[32,32,256]{2,1,0:T(8,128)(2,1)S(1)} copy-done((bf16[32,32,256]{2,1,0:T(8,128)(2,1)S(1)}, bf16[32,32,256]{2,1,0:T(8,128)(2,1)}, u32[]{:S(2)}) %copy-start.3) | copy-done | bytes 524312
  4.9 3.0 %shard_map.101 = (f32[6,824,128]{2,1,0:T(8,128)S(1)}, f32[6,512,128]{2,1,0:T(8,128)S(1)}, f32[2,2,512,128]{3,2,1,0:T(8,128)S(1)}) custom-call(f32[6,824,128]{2,1,0:T(8,128)S(1)} %get-tuple-element.20._, bf16[32,32,256]{2,1,0:T(8,128)(2,1)S(1)} %copy-done.3, bf16[32,256]{1,0:T(8,128)(2,1)S(1)} %fusion.1.other_strip_ref, ...), custom_call_target="tpu_custom_call", output_to_operand_aliasing={{0}: (0, {})} | custom-call | flops 1000000000 | bytes 12582912 | tf_op jit(solution)/shard_map/pallas_call | solution.py:513
  8.0 0.0 collective-permute-done.1.halo_ref
  8.0 1.9 %shard_map.102 = (f32[2,2,512,128]{3,2,1,0:T(8,128)S(1)}, f32[6,512,128]{2,1,0:T(8,128)S(1)}, f32[512,512]{1,0:T(8,128)S(1)}, bf16[32,16,256]{2,1,0:T(8,128)(2,1)}) custom-call(f32[2,2,512,128]{3,2,1,0:T(8,128)S(1)} %get-tuple-element.27._, f32[6,512,128]{2,1,0:T(8,128)S(1)} %get-tuple-element.28.__, ...), custom_call_target="tpu_custom_call", output_to_operand_aliasing={{0}: (0, {}), {1}: (1, {})} | custom-call | flops 300000000 | bytes 4194304 | tf_op jit(solution)/shard_map/pallas_call | solution.py:531
  9.8 0.0 copy-start
  9.8 1.0 %copy-done = f32[512,512]{1,0:T(8,128)} copy-done((f32[512,512]{1,0:T(8,128)}, f32[512,512]{1,0:T(8,128)S(1)}, u32[]{:S(2)}) %copy-start) | copy-done | bytes 1048600
  10.8 4.1 %collective-permute-start.2 = (bf16[32,16,256]{2,1,0:T(8,128)(2,1)}, bf16[32,16,256]{2,1,0:T(8,128)(2,1)}, u32[]{:S(2)}, u32[]{:S(2)}) collective-permute-start(bf16[32,16,256]{2,1,0:T(8,128)(2,1)} %get-tuple-element.34), channel_id=1, source_target_pairs={{0,16},{16,0},{1,17},{17,1},{2,18},{18,2},{3,19},{19,3},{4,20},{20... | collective-permute-start | bytes 786440 | tf_op jit(solution)/shard_map/ppermute | solution.py:545
  14.9 0.0 copy-start.1
  14.9 1.2 %copy-done.1 = f32[512,512]{1,0:T(8,128)S(1)} copy-done((f32[512,512]{1,0:T(8,128)S(1)}, f32[512,512]{1,0:T(8,128)}, u32[]{:S(2)}) %copy-start.1) | copy-done | bytes 1048600
  16.2 0.5 %shard_map.103 = (f32[2,2,512,128]{3,2,1,0:T(8,128)S(1)}, bf16[32,16,256]{2,1,0:T(8,128)(2,1)S(1)}) custom-call(f32[2,2,512,128]{3,2,1,0:T(8,128)S(1)} %get-tuple-element.30._, f32[6,512,128]{2,1,0:T(8,128)S(1)} %get-tuple-element.31.mixed_ref, f32[512,512]{1,0:T(8,128)S(1)} %copy-done.1, ...), custom_call_target="tpu_custom_call", output_to_operand_aliasing={{0}: (0, {})} | custom-call | flops 100000000 | bytes 2097152 | tf_op jit(solution)/shard_map/pallas_call | solution.py:546
  16.7 0.8 %pad_maximum_fusion = bf16[32,32,256]{2,1,0:T(8,128)(2,1)} fusion(bf16[32,16,256]{2,1,0:T(8,128)(2,1)S(1)} %get-tuple-element.33), kind=kLoop, calls=%fused_computation | loop fusion | flops 1048576 | bytes 786432 | tf_op jit(solution)/shard_map/concatenate | solution.py:556
  17.5 0.0 collective-permute-done.2
  17.5 1.7 %constant_dynamic-update-slice_fusion = bf16[32,32,256]{2,1,0:T(8,128)(2,1)} fusion(bf16[32,32,256]{2,1,0:T(8,128)(2,1)} %pad_maximum_fusion, bf16[32,16,256]{2,1,0:T(8,128)(2,1)} %collective-permute-done.2, s32[]{:T(128)S(6)} %select_n.25), kind=kLoop, calls=%fused_computation.6 | loop fusion | bytes 524292 | tf_op jit(solution)/shard_map/dynamic_update_slice | solution.py:557
  (3 shorter events, 0.0 us)
Async XLA Ops:
  0.0 2.3 %collective-permute-start = (bf16[32,32,256]{2,1,0:T(8,128)(2,1)}, bf16[32,32,256]{2,1,0:T(8,128)(2,1)S(1)}, u32[]{:S(2)}, u32[]{:S(2)}) collective-permute-start(bf16[32,32,256]{2,1,0:T(8,128)(2,1)} %own_hbm), channel_id=1, source_target_pairs={{0,16},{16,0},{1,17},{17,1},{2,18},{18,2},{3,19},{19,3},{4,20},{20... | collective-permute-start | bytes 1572872 | tf_op jit(solution)/shard_map/ppermute | solution.py:468
  2.4 0.8 %copy-start.2 = (bf16[32,32,256]{2,1,0:T(8,128)(2,1)}, bf16[32,32,256]{2,1,0:T(8,128)(2,1)S(1)}, u32[]{:S(2)}) copy-start(bf16[32,32,256]{2,1,0:T(8,128)(2,1)S(1)} %collective-permute-done.other_ref) | copy-start | bytes 1572868
  3.2 4.7 %collective-permute-start.1 = (bf16[64,256]{1,0:T(8,128)(2,1)S(1)}, bf16[64,256]{1,0:T(8,128)(2,1)S(1)}, u32[]{:S(2)}, u32[]{:S(2)}) collective-permute-start(bf16[64,256]{1,0:T(8,128)(2,1)S(1)} %pad_maximum_fusion.1), channel_id=1, source_target_pairs={{16,1},{1,16},{17,2},{2,17},{18,3},{3,18},{19,4},{4,19},{20,5},{5,... | collective-permute-start | bytes 98312 | tf_op jit(solution)/shard_map/ppermute | solution.py:512
  3.9 1.0 %copy-start.3 = (bf16[32,32,256]{2,1,0:T(8,128)(2,1)S(1)}, bf16[32,32,256]{2,1,0:T(8,128)(2,1)}, u32[]{:S(2)}) copy-start(bf16[32,32,256]{2,1,0:T(8,128)(2,1)} %copy-done.2) | copy-start | bytes 1572868
  9.8 1.0 %copy-start = (f32[512,512]{1,0:T(8,128)}, f32[512,512]{1,0:T(8,128)S(1)}, u32[]{:S(2)}) copy-start(f32[512,512]{1,0:T(8,128)S(1)} %get-tuple-element.32.s_ref) | copy-start | bytes 3145732
  10.8 6.7 %collective-permute-start.2 = (bf16[32,16,256]{2,1,0:T(8,128)(2,1)}, bf16[32,16,256]{2,1,0:T(8,128)(2,1)}, u32[]{:S(2)}, u32[]{:S(2)}) collective-permute-start(bf16[32,16,256]{2,1,0:T(8,128)(2,1)} %get-tuple-element.34), channel_id=1, source_target_pairs={{0,16},{16,0},{1,17},{17,1},{2,18},{18,2},{3,19},{19,3},{4,20},{20... | collective-permute-start | bytes 786440 | tf_op jit(solution)/shard_map/ppermute | solution.py:545
  14.9 1.2 %copy-start.1 = (f32[512,512]{1,0:T(8,128)S(1)}, f32[512,512]{1,0:T(8,128)}, u32[]{:S(2)}) copy-start(f32[512,512]{1,0:T(8,128)} %copy-done) | copy-start | bytes 3145732

commit v14 on v13

--- a/solution.py
+++ b/solution.py
@@ -464,6 +464,9 @@
 
     swap = [(0, 1), (1, 0)]
     rowmajor = Layout((0, 1, 2))
+    on_first = core == 0
+    offset = ((1 - core) * part).astype(jnp.uint32)
+    image_tokens, on_first, offset = lax.optimization_barrier((image_tokens, on_first, offset))
     image_tokens = with_layout_constraint(image_tokens, rowmajor)
     other = with_layout_constraint(lax.ppermute(image_tokens, "row", swap), rowmajor)
 
@@ -501,7 +504,7 @@
     )
 
     def by_core(low, high):
-        return jnp.where(core == 0, low, high)
+        return jnp.where(on_first, low, high)
 
     def column(low):
         return by_core(other[:, low], other[:, cols - 1 - low])
@@ -554,7 +557,8 @@
         cost_estimate=pl.CostEstimate(flops=10**8, bytes_accessed=2 * 1024 * 1024, transcendentals=0),
     )(out, edge_mixed, transforms_edge, bwd_v, w_out_v, spectrum)
     both = jnp.concatenate([mine, mine], 1)
-    return lax.dynamic_update_slice_in_dim(both, theirs, (1 - core) * part, 1)
+    zero = jnp.uint32(0)
+    return lax.dynamic_update_slice(both, theirs, (zero, offset, zero))
 
 
 def solution(mesh):

time: 19.5 us -> 16.5 us (0.85)
  the two profiles are of different devices: /device:TPU:0 before, /device:TPU:25 now
where the time goes in v14:
time: 16.5 us; the launch traced here: 16.3 us
  Pallas kernels  6.59 us (40%)
  starting transfers between devices  5.09 us (31%)
  local copies, waits for them, and re-layouts  3.69 us (22%)
  other arithmetic  0.86 us (5%)
    dynamic_update_slice x1, local copies, waits for them, and re-layouts, on_device(): return lax.dynamic_update_slice(both, theirs, (zero, offset, zero))  3.58 us
    ppermute x1, starting transfers between devices, on_device(): lax.ppermute(jnp.concatenate([outer, column(0)], 0), ('row', 'col'), pairs)  3.29 us
    pallas_call x1, Pallas kernels, on_device(): pl.pallas_call(inner_kernel, out_shape=(p_shape, mixed_shape, out_shape),...  3.02 us
    pallas_call x1, Pallas kernels, on_device(): pl.pallas_call(prep_kernel, out_shape=(p_shape, shape(w_in.shape, BF16),...  1.81 us
    pallas_call x1, Pallas kernels, on_device(): pl.pallas_call(edge_kernel, out_shape=(out_shape, mixed_shape, s_shape, h...  1.18 us
    ppermute x1, starting transfers between devices, on_device(): theirs = lax.ppermute(send, 'row', swap)  1.13 us
    concatenate x1, other arithmetic, on_device(): both = jnp.concatenate([mine, mine], 1)  0.84 us
    ppermute x1, starting transfers between devices, on_device(): lax.ppermute(image_tokens, 'row', swap)  0.68 us
  transfers between devices with their start and end apart: 3, of which 0 were waited for; matrix products, arithmetic and copies ran while one was open for 5% of the time, Pallas kernels for 33%

profile of v14, /device:TPU:25, one launch (start us, length us, event | category | flops | bytes accessed | tf_op | source)
XLA Modules:
  0.0 16.3 jit_solution(13447485242995325612)
XLA Ops:
  0.0 0.7 %collective-permute-start = (bf16[32,32,256]{2,1,0:T(8,128)(2,1)}, bf16[32,32,256]{2,1,0:T(8,128)(2,1)S(1)}, u32[]{:S(2)}, u32[]{:S(2)}) collective-permute-start(bf16[32,32,256]{2,1,0:T(8,128)(2,1)} %own_hbm), channel_id=1, source_target_pairs={{0,16},{16,0},{1,17},{17,1},{2,18},{18,2},{3,19},{19,3},{4,20},{20... | collective-permute-start | bytes 1572872 | tf_op jit(solution)/shard_map/ppermute | solution.py:471
  0.7 1.8 %shard_map.100 = (f32[6,824,128]{2,1,0:T(8,128)S(1)}, bf16[256,768]{1,0:T(8,128)(2,1)S(1)}, bf16[256,256]{1,0:T(8,128)(2,1)S(1)}, bf16[512,256]{1,0:T(8,128)(2,1...) custom-call(bf16[32,32,256]{2,1,0:T(8,128)(2,1)} %own_hbm, ...), custom_call_target="tpu_custom_call" | custom-call | bytes 3145728 | tf_op jit(solution)/shard_map/pallas_call | solution.py:476
  2.5 0.0 collective-permute-done.other_ref
  2.5 0.1 fusion.2
  2.7 3.3 %collective-permute-start.1 = (bf16[64,256]{1,0:T(8,128)(2,1)S(1)}, bf16[64,256]{1,0:T(8,128)(2,1)S(1)}, u32[]{:S(2)}, u32[]{:S(2)}) collective-permute-start(bf16[64,256]{1,0:T(8,128)(2,1)S(1)} %pad_maximum_fusion.1), channel_id=1, source_target_pairs={{16,1},{1,16},{17,2},{2,17},{18,3},{3,18},{19,4},{4,19},{20,5},{5,... | collective-permute-start | bytes 98312 | tf_op jit(solution)/shard_map/ppermute | solution.py:515
  6.0 3.0 %shard_map.101 = (f32[6,824,128]{2,1,0:T(8,128)S(1)}, f32[6,512,128]{2,1,0:T(8,128)S(1)}, f32[2,2,512,128]{3,2,1,0:T(8,128)S(1)}) custom-call(f32[6,824,128]{2,1,0:T(8,128)S(1)} %get-tuple-element.24._, bf16[32,32,256]{2,1,0:T(8,128)(2,1)S(1)} %collective-permute-done.other_ref, ...), custom_call_target="tpu_custom_call", output_to_operand_aliasing={{0}: (0, {})} | custom-call | flops 1000000000 | bytes 12582912 | tf_op jit(solution)/shard_map/pallas_call | solution.py:516
  9.0 0.0 collective-permute-done.1.halo_ref
  9.0 1.2 %shard_map.102 = (f32[2,2,512,128]{3,2,1,0:T(8,128)S(1)}, f32[6,512,128]{2,1,0:T(8,128)S(1)}, f32[512,512]{1,0:T(8,128)S(1)}, bf16[32,16,256]{2,1,0:T(8,128)(2,1)S(1)}) custom-call(f32[2,2,512,128]{3,2,1,0:T(8,128)S(1)} %get-tuple-element.32._, f32[6,512,128]{2,1,0:T(8,128)S(1)} %get-tuple-element.33.__, ...), custom_call_target="tpu_custom_call", output_to_operand_aliasing={{0}: (0, {}), {1}: (1, {})} | custom-call | flops 300000000 | bytes 4194304 | tf_op jit(solution)/shard_map/pallas_call | solution.py:534
  10.2 1.1 %collective-permute-start.2 = (bf16[32,16,256]{2,1,0:T(8,128)(2,1)S(1)}, bf16[32,16,256]{2,1,0:T(8,128)(2,1)S(1)}, u32[]{:S(2)}, u32[]{:S(2)}) collective-permute-start(bf16[32,16,256]{2,1,0:T(8,128)(2,1)S(1)} %get-tuple-element.39), channel_id=1, source_target_pairs={{0,16},{16,0},{1,17},{17,1},{2,18},{18,2},{3,19},{19,3},{4,20},{20... | collective-permute-start | bytes 786440 | tf_op jit(solution)/shard_map/ppermute | solution.py:548
  11.3 0.6 %shard_map.103 = (f32[2,2,512,128]{3,2,1,0:T(8,128)S(1)}, bf16[32,16,256]{2,1,0:T(8,128)(2,1)S(1)}) custom-call(f32[2,2,512,128]{3,2,1,0:T(8,128)S(1)} %get-tuple-element.35._, f32[6,512,128]{2,1,0:T(8,128)S(1)} %get-tuple-element.36.mixed_ref, f32[512,512]{1,0:T(8,128)S(1)} %get-tuple-element.37.s_ref, ...), custom_call_target="tpu_custom_call", output_to_operand_aliasing={{0}: (0, {})} | custom-call | flops 100000000 | bytes 2097152 | tf_op jit(solution)/shard_map/pallas_call | solution.py:549
  11.9 0.8 %pad_maximum_fusion = bf16[32,32,256]{2,1,0:T(8,128)(2,1)} fusion(bf16[32,16,256]{2,1,0:T(8,128)(2,1)S(1)} %get-tuple-element.38), kind=kLoop, calls=%fused_computation | loop fusion | flops 1048576 | bytes 786432 | tf_op jit(solution)/shard_map/concatenate | solution.py:559
  12.7 0.0 collective-permute-done.2
  12.7 3.6 %dynamic_update_slice.3 = bf16[32,32,256]{2,1,0:T(8,128)(2,1)} dynamic-update-slice(bf16[32,32,256]{2,1,0:T(8,128)(2,1)} %pad_maximum_fusion, bf16[32,16,256]{2,1,0:T(8,128)(2,1)S(1)} %collective-permute-done.2, u32[]{:T(128)} %constant.19.clone.1, u32[]{:T(128)S(6)} %convert_element_type.3, u32[]{:T(128)} %constant.19.clone.1) | dynamic-update-slice | bytes 524292 | tf_op jit(solution)/shard_map/dynamic_update_slice | solution.py:561
  (3 shorter events, 0.0 us)
Async XLA Ops:
  0.0 2.5 %collective-permute-start = (bf16[32,32,256]{2,1,0:T(8,128)(2,1)}, bf16[32,32,256]{2,1,0:T(8,128)(2,1)S(1)}, u32[]{:S(2)}, u32[]{:S(2)}) collective-permute-start(bf16[32,32,256]{2,1,0:T(8,128)(2,1)} %own_hbm), channel_id=1, source_target_pairs={{0,16},{16,0},{1,17},{17,1},{2,18},{18,2},{3,19},{19,3},{4,20},{20... | collective-permute-start | bytes 1572872 | tf_op jit(solution)/shard_map/ppermute | solution.py:471
  2.7 6.3 %collective-permute-start.1 = (bf16[64,256]{1,0:T(8,128)(2,1)S(1)}, bf16[64,256]{1,0:T(8,128)(2,1)S(1)}, u32[]{:S(2)}, u32[]{:S(2)}) collective-permute-start(bf16[64,256]{1,0:T(8,128)(2,1)S(1)} %pad_maximum_fusion.1), channel_id=1, source_target_pairs={{16,1},{1,16},{17,2},{2,17},{18,3},{3,18},{19,4},{4,19},{20,5},{5,... | collective-permute-start | bytes 98312 | tf_op jit(solution)/shard_map/ppermute | solution.py:515
  10.2 2.6 %collective-permute-start.2 = (bf16[32,16,256]{2,1,0:T(8,128)(2,1)S(1)}, bf16[32,16,256]{2,1,0:T(8,128)(2,1)S(1)}, u32[]{:S(2)}, u32[]{:S(2)}) collective-permute-start(bf16[32,16,256]{2,1,0:T(8,128)(2,1)S(1)} %get-tuple-element.39), channel_id=1, source_target_pairs={{0,16},{16,0},{1,17},{17,1},{2,18},{18,2},{3,19},{19,3},{4,20},{20... | collective-permute-start | bytes 786440 | tf_op jit(solution)/shard_map/ppermute | solution.py:548

commit v15 on v14

--- a/solution.py
+++ b/solution.py
@@ -465,8 +465,7 @@
     swap = [(0, 1), (1, 0)]
     rowmajor = Layout((0, 1, 2))
     on_first = core == 0
-    offset = ((1 - core) * part).astype(jnp.uint32)
-    image_tokens, on_first, offset = lax.optimization_barrier((image_tokens, on_first, offset))
+    image_tokens, on_first = lax.optimization_barrier((image_tokens, on_first))
     image_tokens = with_layout_constraint(image_tokens, rowmajor)
     other = with_layout_constraint(lax.ppermute(image_tokens, "row", swap), rowmajor)
 
@@ -556,9 +555,11 @@
         compiler_params=limit,
         cost_estimate=pl.CostEstimate(flops=10**8, bytes_accessed=2 * 1024 * 1024, transcendentals=0),
     )(out, edge_mixed, transforms_edge, bwd_v, w_out_v, spectrum)
+    mine, late_core = lax.optimization_barrier((mine, core))
+    offset = (1 - late_core) * part
     both = jnp.concatenate([mine, mine], 1)
-    zero = jnp.uint32(0)
-    return lax.dynamic_update_slice(both, theirs, (zero, offset, zero))
+    zero = jnp.int32(0)
+    return lax.dynamic_update_slice_p.bind(both, theirs, zero, offset, zero)
 
 
 def solution(mesh):

time: 16.5 us -> 13.8 us (0.84)
  the two profiles are of different devices: /device:TPU:25 before, /device:TPU:0 now
where the time goes in v15:
time: 13.8 us; the launch traced here: 13.7 us
  Pallas kernels  6.58 us (48%)
  starting transfers between devices  5.32 us (39%)
  other arithmetic  0.86 us (6%)
  local copies, waits for them, and re-layouts  0.83 us (6%)
    ppermute x1, starting transfers between devices, on_device(): theirs = lax.ppermute(send, 'row', swap)  4.2 us
    pallas_call x1, Pallas kernels, on_device(): pl.pallas_call(inner_kernel, out_shape=(p_shape, mixed_shape, out_shape),...  3.01 us
    pallas_call x1, Pallas kernels, on_device(): pl.pallas_call(prep_kernel, out_shape=(p_shape, shape(w_in.shape, BF16),...  1.81 us
    pallas_call x1, Pallas kernels, on_device(): pl.pallas_call(edge_kernel, out_shape=(out_shape, mixed_shape, s_shape, h...  1.18 us
    concatenate x1, other arithmetic, on_device(): both = jnp.concatenate([mine, mine], 1)  0.84 us
    dynamic_update_slice x1, local copies, waits for them, and re-layouts, on_device(): return lax.dynamic_update_slice_p.bind(both, theirs, zero, offset, zero)  0.72 us
    ppermute x1, starting transfers between devices, on_device(): lax.ppermute(jnp.concatenate([outer, column(0)], 0), ('row', 'col'), pairs)  0.66 us
    pallas_call x1, Pallas kernels, on_device(): pl.pallas_call(own_kernel, out_shape=(out_shape, half_shape), in_specs=[v...  0.58 us
  transfers between devices with their start and end apart: 3, of which 0 were waited for; matrix products, arithmetic and copies ran while one was open for 6% of the time, Pallas kernels for 39%

profile of v15, /device:TPU:0, one launch (start us, length us, event | category | flops | bytes accessed | tf_op | source)
XLA Modules:
  0.0 13.7 jit_solution(7151780499685253406)
XLA Ops:
  0.0 0.5 %collective-permute-start = (bf16[32,32,256]{2,1,0:T(8,128)(2,1)}, bf16[32,32,256]{2,1,0:T(8,128)(2,1)S(1)}, u32[]{:S(2)}, u32[]{:S(2)}) collective-permute-start(bf16[32,32,256]{2,1,0:T(8,128)(2,1)} %own_hbm), channel_id=1, source_target_pairs={{0,16},{16,0},{1,17},{17,1},{2,18},{18,2},{3,19},{19,3},{4,20},{20... | collective-permute-start | bytes 1572872 | tf_op jit(solution)/shard_map/ppermute | solution.py:470
  0.5 1.8 %shard_map.100 = (f32[6,824,128]{2,1,0:T(8,128)S(1)}, bf16[256,768]{1,0:T(8,128)(2,1)S(1)}, bf16[256,256]{1,0:T(8,128)(2,1)S(1)}, bf16[512,256]{1,0:T(8,128)(2,1...) custom-call(bf16[32,32,256]{2,1,0:T(8,128)(2,1)} %own_hbm, ...), custom_call_target="tpu_custom_call" | custom-call | bytes 3145728 | tf_op jit(solution)/shard_map/pallas_call | solution.py:475
  2.3 0.0 collective-permute-done.other_ref
  2.3 0.1 fusion.2
  2.4 0.7 %collective-permute-start.1 = (bf16[64,256]{1,0:T(8,128)(2,1)S(1)}, bf16[64,256]{1,0:T(8,128)(2,1)S(1)}, u32[]{:S(2)}, u32[]{:S(2)}) collective-permute-start(bf16[64,256]{1,0:T(8,128)(2,1)S(1)} %pad_maximum_fusion.1), channel_id=1, source_target_pairs={{16,1},{1,16},{17,2},{2,17},{18,3},{3,18},{19,4},{4,19},{20,5},{5,... | collective-permute-start | bytes 98312 | tf_op jit(solution)/shard_map/ppermute | solution.py:514
  3.1 3.0 %shard_map.101 = (f32[6,824,128]{2,1,0:T(8,128)S(1)}, f32[6,512,128]{2,1,0:T(8,128)S(1)}, f32[2,2,512,128]{3,2,1,0:T(8,128)S(1)}) custom-call(f32[6,824,128]{2,1,0:T(8,128)S(1)} %get-tuple-element.25._, bf16[32,32,256]{2,1,0:T(8,128)(2,1)S(1)} %collective-permute-done.other_ref, ...), custom_call_target="tpu_custom_call", output_to_operand_aliasing={{0}: (0, {})} | custom-call | flops 1000000000 | bytes 12582912 | tf_op jit(solution)/shard_map/pallas_call | solution.py:515
  6.1 0.0 collective-permute-done.1.halo_ref
  6.1 1.2 %shard_map.102 = (f32[2,2,512,128]{3,2,1,0:T(8,128)S(1)}, f32[6,512,128]{2,1,0:T(8,128)S(1)}, f32[512,512]{1,0:T(8,128)S(1)}, bf16[32,16,256]{2,1,0:T(8,128)(2,1)S(1)}) custom-call(f32[2,2,512,128]{3,2,1,0:T(8,128)S(1)} %get-tuple-element.33._, f32[6,512,128]{2,1,0:T(8,128)S(1)} %get-tuple-element.34.__, ...), custom_call_target="tpu_custom_call", output_to_operand_aliasing={{0}: (0, {}), {1}: (1, {})} | custom-call | flops 300000000 | bytes 4194304 | tf_op jit(solution)/shard_map/pallas_call | solution.py:533
  7.3 4.2 %collective-permute-start.2 = (bf16[32,16,256]{2,1,0:T(8,128)(2,1)S(1)}, bf16[32,16,256]{2,1,0:T(8,128)(2,1)S(1)}, u32[]{:S(2)}, u32[]{:S(2)}) collective-permute-start(bf16[32,16,256]{2,1,0:T(8,128)(2,1)S(1)} %get-tuple-element.41), channel_id=1, source_target_pairs={{0,16},{16,0},{1,17},{17,1},{2,18},{18,2},{3,19},{19,3},{4,20},{20... | collective-permute-start | bytes 786440 | tf_op jit(solution)/shard_map/ppermute | solution.py:547
  11.5 0.6 %shard_map.103 = (f32[2,2,512,128]{3,2,1,0:T(8,128)S(1)}, bf16[32,16,256]{2,1,0:T(8,128)(2,1)S(1)}) custom-call(f32[2,2,512,128]{3,2,1,0:T(8,128)S(1)} %get-tuple-element.36._, f32[6,512,128]{2,1,0:T(8,128)S(1)} %get-tuple-element.37.mixed_ref, f32[512,512]{1,0:T(8,128)S(1)} %get-tuple-element.38.s_ref, ...), custom_call_target="tpu_custom_call", output_to_operand_aliasing={{0}: (0, {})} | custom-call | flops 100000000 | bytes 2097152 | tf_op jit(solution)/shard_map/pallas_call | solution.py:548
  12.1 0.8 %pad_maximum_fusion = bf16[32,32,256]{2,1,0:T(8,128)(2,1)} fusion(bf16[32,16,256]{2,1,0:T(8,128)(2,1)S(1)} %get-tuple-element.40), kind=kLoop, calls=%fused_computation | loop fusion | flops 1048576 | bytes 786432 | tf_op jit(solution)/shard_map/concatenate | solution.py:560
  13.0 0.0 collective-permute-done.2
  13.0 0.7 %constant_dynamic-update-slice_fusion = bf16[32,32,256]{2,1,0:T(8,128)(2,1)} fusion(bf16[32,32,256]{2,1,0:T(8,128)(2,1)} %pad_maximum_fusion, bf16[32,16,256]{2,1,0:T(8,128)(2,1)S(1)} %collective-permute-done.2, s32[]{:T(128)S(6)} %mul.3), kind=kLoop, calls=%fused_computation.6 | loop fusion | bytes 524292 | tf_op jit(solution)/shard_map/dynamic_update_slice | solution.py:562
  (3 shorter events, 0.0 us)
Async XLA Ops:
  0.0 2.3 %collective-permute-start = (bf16[32,32,256]{2,1,0:T(8,128)(2,1)}, bf16[32,32,256]{2,1,0:T(8,128)(2,1)S(1)}, u32[]{:S(2)}, u32[]{:S(2)}) collective-permute-start(bf16[32,32,256]{2,1,0:T(8,128)(2,1)} %own_hbm), channel_id=1, source_target_pairs={{0,16},{16,0},{1,17},{17,1},{2,18},{18,2},{3,19},{19,3},{4,20},{20... | collective-permute-start | bytes 1572872 | tf_op jit(solution)/shard_map/ppermute | solution.py:470
  2.4 3.7 %collective-permute-start.1 = (bf16[64,256]{1,0:T(8,128)(2,1)S(1)}, bf16[64,256]{1,0:T(8,128)(2,1)S(1)}, u32[]{:S(2)}, u32[]{:S(2)}) collective-permute-start(bf16[64,256]{1,0:T(8,128)(2,1)S(1)} %pad_maximum_fusion.1), channel_id=1, source_target_pairs={{16,1},{1,16},{17,2},{2,17},{18,3},{3,18},{19,4},{4,19},{20,5},{5,... | collective-permute-start | bytes 98312 | tf_op jit(solution)/shard_map/ppermute | solution.py:514
  7.3 5.6 %collective-permute-start.2 = (bf16[32,16,256]{2,1,0:T(8,128)(2,1)S(1)}, bf16[32,16,256]{2,1,0:T(8,128)(2,1)S(1)}, u32[]{:S(2)}, u32[]{:S(2)}) collective-permute-start(bf16[32,16,256]{2,1,0:T(8,128)(2,1)S(1)} %get-tuple-element.41), channel_id=1, source_target_pairs={{0,16},{16,0},{1,17},{17,1},{2,18},{18,2},{3,19},{19,3},{4,20},{20... | collective-permute-start | bytes 786440 | tf_op jit(solution)/shard_map/ppermute | solution.py:547

commit v16 on v15

--- a/solution.py
+++ b/solution.py
@@ -557,7 +557,7 @@
     )(out, edge_mixed, transforms_edge, bwd_v, w_out_v, spectrum)
     mine, late_core = lax.optimization_barrier((mine, core))
     offset = (1 - late_core) * part
-    both = jnp.concatenate([mine, mine], 1)
+    both = jnp.broadcast_to(mine[:, None], (rows, 2, part, width)).reshape(rows, cols, width)
     zero = jnp.int32(0)
     return lax.dynamic_update_slice_p.bind(both, theirs, zero, offset, zero)
 

time: 13.8 us -> 14.4 us (1.043)
  other arithmetic: 0.86 us -> 0.02 us
  local copies, waits for them, and re-layouts: 0.83 us -> 1.66 us
  waiting for transfers between devices: 0.01 us -> 0.58 us
    concatenate x1 -> x0, other arithmetic: 0.84 us -> none  [on_device(): both = jnp.concatenate([mine, mine], 1)]
    broadcast_in_dim x0 -> x1, local copies, waits for them, and re-layouts: none -> 0.83 us  [on_device(): jnp.broadcast_to(mine[:, None], (rows, 2, part, width))]
    ppermute x1, waiting for transfers between devices: 0.01 us -> 0.57 us  [on_device(): theirs = lax.ppermute(send, 'row', swap)]
  transfers between devices with their start and end apart: 3 -> 3, of which waited for: 0 -> 1; matrix products, arithmetic and copies ran while one was open for 6% -> 0% of each run, Pallas kernels for 39% -> 38%
where the time goes in v16:
time: 14.4 us; the launch traced here: 14.3 us
  Pallas kernels  6.58 us (46%)
  starting transfers between devices  5.32 us (37%)
  local copies, waits for them, and re-layouts  1.66 us (12%)
  waiting for transfers between devices  0.58 us (4%)
    ppermute x1, starting transfers between devices, on_device(): theirs = lax.ppermute(send, 'row', swap)  4.2 us
    pallas_call x1, Pallas kernels, on_device(): pl.pallas_call(inner_kernel, out_shape=(p_shape, mixed_shape, out_shape),...  3.01 us
    pallas_call x1, Pallas kernels, on_device(): pl.pallas_call(prep_kernel, out_shape=(p_shape, shape(w_in.shape, BF16),...  1.81 us
    pallas_call x1, Pallas kernels, on_device(): pl.pallas_call(edge_kernel, out_shape=(out_shape, mixed_shape, s_shape, h...  1.18 us
    broadcast_in_dim x1, local copies, waits for them, and re-layouts, on_device(): jnp.broadcast_to(mine[:, None], (rows, 2, part, width))  0.83 us
    dynamic_update_slice x1, local copies, waits for them, and re-layouts, on_device(): return lax.dynamic_update_slice_p.bind(both, theirs, zero, offset, zero)  0.72 us
    ppermute x1, starting transfers between devices, on_device(): lax.ppermute(jnp.concatenate([outer, column(0)], 0), ('row', 'col'), pairs)  0.66 us
    pallas_call x1, Pallas kernels, on_device(): pl.pallas_call(own_kernel, out_shape=(out_shape, half_shape), in_specs=[v...  0.58 us
  transfers between devices with their start and end apart: 3, of which 1 were waited for; matrix products, arithmetic and copies ran while one was open for 0% of the time, Pallas kernels for 38%

profile of v16, /device:TPU:0, one launch (start us, length us, event | category | flops | bytes accessed | tf_op | source)
XLA Modules:
  0.0 14.3 jit_solution(10158146430296157356)
XLA Ops:
  0.0 0.5 %collective-permute-start = (bf16[32,32,256]{2,1,0:T(8,128)(2,1)}, bf16[32,32,256]{2,1,0:T(8,128)(2,1)S(1)}, u32[]{:S(2)}, u32[]{:S(2)}) collective-permute-start(bf16[32,32,256]{2,1,0:T(8,128)(2,1)} %own_hbm), channel_id=1, source_target_pairs={{0,16},{16,0},{1,17},{17,1},{2,18},{18,2},{3,19},{19,3},{4,20},{20... | collective-permute-start | bytes 1572872 | tf_op jit(solution)/shard_map/ppermute | solution.py:470
  0.5 1.8 %shard_map.100 = (f32[6,824,128]{2,1,0:T(8,128)S(1)}, bf16[256,768]{1,0:T(8,128)(2,1)S(1)}, bf16[256,256]{1,0:T(8,128)(2,1)S(1)}, bf16[512,256]{1,0:T(8,128)(2,1...) custom-call(bf16[32,32,256]{2,1,0:T(8,128)(2,1)} %own_hbm, ...), custom_call_target="tpu_custom_call" | custom-call | bytes 3145728 | tf_op jit(solution)/shard_map/pallas_call | solution.py:475
  2.3 0.0 collective-permute-done.other_ref
  2.3 0.1 fusion.2
  2.4 0.7 %collective-permute-start.1 = (bf16[64,256]{1,0:T(8,128)(2,1)S(1)}, bf16[64,256]{1,0:T(8,128)(2,1)S(1)}, u32[]{:S(2)}, u32[]{:S(2)}) collective-permute-start(bf16[64,256]{1,0:T(8,128)(2,1)S(1)} %pad_maximum_fusion), channel_id=1, source_target_pairs={{16,1},{1,16},{17,2},{2,17},{18,3},{3,18},{19,4},{4,19},{20,5},{5,... | collective-permute-start | bytes 98312 | tf_op jit(solution)/shard_map/ppermute | solution.py:514
  3.1 3.0 %shard_map.101 = (f32[6,824,128]{2,1,0:T(8,128)S(1)}, f32[6,512,128]{2,1,0:T(8,128)S(1)}, f32[2,2,512,128]{3,2,1,0:T(8,128)S(1)}) custom-call(f32[6,824,128]{2,1,0:T(8,128)S(1)} %get-tuple-element.25._, bf16[32,32,256]{2,1,0:T(8,128)(2,1)S(1)} %collective-permute-done.other_ref, ...), custom_call_target="tpu_custom_call", output_to_operand_aliasing={{0}: (0, {})} | custom-call | flops 1000000000 | bytes 12582912 | tf_op jit(solution)/shard_map/pallas_call | solution.py:515
  6.1 0.0 collective-permute-done.1.halo_ref
  6.1 1.2 %shard_map.102 = (f32[2,2,512,128]{3,2,1,0:T(8,128)S(1)}, f32[6,512,128]{2,1,0:T(8,128)S(1)}, f32[512,512]{1,0:T(8,128)S(1)}, bf16[32,16,256]{2,1,0:T(8,128)(2,1)S(1)}) custom-call(f32[2,2,512,128]{3,2,1,0:T(8,128)S(1)} %get-tuple-element.33._, f32[6,512,128]{2,1,0:T(8,128)S(1)} %get-tuple-element.34.__, ...), custom_call_target="tpu_custom_call", output_to_operand_aliasing={{0}: (0, {}), {1}: (1, {})} | custom-call | flops 300000000 | bytes 4194304 | tf_op jit(solution)/shard_map/pallas_call | solution.py:533
  7.3 4.2 %collective-permute-start.2 = (bf16[32,16,256]{2,1,0:T(8,128)(2,1)S(1)}, bf16[32,16,256]{2,1,0:T(8,128)(2,1)S(1)}, u32[]{:S(2)}, u32[]{:S(2)}) collective-permute-start(bf16[32,16,256]{2,1,0:T(8,128)(2,1)S(1)} %get-tuple-element.41), channel_id=1, source_target_pairs={{0,16},{16,0},{1,17},{17,1},{2,18},{18,2},{3,19},{19,3},{4,20},{20... | collective-permute-start | bytes 786440 | tf_op jit(solution)/shard_map/ppermute | solution.py:547
  11.5 0.6 %shard_map.103 = (f32[2,2,512,128]{3,2,1,0:T(8,128)S(1)}, bf16[32,16,256]{2,1,0:T(8,128)(2,1)S(1)}) custom-call(f32[2,2,512,128]{3,2,1,0:T(8,128)S(1)} %get-tuple-element.36._, f32[6,512,128]{2,1,0:T(8,128)S(1)} %get-tuple-element.37.mixed_ref, f32[512,512]{1,0:T(8,128)S(1)} %get-tuple-element.38.s_ref, ...), custom_call_target="tpu_custom_call", output_to_operand_aliasing={{0}: (0, {})} | custom-call | flops 100000000 | bytes 2097152 | tf_op jit(solution)/shard_map/pallas_call | solution.py:548
  12.1 0.6 %collective-permute-done.2 = bf16[32,16,256]{2,1,0:T(8,128)(2,1)S(1)} collective-permute-done((bf16[32,16,256]{2,1,0:T(8,128)(2,1)S(1)}, bf16[32,16,256]{2,1,0:T(8,128)(2,1)S(1)}, u32[]{:S(2)}, u32[]{:S(2)}) %collective-permute-start.2) | collective-permute-done | bytes 262176 | tf_op jit(solution)/shard_map/ppermute | solution.py:547
  12.7 0.8 %broadcast_in_dim.10 = bf16[32,2,16,256]{3,2,1,0:T(8,128)(2,1)} broadcast(bf16[32,16,256]{2,1,0:T(8,128)(2,1)S(1)} %get-tuple-element.40), dimensions={0,2,3} | broadcast | bytes 786432 | tf_op jit(solution)/shard_map/broadcast_in_dim | solution.py:560
  13.5 0.7 %constant_dynamic-update-slice_fusion = bf16[32,32,256]{2,1,0:T(8,128)(2,1)} fusion(bf16[32,32,256]{2,1,0:T(8,128)(2,1)} %bitcast.6, bf16[32,16,256]{2,1,0:T(8,128)(2,1)S(1)} %collective-permute-done.2, s32[]{:T(128)S(6)} %mul.3), kind=kLoop, calls=%fused_computation.5 | loop fusion | bytes 524292 | tf_op jit(solution)/shard_map/dynamic_update_slice | solution.py:562
  (3 shorter events, 0.0 us)
Async XLA Ops:
  0.0 2.3 %collective-permute-start = (bf16[32,32,256]{2,1,0:T(8,128)(2,1)}, bf16[32,32,256]{2,1,0:T(8,128)(2,1)S(1)}, u32[]{:S(2)}, u32[]{:S(2)}) collective-permute-start(bf16[32,32,256]{2,1,0:T(8,128)(2,1)} %own_hbm), channel_id=1, source_target_pairs={{0,16},{16,0},{1,17},{17,1},{2,18},{18,2},{3,19},{19,3},{4,20},{20... | collective-permute-start | bytes 1572872 | tf_op jit(solution)/shard_map/ppermute | solution.py:470
  2.4 3.7 %collective-permute-start.1 = (bf16[64,256]{1,0:T(8,128)(2,1)S(1)}, bf16[64,256]{1,0:T(8,128)(2,1)S(1)}, u32[]{:S(2)}, u32[]{:S(2)}) collective-permute-start(bf16[64,256]{1,0:T(8,128)(2,1)S(1)} %pad_maximum_fusion), channel_id=1, source_target_pairs={{16,1},{1,16},{17,2},{2,17},{18,3},{3,18},{19,4},{4,19},{20,5},{5,... | collective-permute-start | bytes 98312 | tf_op jit(solution)/shard_map/ppermute | solution.py:514
  7.3 5.4 %collective-permute-start.2 = (bf16[32,16,256]{2,1,0:T(8,128)(2,1)S(1)}, bf16[32,16,256]{2,1,0:T(8,128)(2,1)S(1)}, u32[]{:S(2)}, u32[]{:S(2)}) collective-permute-start(bf16[32,16,256]{2,1,0:T(8,128)(2,1)S(1)} %get-tuple-element.41), channel_id=1, source_target_pairs={{0,16},{16,0},{1,17},{17,1},{2,18},{18,2},{3,19},{19,3},{4,20},{20... | collective-permute-start | bytes 786440 | tf_op jit(solution)/shard_map/ppermute | solution.py:547

commit v17 on v15

--- a/solution.py
+++ b/solution.py
@@ -361,8 +361,8 @@
         pass
 
 
-def finish_half(half, core, s_ref, mixed_ref, bwd_ref, w_out_ref, h_ref, z_ref, out_ref, to_ref):
-    rows, part, width = to_ref.shape
+def inverse_half(half, s_ref, bwd_ref, h_ref, z_ref):
+    rows, width = h_ref.shape[2:]
     block = rows * GROUP
     for k in range(0, rows, 2):
         parts = [[], []]
@@ -382,7 +382,11 @@
         for j in range(2):
             at = j * block + k * GROUP
             z_ref[at : at + 2 * GROUP, :] = jnp.concatenate(parts[j], 0).astype(BF16)
-    conv = jnp.dot(bwd_ref[...], z_ref[...], preferred_element_type=F32)
+    return jnp.dot(bwd_ref[...], z_ref[...], preferred_element_type=F32)
+
+
+def finish_half(half, core, conv, mixed_ref, w_out_ref, out_ref, to_ref):
+    rows, part, width = to_ref.shape
     columns = []
     for t in range(width // LANES):
         line = [
@@ -403,8 +407,8 @@
 
 def edge_kernel(
     _, __, halo_ref, w_in_ref, taps_ref, fwd_ref, bwd_ref, w_out_ref, h_ref,
-    out_ref, mixed_ref, s_ref, send_ref,
-    strip_ref, prod_ref, z_ref,
+    out_ref, mixed_ref, own_conv_ref, send_ref,
+    strip_ref, prod_ref, s_ref, z_ref, own_z_ref,
 ):
     core = lax.axis_index("row")
     rows, part, width = send_ref.shape
@@ -429,18 +433,14 @@
                     two, 0
                 ).astype(BF16)
     s_ref[...] = jnp.dot(fwd_ref[...], prod_ref[...], preferred_element_type=F32)
-    finish_half(
-        1 - core, core, s_ref, mixed_ref, bwd_ref, w_out_ref, h_ref, z_ref, out_ref, send_ref
-    )
-
-
-def own_kernel(
-    _, mixed_ref, s_ref, bwd_ref, w_out_ref, h_ref,
-    out_ref, mine_ref,
-    z_ref,
-):
+    conv = inverse_half(1 - core, s_ref, bwd_ref, h_ref, z_ref)
+    own_conv_ref[...] = inverse_half(core, s_ref, bwd_ref, h_ref, own_z_ref)
+    finish_half(1 - core, core, conv, mixed_ref, w_out_ref, out_ref, send_ref)
+
+
+def own_kernel(_, mixed_ref, conv_ref, w_out_ref, out_ref, mine_ref):
     core = lax.axis_index("row")
-    finish_half(core, core, s_ref, mixed_ref, bwd_ref, w_out_ref, h_ref, z_ref, out_ref, mine_ref)
+    finish_half(core, core, conv_ref, mixed_ref, w_out_ref, out_ref, mine_ref)
 
 
 def on_device(image_tokens, w_in, conv_kernel, conv_bias, long_filter, skip_gain, w_out):
@@ -528,17 +528,19 @@
         cost_estimate=pl.CostEstimate(flops=10**9, bytes_accessed=12 * 1024 * 1024, transcendentals=0),
     )(projected, other, column(part), w_in_v, taps, fwd_v, bwd_v, w_out_v, spectrum)
     half_shape = shape((rows, part, width), BF16)
-    s_shape = shape((2 * rows * GROUP, 2 * width), F32)
+    conv_shape = shape((rows * GROUP, width), F32)
     z_scratch = pltpu.VMEM((2 * rows * GROUP, width), BF16)
-    out, edge_mixed, transforms_edge, send = pl.pallas_call(
+    out, edge_mixed, own_conv, send = pl.pallas_call(
         edge_kernel,
-        out_shape=(out_shape, mixed_shape, s_shape, half_shape),
+        out_shape=(out_shape, mixed_shape, conv_shape, half_shape),
         in_specs=[vmem] * 9,
         out_specs=(vmem,) * 4,
         input_output_aliases={0: 0, 1: 1},
         scratch_shapes=[
             pltpu.VMEM((3 * width // LANES, 2 * height + 8, LANES), F32),
             pltpu.VMEM((rows * GROUP, 2 * width), BF16),
+            pltpu.VMEM((2 * rows * GROUP, 2 * width), F32),
+            z_scratch,
             z_scratch,
         ],
         compiler_params=limit,
@@ -548,13 +550,12 @@
     _, mine = pl.pallas_call(
         own_kernel,
         out_shape=(out_shape, half_shape),
-        in_specs=[vmem] * 6,
+        in_specs=[vmem] * 4,
         out_specs=(vmem,) * 2,
         input_output_aliases={0: 0},
-        scratch_shapes=[z_scratch],
         compiler_params=limit,
         cost_estimate=pl.CostEstimate(flops=10**8, bytes_accessed=2 * 1024 * 1024, transcendentals=0),
-    )(out, edge_mixed, transforms_edge, bwd_v, w_out_v, spectrum)
+    )(out, edge_mixed, own_conv, w_out_v)
     mine, late_core = lax.optimization_barrier((mine, core))
     offset = (1 - late_core) * part
     both = jnp.concatenate([mine, mine], 1)

time: 13.8 us -> 13.8 us (level)
    pallas_call x1, Pallas kernels: 0.58 us -> 0.24 us  [on_device(): pl.pallas_call(own_kernel, out_shape=(out_shape, half_shape), in_specs=[v...]
    pallas_call x1, Pallas kernels: 1.18 us -> 1.44 us  [on_device(): pl.pallas_call(edge_kernel, out_shape=(out_shape, mixed_shape, conv_shape...]
  transfers between devices with their start and end apart: 3 -> 3, of which waited for: 0 -> 1; matrix products, arithmetic and copies ran while one was open for 6% -> 6% of each run, Pallas kernels for 39% -> 37%
where the time goes in v17:
time: 13.8 us; the launch traced here: 13.7 us
  Pallas kernels  6.52 us (47%)
  starting transfers between devices  5.32 us (39%)
  other arithmetic  0.86 us (6%)
  local copies, waits for them, and re-layouts  0.83 us (6%)
    ppermute x1, starting transfers between devices, on_device(): theirs = lax.ppermute(send, 'row', swap)  4.2 us
    pallas_call x1, Pallas kernels, on_device(): pl.pallas_call(inner_kernel, out_shape=(p_shape, mixed_shape, out_shape),...  3.03 us
    pallas_call x1, Pallas kernels, on_device(): pl.pallas_call(prep_kernel, out_shape=(p_shape, shape(w_in.shape, BF16),...  1.81 us
    pallas_call x1, Pallas kernels, on_device(): pl.pallas_call(edge_kernel, out_shape=(out_shape, mixed_shape, conv_shape...  1.44 us
    concatenate x1, other arithmetic, on_device(): both = jnp.concatenate([mine, mine], 1)  0.84 us
    dynamic_update_slice x1, local copies, waits for them, and re-layouts, on_device(): return lax.dynamic_update_slice_p.bind(both, theirs, zero, offset, zero)  0.72 us
    ppermute x1, starting transfers between devices, on_device(): lax.ppermute(jnp.concatenate([outer, column(0)], 0), ('row', 'col'), pairs)  0.66 us
    ppermute x1, starting transfers between devices, on_device(): lax.ppermute(image_tokens, 'row', swap)  0.45 us
  transfers between devices with their start and end apart: 3, of which 1 were waited for; matrix products, arithmetic and copies ran while one was open for 6% of the time, Pallas kernels for 37%

profile of v17, /device:TPU:0, one launch (start us, length us, event | category | flops | bytes accessed | tf_op | source)
XLA Modules:
  0.0 13.7 jit_solution(5701291277886090596)
XLA Ops:
  0.0 0.5 %collective-permute-start = (bf16[32,32,256]{2,1,0:T(8,128)(2,1)}, bf16[32,32,256]{2,1,0:T(8,128)(2,1)S(1)}, u32[]{:S(2)}, u32[]{:S(2)}) collective-permute-start(bf16[32,32,256]{2,1,0:T(8,128)(2,1)} %own_hbm), channel_id=1, source_target_pairs={{0,16},{16,0},{1,17},{17,1},{2,18},{18,2},{3,19},{19,3},{4,20},{20... | collective-permute-start | bytes 1572872 | tf_op jit(solution)/shard_map/ppermute | solution.py:470
  0.5 1.8 %shard_map.100 = (f32[6,824,128]{2,1,0:T(8,128)S(1)}, bf16[256,768]{1,0:T(8,128)(2,1)S(1)}, bf16[256,256]{1,0:T(8,128)(2,1)S(1)}, bf16[512,256]{1,0:T(8,128)(2,1...) custom-call(bf16[32,32,256]{2,1,0:T(8,128)(2,1)} %own_hbm, ...), custom_call_target="tpu_custom_call" | custom-call | bytes 3145728 | tf_op jit(solution)/shard_map/pallas_call | solution.py:475
  2.3 0.0 collective-permute-done.other_ref
  2.3 0.1 fusion.2
  2.4 0.7 %collective-permute-start.1 = (bf16[64,256]{1,0:T(8,128)(2,1)S(1)}, bf16[64,256]{1,0:T(8,128)(2,1)S(1)}, u32[]{:S(2)}, u32[]{:S(2)}) collective-permute-start(bf16[64,256]{1,0:T(8,128)(2,1)S(1)} %pad_maximum_fusion.1), channel_id=1, source_target_pairs={{16,1},{1,16},{17,2},{2,17},{18,3},{3,18},{19,4},{4,19},{20,5},{5,... | collective-permute-start | bytes 98312 | tf_op jit(solution)/shard_map/ppermute | solution.py:514
  3.1 3.0 %shard_map.101 = (f32[6,824,128]{2,1,0:T(8,128)S(1)}, f32[6,512,128]{2,1,0:T(8,128)S(1)}, f32[2,2,512,128]{3,2,1,0:T(8,128)S(1)}) custom-call(f32[6,824,128]{2,1,0:T(8,128)S(1)} %get-tuple-element.25._, bf16[32,32,256]{2,1,0:T(8,128)(2,1)S(1)} %collective-permute-done.other_ref, ...), custom_call_target="tpu_custom_call", output_to_operand_aliasing={{0}: (0, {})} | custom-call | flops 1000000000 | bytes 12582912 | tf_op jit(solution)/shard_map/pallas_call | solution.py:515
  6.2 0.0 collective-permute-done.1.halo_ref
  6.2 1.4 %shard_map.102 = (f32[2,2,512,128]{3,2,1,0:T(8,128)S(1)}, f32[6,512,128]{2,1,0:T(8,128)S(1)}, f32[256,256]{1,0:T(8,128)S(1)}, bf16[32,16,256]{2,1,0:T(8,128)(2,1)S(1)}) custom-call(f32[2,2,512,128]{3,2,1,0:T(8,128)S(1)} %get-tuple-element.33._, f32[6,512,128]{2,1,0:T(8,128)S(1)} %get-tuple-element.34.__, ...), custom_call_target="tpu_custom_call", output_to_operand_aliasing={{0}: (0, {}), {1}: (1, {})} | custom-call | flops 300000000 | bytes 4194304 | tf_op jit(solution)/shard_map/pallas_call | solution.py:533
  7.6 4.2 %collective-permute-start.2 = (bf16[32,16,256]{2,1,0:T(8,128)(2,1)S(1)}, bf16[32,16,256]{2,1,0:T(8,128)(2,1)S(1)}, u32[]{:S(2)}, u32[]{:S(2)}) collective-permute-start(bf16[32,16,256]{2,1,0:T(8,128)(2,1)S(1)} %get-tuple-element.41), channel_id=1, source_target_pairs={{0,16},{16,0},{1,17},{17,1},{2,18},{18,2},{3,19},{19,3},{4,20},{20... | collective-permute-start | bytes 786440 | tf_op jit(solution)/shard_map/ppermute | solution.py:549
  11.8 0.2 %shard_map.103 = (f32[2,2,512,128]{3,2,1,0:T(8,128)S(1)}, bf16[32,16,256]{2,1,0:T(8,128)(2,1)S(1)}) custom-call(f32[2,2,512,128]{3,2,1,0:T(8,128)S(1)} %get-tuple-element.36._, f32[6,512,128]{2,1,0:T(8,128)S(1)} %get-tuple-element.37.mixed_ref, f32[256,256]{1,0:T(8,128)S(1)} %get-tuple-element.38.conv_ref, ...), custom_call_target="tpu_custom_call", output_to_operand_aliasing={{0}: (0, {})} | custom-call | flops 100000000 | bytes 2097152 | tf_op jit(solution)/shard_map/pallas_call | solution.py:550
  12.1 0.8 %pad_maximum_fusion = bf16[32,32,256]{2,1,0:T(8,128)(2,1)} fusion(bf16[32,16,256]{2,1,0:T(8,128)(2,1)S(1)} %get-tuple-element.40), kind=kLoop, calls=%fused_computation | loop fusion | flops 1048576 | bytes 786432 | tf_op jit(solution)/shard_map/concatenate | solution.py:561
  12.9 0.1 collective-permute-done.2
  13.0 0.7 %constant_dynamic-update-slice_fusion = bf16[32,32,256]{2,1,0:T(8,128)(2,1)} fusion(bf16[32,32,256]{2,1,0:T(8,128)(2,1)} %pad_maximum_fusion, bf16[32,16,256]{2,1,0:T(8,128)(2,1)S(1)} %collective-permute-done.2, s32[]{:T(128)S(6)} %mul.3), kind=kLoop, calls=%fused_computation.6 | loop fusion | bytes 524292 | tf_op jit(solution)/shard_map/dynamic_update_slice | solution.py:563
  (3 shorter events, 0.0 us)
Async XLA Ops:
  0.0 2.3 %collective-permute-start = (bf16[32,32,256]{2,1,0:T(8,128)(2,1)}, bf16[32,32,256]{2,1,0:T(8,128)(2,1)S(1)}, u32[]{:S(2)}, u32[]{:S(2)}) collective-permute-start(bf16[32,32,256]{2,1,0:T(8,128)(2,1)} %own_hbm), channel_id=1, source_target_pairs={{0,16},{16,0},{1,17},{17,1},{2,18},{18,2},{3,19},{19,3},{4,20},{20... | collective-permute-start | bytes 1572872 | tf_op jit(solution)/shard_map/ppermute | solution.py:470
  2.4 3.7 %collective-permute-start.1 = (bf16[64,256]{1,0:T(8,128)(2,1)S(1)}, bf16[64,256]{1,0:T(8,128)(2,1)S(1)}, u32[]{:S(2)}, u32[]{:S(2)}) collective-permute-start(bf16[64,256]{1,0:T(8,128)(2,1)S(1)} %pad_maximum_fusion.1), channel_id=1, source_target_pairs={{16,1},{1,16},{17,2},{2,17},{18,3},{3,18},{19,4},{4,19},{20,5},{5,... | collective-permute-start | bytes 98312 | tf_op jit(solution)/shard_map/ppermute | solution.py:514
  7.6 5.4 %collective-permute-start.2 = (bf16[32,16,256]{2,1,0:T(8,128)(2,1)S(1)}, bf16[32,16,256]{2,1,0:T(8,128)(2,1)S(1)}, u32[]{:S(2)}, u32[]{:S(2)}) collective-permute-start(bf16[32,16,256]{2,1,0:T(8,128)(2,1)S(1)} %get-tuple-element.41), channel_id=1, source_target_pairs={{0,16},{16,0},{1,17},{17,1},{2,18},{18,2},{3,19},{19,3},{4,20},{20... | collective-permute-start | bytes 786440 | tf_op jit(solution)/shard_map/ppermute | solution.py:549

commit v18 on v10

--- a/solution.py
+++ b/solution.py
@@ -352,7 +352,7 @@
         fwd_ref, bwd_ref, w_out_ref, h_ref, prod_ref, z_ref, put,
     )
     for _ in conv:
-        for _ in range(5):
+        for _ in range(8):
             next(steps, None)
     for _ in steps:
         pass
@@ -464,8 +464,8 @@
         scratch_shapes=[
             pltpu.VMEM(p_shape.shape, F32),
             pltpu.VMEM(mixed_shape.shape, F32),
-            pltpu.VMEM((width // LANES, rows * GROUP, 2 * LANES), BF16),
-            pltpu.VMEM((width // LANES, 2 * rows * GROUP, 2 * LANES), BF16),
+            pltpu.VMEM((1, rows * GROUP, 2 * width), BF16),
+            pltpu.VMEM((1, 2 * rows * GROUP, 2 * width), BF16),
         ],
         compiler_params=limit,
         cost_estimate=pl.CostEstimate(flops=10**9, bytes_accessed=12 * 1024 * 1024, transcendentals=0),

time: 13.8 us -> 13.7 us (level)
  transfers between devices with their start and end apart: 3 -> 3, of which waited for: 1 -> 1; matrix products, arithmetic and copies ran while one was open for 6% -> 6% of each run, Pallas kernels for 36% -> 35%
where the time goes in v18:
time: 13.7 us; the launch traced here: 13.6 us
  Pallas kernels  6.16 us (45%)
  starting transfers between devices  5.34 us (39%)
  other arithmetic  0.86 us (6%)
  local copies, waits for them, and re-layouts  0.83 us (6%)
  waiting for transfers between devices  0.33 us (2%)
    ppermute x1, starting transfers between devices, on_device(): theirs = lax.ppermute(send, 'row', swap)  4.23 us
    pallas_call x1, Pallas kernels, on_device(): pl.pallas_call(inner_kernel, out_shape=(p_shape, mixed_shape, out_shape),...  2.99 us
    pallas_call x1, Pallas kernels, on_device(): pl.pallas_call(prep_kernel, out_shape=(p_shape, shape(w_in.shape, BF16),...  1.81 us
    pallas_call x1, Pallas kernels, on_device(): pl.pallas_call(edge_kernel, out_shape=(out_shape, mixed_shape, half_shape...  1.36 us
    concatenate x1, other arithmetic, on_device(): both = jnp.concatenate([mine, mine], 1)  0.83 us
    dynamic_update_slice x1, local copies, waits for them, and re-layouts, on_device(): return lax.dynamic_update_slice_in_dim(both, theirs, (1 - core) * part, 1)  0.72 us
    ppermute x1, starting transfers between devices, on_device(): lax.ppermute(jnp.concatenate([outer, column(0)], 0), ('row', 'col'), pairs)  0.66 us
    ppermute x1, starting transfers between devices, on_device(): lax.ppermute(image_tokens, 'row', swap)  0.45 us
  transfers between devices with their start and end apart: 3, of which 1 were waited for; matrix products, arithmetic and copies ran while one was open for 6% of the time, Pallas kernels for 35%

profile of v18, /device:TPU:0, one launch (start us, length us, event | category | flops | bytes accessed | tf_op | source)
XLA Modules:
  0.0 13.6 jit_solution(16372776914375129918)
XLA Ops:
  0.0 0.5 %collective-permute-start = (bf16[32,32,256]{2,1,0:T(8,128)(2,1)}, bf16[32,32,256]{2,1,0:T(8,128)(2,1)S(1)}, u32[]{:S(2)}, u32[]{:S(2)}) collective-permute-start(bf16[32,32,256]{2,1,0:T(8,128)(2,1)} %own_hbm), channel_id=1, source_target_pairs={{0,16},{16,0},{1,17},{17,1},{2,18},{18,2},{3,19},{19,3},{4,20},{20... | collective-permute-start | bytes 1572872 | tf_op jit(solution)/shard_map/ppermute | solution.py:413
  0.5 1.8 %shard_map.100 = (f32[6,824,128]{2,1,0:T(8,128)S(1)}, bf16[256,768]{1,0:T(8,128)(2,1)S(1)}, bf16[256,256]{1,0:T(8,128)(2,1)S(1)}, bf16[512,256]{1,0:T(8,128)(2,1...) custom-call(bf16[32,32,256]{2,1,0:T(8,128)(2,1)} %own_hbm, ...), custom_call_target="tpu_custom_call" | custom-call | bytes 3145728 | tf_op jit(solution)/shard_map/pallas_call | solution.py:418
  2.3 0.0 collective-permute-done.other_ref
  2.3 0.1 fusion.2
  2.4 0.7 %collective-permute-start.1 = (bf16[64,256]{1,0:T(8,128)(2,1)S(1)}, bf16[64,256]{1,0:T(8,128)(2,1)S(1)}, u32[]{:S(2)}, u32[]{:S(2)}) collective-permute-start(bf16[64,256]{1,0:T(8,128)(2,1)S(1)} %pad_maximum_fusion.1), channel_id=1, source_target_pairs={{16,1},{1,16},{17,2},{2,17},{18,3},{3,18},{19,4},{4,19},{20,5},{5,... | collective-permute-start | bytes 98312 | tf_op jit(solution)/shard_map/ppermute | solution.py:457
  3.1 3.0 %shard_map.101 = (f32[6,824,128]{2,1,0:T(8,128)S(1)}, f32[6,512,128]{2,1,0:T(8,128)S(1)}, f32[2,2,512,128]{3,2,1,0:T(8,128)S(1)}) custom-call(f32[6,824,128]{2,1,0:T(8,128)S(1)} %get-tuple-element.17._, bf16[32,32,256]{2,1,0:T(8,128)(2,1)S(1)} %collective-permute-done.other_ref, ...), custom_call_target="tpu_custom_call", output_to_operand_aliasing={{0}: (0, {})} | custom-call | flops 1000000000 | bytes 12582912 | tf_op jit(solution)/shard_map/pallas_call | solution.py:458
  6.1 0.0 collective-permute-done.1.halo_ref
  6.1 1.4 %shard_map.102 = (f32[2,2,512,128]{3,2,1,0:T(8,128)S(1)}, f32[6,512,128]{2,1,0:T(8,128)S(1)}, bf16[32,16,256]{2,1,0:T(8,128)(2,1)S(1)}, bf16[32,16,256]{2,1,0:T(8,128)(2,1)S(1)}) custom-call(f32[2,2,512,128]{3,2,1,0:T(8,128)S(1)} %get-tuple-element.24._, f32[6,512,128]{2,1,0:T(8,128)S(1)} %get-tuple-element.25.__, ...), custom_call_target="tpu_custom_call", output_to_operand_aliasing={{0}: (0, {}), {1}: (1, {})} | custom-call | flops 300000000 | bytes 4194304 | tf_op jit(solution)/shard_map/pallas_call | solution.py:474
  7.5 4.2 %collective-permute-start.2 = (bf16[32,16,256]{2,1,0:T(8,128)(2,1)S(1)}, bf16[32,16,256]{2,1,0:T(8,128)(2,1)S(1)}, u32[]{:S(2)}, u32[]{:S(2)}) collective-permute-start(bf16[32,16,256]{2,1,0:T(8,128)(2,1)S(1)} %get-tuple-element.28), channel_id=1, source_target_pairs={{0,16},{16,0},{1,17},{17,1},{2,18},{18,2},{3,19},{19,3},{4,20},{20... | collective-permute-start | bytes 786440 | tf_op jit(solution)/shard_map/ppermute | solution.py:488
  11.7 0.8 %pad_maximum_fusion = bf16[32,32,256]{2,1,0:T(8,128)(2,1)} fusion(bf16[32,16,256]{2,1,0:T(8,128)(2,1)S(1)} %get-tuple-element.27), kind=kLoop, calls=%fused_computation | loop fusion | flops 1048576 | bytes 786432 | tf_op jit(solution)/shard_map/concatenate | solution.py:489
  12.6 0.3 %collective-permute-done.2 = bf16[32,16,256]{2,1,0:T(8,128)(2,1)S(1)} collective-permute-done((bf16[32,16,256]{2,1,0:T(8,128)(2,1)S(1)}, bf16[32,16,256]{2,1,0:T(8,128)(2,1)S(1)}, u32[]{:S(2)}, u32[]{:S(2)}) %collective-permute-start.2) | collective-permute-done | bytes 262176 | tf_op jit(solution)/shard_map/ppermute | solution.py:488
  12.9 0.7 %constant_dynamic-update-slice_fusion = bf16[32,32,256]{2,1,0:T(8,128)(2,1)} fusion(bf16[32,32,256]{2,1,0:T(8,128)(2,1)} %pad_maximum_fusion, bf16[32,16,256]{2,1,0:T(8,128)(2,1)S(1)} %collective-permute-done.2, s32[]{:T(128)S(6)} %select_n.25), kind=kLoop, calls=%fused_computation.6 | loop fusion | bytes 524292 | tf_op jit(solution)/shard_map/dynamic_update_slice | solution.py:490
  (3 shorter events, 0.0 us)
Async XLA Ops:
  0.0 2.3 %collective-permute-start = (bf16[32,32,256]{2,1,0:T(8,128)(2,1)}, bf16[32,32,256]{2,1,0:T(8,128)(2,1)S(1)}, u32[]{:S(2)}, u32[]{:S(2)}) collective-permute-start(bf16[32,32,256]{2,1,0:T(8,128)(2,1)} %own_hbm), channel_id=1, source_target_pairs={{0,16},{16,0},{1,17},{17,1},{2,18},{18,2},{3,19},{19,3},{4,20},{20... | collective-permute-start | bytes 1572872 | tf_op jit(solution)/shard_map/ppermute | solution.py:413
  2.4 3.7 %collective-permute-start.1 = (bf16[64,256]{1,0:T(8,128)(2,1)S(1)}, bf16[64,256]{1,0:T(8,128)(2,1)S(1)}, u32[]{:S(2)}, u32[]{:S(2)}) collective-permute-start(bf16[64,256]{1,0:T(8,128)(2,1)S(1)} %pad_maximum_fusion.1), channel_id=1, source_target_pairs={{16,1},{1,16},{17,2},{2,17},{18,3},{3,18},{19,4},{4,19},{20,5},{5,... | collective-permute-start | bytes 98312 | tf_op jit(solution)/shard_map/ppermute | solution.py:457
  7.5 5.4 %collective-permute-start.2 = (bf16[32,16,256]{2,1,0:T(8,128)(2,1)S(1)}, bf16[32,16,256]{2,1,0:T(8,128)(2,1)S(1)}, u32[]{:S(2)}, u32[]{:S(2)}) collective-permute-start(bf16[32,16,256]{2,1,0:T(8,128)(2,1)S(1)} %get-tuple-element.28), channel_id=1, source_target_pairs={{0,16},{16,0},{1,17},{17,1},{2,18},{18,2},{3,19},{19,3},{4,20},{20... | collective-permute-start | bytes 786440 | tf_op jit(solution)/shard_map/ppermute | solution.py:488

commit v19 on v10

--- a/solution.py
+++ b/solution.py
@@ -331,12 +331,9 @@
     for _ in inner(p_ref, own_at, (1 - core) * (n_chunk - 1)):
         pass
 
-    def inner_chunk(i, carry):
+    for i in range(n_chunk):
         for _ in inner(q_ref, other_at, i):
             pass
-        return carry
-
-    lax.fori_loop(0, n_chunk, inner_chunk, 0)
 
     def put(final):
         interleave(out_ref, final, 1 - core)

time: 13.8 us -> 14.4 us (1.043)
  Pallas kernels: 6.2 us -> 6.77 us
    pallas_call x1, Pallas kernels: 3.03 us -> 3.61 us  [on_device(): pl.pallas_call(inner_kernel, out_shape=(p_shape, mixed_shape, out_shape),...]
  transfers between devices with their start and end apart: 3 -> 3, of which waited for: 1 -> 1; matrix products, arithmetic and copies ran while one was open for 6% -> 6% of each run, Pallas kernels for 36% -> 38%
where the time goes in v19:
time: 14.4 us; the launch traced here: 14.2 us
  Pallas kernels  6.77 us (47%)
  starting transfers between devices  5.35 us (37%)
  other arithmetic  0.86 us (6%)
  local copies, waits for them, and re-layouts  0.83 us (6%)
  waiting for transfers between devices  0.33 us (2%)
    ppermute x1, starting transfers between devices, on_device(): theirs = lax.ppermute(send, 'row', swap)  4.24 us
    pallas_call x1, Pallas kernels, on_device(): pl.pallas_call(inner_kernel, out_shape=(p_shape, mixed_shape, out_shape),...  3.61 us
    pallas_call x1, Pallas kernels, on_device(): pl.pallas_call(prep_kernel, out_shape=(p_shape, shape(w_in.shape, BF16),...  1.81 us
    pallas_call x1, Pallas kernels, on_device(): pl.pallas_call(edge_kernel, out_shape=(out_shape, mixed_shape, half_shape...  1.36 us
    concatenate x1, other arithmetic, on_device(): both = jnp.concatenate([mine, mine], 1)  0.83 us
    dynamic_update_slice x1, local copies, waits for them, and re-layouts, on_device(): return lax.dynamic_update_slice_in_dim(both, theirs, (1 - core) * part, 1)  0.72 us
    ppermute x1, starting transfers between devices, on_device(): lax.ppermute(jnp.concatenate([outer, column(0)], 0), ('row', 'col'), pairs)  0.66 us
    ppermute x1, starting transfers between devices, on_device(): lax.ppermute(image_tokens, 'row', swap)  0.45 us
  transfers between devices with their start and end apart: 3, of which 1 were waited for; matrix products, arithmetic and copies ran while one was open for 6% of the time, Pallas kernels for 38%

profile of v19, /device:TPU:0, one launch (start us, length us, event | category | flops | bytes accessed | tf_op | source)
XLA Modules:
  0.0 14.2 jit_solution(16731386446819327735)
XLA Ops:
  0.0 0.5 %collective-permute-start = (bf16[32,32,256]{2,1,0:T(8,128)(2,1)}, bf16[32,32,256]{2,1,0:T(8,128)(2,1)S(1)}, u32[]{:S(2)}, u32[]{:S(2)}) collective-permute-start(bf16[32,32,256]{2,1,0:T(8,128)(2,1)} %own_hbm), channel_id=1, source_target_pairs={{0,16},{16,0},{1,17},{17,1},{2,18},{18,2},{3,19},{19,3},{4,20},{20... | collective-permute-start | bytes 1572872 | tf_op jit(solution)/shard_map/ppermute | solution.py:410
  0.5 1.8 %shard_map.100 = (f32[6,824,128]{2,1,0:T(8,128)S(1)}, bf16[256,768]{1,0:T(8,128)(2,1)S(1)}, bf16[256,256]{1,0:T(8,128)(2,1)S(1)}, bf16[512,256]{1,0:T(8,128)(2,1...) custom-call(bf16[32,32,256]{2,1,0:T(8,128)(2,1)} %own_hbm, ...), custom_call_target="tpu_custom_call" | custom-call | bytes 3145728 | tf_op jit(solution)/shard_map/pallas_call | solution.py:415
  2.3 0.0 collective-permute-done.other_ref
  2.3 0.1 fusion.2
  2.4 0.7 %collective-permute-start.1 = (bf16[64,256]{1,0:T(8,128)(2,1)S(1)}, bf16[64,256]{1,0:T(8,128)(2,1)S(1)}, u32[]{:S(2)}, u32[]{:S(2)}) collective-permute-start(bf16[64,256]{1,0:T(8,128)(2,1)S(1)} %pad_maximum_fusion.1), channel_id=1, source_target_pairs={{16,1},{1,16},{17,2},{2,17},{18,3},{3,18},{19,4},{4,19},{20,5},{5,... | collective-permute-start | bytes 98312 | tf_op jit(solution)/shard_map/ppermute | solution.py:454
  3.1 3.6 %shard_map.101 = (f32[6,824,128]{2,1,0:T(8,128)S(1)}, f32[6,512,128]{2,1,0:T(8,128)S(1)}, f32[2,2,512,128]{3,2,1,0:T(8,128)S(1)}) custom-call(f32[6,824,128]{2,1,0:T(8,128)S(1)} %get-tuple-element.17._, bf16[32,32,256]{2,1,0:T(8,128)(2,1)S(1)} %collective-permute-done.other_ref, ...), custom_call_target="tpu_custom_call", output_to_operand_aliasing={{0}: (0, {})} | custom-call | flops 1000000000 | bytes 12582912 | tf_op jit(solution)/shard_map/pallas_call | solution.py:455
  6.7 0.0 collective-permute-done.1.halo_ref
  6.7 1.4 %shard_map.102 = (f32[2,2,512,128]{3,2,1,0:T(8,128)S(1)}, f32[6,512,128]{2,1,0:T(8,128)S(1)}, bf16[32,16,256]{2,1,0:T(8,128)(2,1)S(1)}, bf16[32,16,256]{2,1,0:T(8,128)(2,1)S(1)}) custom-call(f32[2,2,512,128]{3,2,1,0:T(8,128)S(1)} %get-tuple-element.24._, f32[6,512,128]{2,1,0:T(8,128)S(1)} %get-tuple-element.25.__, ...), custom_call_target="tpu_custom_call", output_to_operand_aliasing={{0}: (0, {}), {1}: (1, {})} | custom-call | flops 300000000 | bytes 4194304 | tf_op jit(solution)/shard_map/pallas_call | solution.py:471
  8.1 4.2 %collective-permute-start.2 = (bf16[32,16,256]{2,1,0:T(8,128)(2,1)S(1)}, bf16[32,16,256]{2,1,0:T(8,128)(2,1)S(1)}, u32[]{:S(2)}, u32[]{:S(2)}) collective-permute-start(bf16[32,16,256]{2,1,0:T(8,128)(2,1)S(1)} %get-tuple-element.28), channel_id=1, source_target_pairs={{0,16},{16,0},{1,17},{17,1},{2,18},{18,2},{3,19},{19,3},{4,20},{20... | collective-permute-start | bytes 786440 | tf_op jit(solution)/shard_map/ppermute | solution.py:485
  12.3 0.8 %pad_maximum_fusion = bf16[32,32,256]{2,1,0:T(8,128)(2,1)} fusion(bf16[32,16,256]{2,1,0:T(8,128)(2,1)S(1)} %get-tuple-element.27), kind=kLoop, calls=%fused_computation | loop fusion | flops 1048576 | bytes 786432 | tf_op jit(solution)/shard_map/concatenate | solution.py:486
  13.2 0.3 %collective-permute-done.2 = bf16[32,16,256]{2,1,0:T(8,128)(2,1)S(1)} collective-permute-done((bf16[32,16,256]{2,1,0:T(8,128)(2,1)S(1)}, bf16[32,16,256]{2,1,0:T(8,128)(2,1)S(1)}, u32[]{:S(2)}, u32[]{:S(2)}) %collective-permute-start.2) | collective-permute-done | bytes 262176 | tf_op jit(solution)/shard_map/ppermute | solution.py:485
  13.5 0.7 %constant_dynamic-update-slice_fusion = bf16[32,32,256]{2,1,0:T(8,128)(2,1)} fusion(bf16[32,32,256]{2,1,0:T(8,128)(2,1)} %pad_maximum_fusion, bf16[32,16,256]{2,1,0:T(8,128)(2,1)S(1)} %collective-permute-done.2, s32[]{:T(128)S(6)} %select_n.25), kind=kLoop, calls=%fused_computation.6 | loop fusion | bytes 524292 | tf_op jit(solution)/shard_map/dynamic_update_slice | solution.py:487
  (3 shorter events, 0.0 us)
Async XLA Ops:
  0.0 2.3 %collective-permute-start = (bf16[32,32,256]{2,1,0:T(8,128)(2,1)}, bf16[32,32,256]{2,1,0:T(8,128)(2,1)S(1)}, u32[]{:S(2)}, u32[]{:S(2)}) collective-permute-start(bf16[32,32,256]{2,1,0:T(8,128)(2,1)} %own_hbm), channel_id=1, source_target_pairs={{0,16},{16,0},{1,17},{17,1},{2,18},{18,2},{3,19},{19,3},{4,20},{20... | collective-permute-start | bytes 1572872 | tf_op jit(solution)/shard_map/ppermute | solution.py:410
  2.4 4.3 %collective-permute-start.1 = (bf16[64,256]{1,0:T(8,128)(2,1)S(1)}, bf16[64,256]{1,0:T(8,128)(2,1)S(1)}, u32[]{:S(2)}, u32[]{:S(2)}) collective-permute-start(bf16[64,256]{1,0:T(8,128)(2,1)S(1)} %pad_maximum_fusion.1), channel_id=1, source_target_pairs={{16,1},{1,16},{17,2},{2,17},{18,3},{3,18},{19,4},{4,19},{20,5},{5,... | collective-permute-start | bytes 98312 | tf_op jit(solution)/shard_map/ppermute | solution.py:454
  8.1 5.4 %collective-permute-start.2 = (bf16[32,16,256]{2,1,0:T(8,128)(2,1)S(1)}, bf16[32,16,256]{2,1,0:T(8,128)(2,1)S(1)}, u32[]{:S(2)}, u32[]{:S(2)}) collective-permute-start(bf16[32,16,256]{2,1,0:T(8,128)(2,1)S(1)} %get-tuple-element.28), channel_id=1, source_target_pairs={{0,16},{16,0},{1,17},{17,1},{2,18},{18,2},{3,19},{19,3},{4,20},{20... | collective-permute-start | bytes 786440 | tf_op jit(solution)/shard_map/ppermute | solution.py:485

commit v20 on v10

--- a/solution.py
+++ b/solution.py
@@ -341,20 +341,20 @@
     def put(final):
         interleave(out_ref, final, 1 - core)
 
-    def edge_all():
-        for ref, row0 in ((p_ref, own_at), (q_ref, other_at)):
-            for i in range(n_chunk):
-                yield from edge(ref, row0, i)
-
-    steps = edge_all()
+    for ref, row0 in ((p_ref, own_at), (q_ref, other_at)):
+
+        def edge_chunk(i, carry, ref=ref, row0=row0):
+            for _ in edge(ref, row0, i):
+                pass
+            return carry
+
+        lax.fori_loop(0, n_chunk, edge_chunk, 0)
+
     conv = conv_steps(
         lambda r, base: mixed_ref[base // LANES, r * GROUP : (r + 1) * GROUP, :],
         fwd_ref, bwd_ref, w_out_ref, h_ref, prod_ref, z_ref, put,
     )
     for _ in conv:
-        for _ in range(5):
-            next(steps, None)
-    for _ in steps:
         pass
 
 

time: 13.8 us -> 14 us (1.014)
  Pallas kernels: 6.2 us -> 6.45 us
    pallas_call x1, Pallas kernels: 3.03 us -> 3.28 us  [on_device(): pl.pallas_call(inner_kernel, out_shape=(p_shape, mixed_shape, out_shape),...]
  transfers between devices with their start and end apart: 3 -> 3, of which waited for: 1 -> 1; matrix products, arithmetic and copies ran while one was open for 6% -> 6% of each run, Pallas kernels for 36% -> 37%
where the time goes in v20:
time: 14 us; the launch traced here: 13.9 us
  Pallas kernels  6.45 us (46%)
  starting transfers between devices  5.33 us (38%)
  other arithmetic  0.86 us (6%)
  local copies, waits for them, and re-layouts  0.83 us (6%)
  waiting for transfers between devices  0.33 us (2%)
    ppermute x1, starting transfers between devices, on_device(): theirs = lax.ppermute(send, 'row', swap)  4.21 us
    pallas_call x1, Pallas kernels, on_device(): pl.pallas_call(inner_kernel, out_shape=(p_shape, mixed_shape, out_shape),...  3.28 us
    pallas_call x1, Pallas kernels, on_device(): pl.pallas_call(prep_kernel, out_shape=(p_shape, shape(w_in.shape, BF16),...  1.81 us
    pallas_call x1, Pallas kernels, on_device(): pl.pallas_call(edge_kernel, out_shape=(out_shape, mixed_shape, half_shape...  1.36 us
    concatenate x1, other arithmetic, on_device(): both = jnp.concatenate([mine, mine], 1)  0.83 us
    dynamic_update_slice x1, local copies, waits for them, and re-layouts, on_device(): return lax.dynamic_update_slice_in_dim(both, theirs, (1 - core) * part, 1)  0.72 us
    ppermute x1, starting transfers between devices, on_device(): lax.ppermute(jnp.concatenate([outer, column(0)], 0), ('row', 'col'), pairs)  0.66 us
    ppermute x1, starting transfers between devices, on_device(): lax.ppermute(image_tokens, 'row', swap)  0.45 us
  transfers between devices with their start and end apart: 3, of which 1 were waited for; matrix products, arithmetic and copies ran while one was open for 6% of the time, Pallas kernels for 37%

profile of v20, /device:TPU:0, one launch (start us, length us, event | category | flops | bytes accessed | tf_op | source)
XLA Modules:
  0.0 13.9 jit_solution(6111366123060960765)
XLA Ops:
  0.0 0.5 %collective-permute-start = (bf16[32,32,256]{2,1,0:T(8,128)(2,1)}, bf16[32,32,256]{2,1,0:T(8,128)(2,1)S(1)}, u32[]{:S(2)}, u32[]{:S(2)}) collective-permute-start(bf16[32,32,256]{2,1,0:T(8,128)(2,1)} %own_hbm), channel_id=1, source_target_pairs={{0,16},{16,0},{1,17},{17,1},{2,18},{18,2},{3,19},{19,3},{4,20},{20... | collective-permute-start | bytes 1572872 | tf_op jit(solution)/shard_map/ppermute | solution.py:413
  0.5 1.8 %shard_map.100 = (f32[6,824,128]{2,1,0:T(8,128)S(1)}, bf16[256,768]{1,0:T(8,128)(2,1)S(1)}, bf16[256,256]{1,0:T(8,128)(2,1)S(1)}, bf16[512,256]{1,0:T(8,128)(2,1...) custom-call(bf16[32,32,256]{2,1,0:T(8,128)(2,1)} %own_hbm, ...), custom_call_target="tpu_custom_call" | custom-call | bytes 3145728 | tf_op jit(solution)/shard_map/pallas_call | solution.py:418
  2.3 0.0 collective-permute-done.other_ref
  2.3 0.1 fusion.2
  2.4 0.7 %collective-permute-start.1 = (bf16[64,256]{1,0:T(8,128)(2,1)S(1)}, bf16[64,256]{1,0:T(8,128)(2,1)S(1)}, u32[]{:S(2)}, u32[]{:S(2)}) collective-permute-start(bf16[64,256]{1,0:T(8,128)(2,1)S(1)} %pad_maximum_fusion.1), channel_id=1, source_target_pairs={{16,1},{1,16},{17,2},{2,17},{18,3},{3,18},{19,4},{4,19},{20,5},{5,... | collective-permute-start | bytes 98312 | tf_op jit(solution)/shard_map/ppermute | solution.py:457
  3.1 3.3 %shard_map.101 = (f32[6,824,128]{2,1,0:T(8,128)S(1)}, f32[6,512,128]{2,1,0:T(8,128)S(1)}, f32[2,2,512,128]{3,2,1,0:T(8,128)S(1)}) custom-call(f32[6,824,128]{2,1,0:T(8,128)S(1)} %get-tuple-element.17._, bf16[32,32,256]{2,1,0:T(8,128)(2,1)S(1)} %collective-permute-done.other_ref, ...), custom_call_target="tpu_custom_call", output_to_operand_aliasing={{0}: (0, {})} | custom-call | flops 1000000000 | bytes 12582912 | tf_op jit(solution)/shard_map/pallas_call | solution.py:458
  6.4 0.0 collective-permute-done.1.halo_ref
  6.4 1.4 %shard_map.102 = (f32[2,2,512,128]{3,2,1,0:T(8,128)S(1)}, f32[6,512,128]{2,1,0:T(8,128)S(1)}, bf16[32,16,256]{2,1,0:T(8,128)(2,1)S(1)}, bf16[32,16,256]{2,1,0:T(8,128)(2,1)S(1)}) custom-call(f32[2,2,512,128]{3,2,1,0:T(8,128)S(1)} %get-tuple-element.24._, f32[6,512,128]{2,1,0:T(8,128)S(1)} %get-tuple-element.25.__, ...), custom_call_target="tpu_custom_call", output_to_operand_aliasing={{0}: (0, {}), {1}: (1, {})} | custom-call | flops 300000000 | bytes 4194304 | tf_op jit(solution)/shard_map/pallas_call | solution.py:474
  7.8 4.2 %collective-permute-start.2 = (bf16[32,16,256]{2,1,0:T(8,128)(2,1)S(1)}, bf16[32,16,256]{2,1,0:T(8,128)(2,1)S(1)}, u32[]{:S(2)}, u32[]{:S(2)}) collective-permute-start(bf16[32,16,256]{2,1,0:T(8,128)(2,1)S(1)} %get-tuple-element.28), channel_id=1, source_target_pairs={{0,16},{16,0},{1,17},{17,1},{2,18},{18,2},{3,19},{19,3},{4,20},{20... | collective-permute-start | bytes 786440 | tf_op jit(solution)/shard_map/ppermute | solution.py:488
  12.0 0.8 %pad_maximum_fusion = bf16[32,32,256]{2,1,0:T(8,128)(2,1)} fusion(bf16[32,16,256]{2,1,0:T(8,128)(2,1)S(1)} %get-tuple-element.27), kind=kLoop, calls=%fused_computation | loop fusion | flops 1048576 | bytes 786432 | tf_op jit(solution)/shard_map/concatenate | solution.py:489
  12.8 0.3 %collective-permute-done.2 = bf16[32,16,256]{2,1,0:T(8,128)(2,1)S(1)} collective-permute-done((bf16[32,16,256]{2,1,0:T(8,128)(2,1)S(1)}, bf16[32,16,256]{2,1,0:T(8,128)(2,1)S(1)}, u32[]{:S(2)}, u32[]{:S(2)}) %collective-permute-start.2) | collective-permute-done | bytes 262176 | tf_op jit(solution)/shard_map/ppermute | solution.py:488
  13.2 0.7 %constant_dynamic-update-slice_fusion = bf16[32,32,256]{2,1,0:T(8,128)(2,1)} fusion(bf16[32,32,256]{2,1,0:T(8,128)(2,1)} %pad_maximum_fusion, bf16[32,16,256]{2,1,0:T(8,128)(2,1)S(1)} %collective-permute-done.2, s32[]{:T(128)S(6)} %select_n.25), kind=kLoop, calls=%fused_computation.6 | loop fusion | bytes 524292 | tf_op jit(solution)/shard_map/dynamic_update_slice | solution.py:490
  (3 shorter events, 0.0 us)
Async XLA Ops:
  0.0 2.3 %collective-permute-start = (bf16[32,32,256]{2,1,0:T(8,128)(2,1)}, bf16[32,32,256]{2,1,0:T(8,128)(2,1)S(1)}, u32[]{:S(2)}, u32[]{:S(2)}) collective-permute-start(bf16[32,32,256]{2,1,0:T(8,128)(2,1)} %own_hbm), channel_id=1, source_target_pairs={{0,16},{16,0},{1,17},{17,1},{2,18},{18,2},{3,19},{19,3},{4,20},{20... | collective-permute-start | bytes 1572872 | tf_op jit(solution)/shard_map/ppermute | solution.py:413
  2.4 4.0 %collective-permute-start.1 = (bf16[64,256]{1,0:T(8,128)(2,1)S(1)}, bf16[64,256]{1,0:T(8,128)(2,1)S(1)}, u32[]{:S(2)}, u32[]{:S(2)}) collective-permute-start(bf16[64,256]{1,0:T(8,128)(2,1)S(1)} %pad_maximum_fusion.1), channel_id=1, source_target_pairs={{16,1},{1,16},{17,2},{2,17},{18,3},{3,18},{19,4},{4,19},{20,5},{5,... | collective-permute-start | bytes 98312 | tf_op jit(solution)/shard_map/ppermute | solution.py:457
  7.8 5.4 %collective-permute-start.2 = (bf16[32,16,256]{2,1,0:T(8,128)(2,1)S(1)}, bf16[32,16,256]{2,1,0:T(8,128)(2,1)S(1)}, u32[]{:S(2)}, u32[]{:S(2)}) collective-permute-start(bf16[32,16,256]{2,1,0:T(8,128)(2,1)S(1)} %get-tuple-element.28), channel_id=1, source_target_pairs={{0,16},{16,0},{1,17},{17,1},{2,18},{18,2},{3,19},{19,3},{4,20},{20... | collective-permute-start | bytes 786440 | tf_op jit(solution)/shard_map/ppermute | solution.py:488
